TPU v7x, 32 devices: a whole 2x2x4 slice. The times are simulated.
32 devices in a mesh: batch: 8 (over y, x, core), seq: 4 (over z).
Axes of the slice: x: 2, y: 2, z: 4, core: 2. Of those that a mesh axis runs over, the one named last changes fastest.
Arguments:
- hidden: bfloat16 [8, 2048, 1024], P('batch', 'seq'), may hold values from -6 to 6
- token_ids: int32 [8, 2048], P('batch', 'seq'), may hold values from 3 to 31
- offsets: int32 [8], P('batch'), may hold values from 0 to 59999, as said below
- end_places: int32 [8], P('batch'), may hold values from 1 to 2048, as said below
- token_table: bfloat16 [32, 1024], replicated, may hold values from -6 to 6
- norm_gain: float32 [1024], replicated, may hold values from 0.5 to 1.5
- norm_bias: float32 [1024], replicated, may hold values from -2 to 2
- qkv_weight: bfloat16 [1024, 3072], replicated, may hold values from -0.1875 to 0.1875
- out_weight: bfloat16 [1024, 1024], replicated, may hold values from -1.5 to 1.5
- in_weight: bfloat16 [1024, 4096], replicated, may hold values from -0.1875 to 0.1875
- in_bias: float32 [4096], replicated, may hold values from -3 to 3
- down_weight: bfloat16 [4096, 1024], replicated, may hold values from -0.09375 to 0.09375
- down_bias: float32 [1024], replicated, may hold values from -3 to 3
- cotangent: bfloat16 [8, 2048, 1024], P('batch', 'seq'), may hold values from -6 to 6
Outputs:
- output: bfloat16 [8, 2048, 1024], P('batch', 'seq')
- hidden_grad: float32 [8, 2048, 1024], P('batch', 'seq')
- norm_gain_grad: float32 [1024], P('seq')
- norm_bias_grad: float32 [1024], P('seq')
- qkv_weight_grad: float32 [1024, 3072], P('seq')
- out_weight_grad: float32 [1024, 1024], P('seq')
- in_weight_grad: float32 [1024, 4096], P('seq')
- in_bias_grad: float32 [4096], P('seq')
- down_weight_grad: float32 [4096, 1024], P('seq')
- down_bias_grad: float32 [1024], P('seq')
Inputs may be any that keep to these rules, and one draw needn't show every extreme that they name: `offsets`: offset 0 means that the window begins at its protein's first residue; a window begins at or before residue 59999 of its protein. `end_places`: 2048 means that the protein runs past the window's end. Of the 1 windows on each index of batch, at least one has its value at 1537 or above.
All inputs are finite; a program needn't handle non-finite values.
Results may differ from a plain program's by a relative error of at most 0.025.
Values may be sent and summed in bfloat16 or wider, within the bound.
No kernel may reach another device: no remote copies, remote signals or barrier semaphores. Data moves between devices by JAX's collectives and lax.ppermute only.
A program may use at most 320 MiB of HBM per device.

v0:
```python
import jax
import jax.numpy as jnp
from jax import lax
from jax.sharding import PartitionSpec as P

HEAD_DIM = 64
ROT = 32


EPSILON = 1e-05
BLOCKED = -1e30


def rotate(vectors, cosine_table, sine_table):
    even_part = vectors[..., 0:ROT:2]
    odd_part = vectors[..., 1:ROT:2]
    turned = jnp.stack(
        [
            even_part * cosine_table - odd_part * sine_table,
            odd_part * cosine_table + even_part * sine_table,
        ],
        axis=-1,
    )
    turned = turned.reshape(vectors.shape[:-1] + (ROT,))
    return jnp.concatenate([turned, vectors[..., ROT:]], axis=-1)


def angles(places):
    inverse = 10000.0 ** (-(jnp.arange(ROT // 2, dtype=jnp.float32) * 2.0) / ROT)
    phases = places.astype(jnp.float32)[:, None] * inverse[None, :]
    return (jnp.cos(phases), jnp.sin(phases))


def visible(query_places, key_places, end_places):
    query_after = query_places[None, :, None] > end_places[:, None, None]
    key_after = key_places[None, None, :] > end_places[:, None, None]
    return (key_places[None, None, :] <= query_places[None, :, None]) & (query_after == key_after)


def norm_rows(stream, gain_row, bias_row):
    centre = stream - jnp.mean(stream, axis=-1, keepdims=True)
    spread = jnp.mean(centre * centre, axis=-1, keepdims=True)
    return centre * lax.rsqrt(spread + EPSILON) * gain_row + bias_row


def gelu_rows(pre_active):
    return jax.nn.gelu(pre_active, approximate=True)


def body(
    hidden,
    token_ids,
    offsets,
    end_places,
    token_table,
    norm_gain,
    norm_bias,
    qkv_weight,
    out_weight,
    in_weight,
    in_bias,
    down_weight,
    down_bias,
    cotangent,
):
    windows_here, shard_rows, model_width = hidden.shape
    head_count = model_width // HEAD_DIM
    seq_count = lax.axis_size("seq")
    seq_place = lax.axis_index("seq")
    home_places = seq_place * shard_rows + jnp.arange(shard_rows, dtype=jnp.int32)
    token_rows = shard_rows * windows_here
    marked = token_ids.T
    marked = jnp.where(home_places[:, None] == end_places[None, :], 2, marked)
    marked = jnp.where(home_places[:, None] == end_places[None, :] + 1, 1, marked)
    marked = jnp.where((home_places[:, None] == 0) & (offsets[None, :] == 0), 1, marked)
    onehot = (marked[..., None] == jnp.arange(token_table.shape[0], dtype=jnp.int32)).astype(
        jnp.bfloat16
    )
    embedded = jnp.einsum("swv,vd->swd", onehot, token_table, preferred_element_type=jnp.float32)
    stream_three = jnp.transpose(hidden, (1, 0, 2)).astype(jnp.float32) + embedded
    cot_three = jnp.transpose(cotangent, (1, 0, 2))
    own_high = jnp.max(home_places)
    stream_rows = stream_three.reshape(token_rows, model_width)
    normed, norm_back = jax.vjp(norm_rows, stream_rows, norm_gain, norm_bias)
    normed_low = normed.astype(jnp.bfloat16)
    projected = jnp.dot(normed_low, qkv_weight, preferred_element_type=jnp.float32)
    cosine_table, sine_table = angles(home_places)
    cosine_table = cosine_table[:, None, None, :]
    sine_table = sine_table[:, None, None, :]

    def turn_heads(projected_rows):
        divided = projected_rows.reshape(shard_rows, windows_here, 3, head_count, HEAD_DIM)
        return (
            rotate(divided[:, :, 0], cosine_table, sine_table),
            rotate(divided[:, :, 1], cosine_table, sine_table),
            divided[:, :, 2],
        )

    (queries, key_rows, values), turn_back = jax.vjp(turn_heads, projected)
    query_low = queries.astype(jnp.bfloat16)
    key_value = jnp.concatenate(
        [
            key_rows.reshape(shard_rows, windows_here, model_width),
            values.reshape(shard_rows, windows_here, model_width),
        ],
        axis=-1,
    ).astype(jnp.bfloat16)

    def split_block(key_block):
        row_count = key_block.shape[0]
        return (
            key_block[..., :model_width].reshape(row_count, windows_here, head_count, HEAD_DIM),
            key_block[..., model_width:].reshape(row_count, windows_here, head_count, HEAD_DIM),
        )

    def block_places(row_start, row_count):
        return row_start + jnp.arange(row_count, dtype=jnp.int32)

    def block_scores(key_block, key_start):
        key_part, value_part = split_block(key_block)
        key_places = block_places(key_start, key_block.shape[0])
        scores = (
            jnp.einsum("qwhd,kwhd->whqk", query_low, key_part, preferred_element_type=jnp.float32)
            * 0.125
        )
        scores = jnp.where(visible(home_places, key_places, end_places)[:, None], scores, BLOCKED)
        return (scores, key_part, value_part)

    def attend(carried, key_block, key_start):
        running, totals, accumulated = carried
        scores, key_part, value_part = block_scores(key_block, key_start)
        highest = jnp.maximum(running, jnp.max(scores, axis=-1))
        factor = jnp.exp(running - highest)
        raised = jnp.exp(scores - highest[..., None])
        totals = totals * factor + jnp.sum(raised, axis=-1)
        accumulated = accumulated * factor[..., None] + jnp.einsum(
            "whqk,kwhd->whqd",
            raised.astype(jnp.bfloat16),
            value_part,
            preferred_element_type=jnp.float32,
        )
        return (highest, totals, accumulated)

    start_state = (
        jnp.full((windows_here, head_count, shard_rows), BLOCKED, jnp.float32),
        jnp.zeros((windows_here, head_count, shard_rows), jnp.float32),
        jnp.zeros((windows_here, head_count, shard_rows, HEAD_DIM), jnp.float32),
    )
    carried = start_state
    fetched_rows = lax.all_gather(key_value, "seq", axis=0, tiled=True)
    row_count = fetched_rows.shape[0]
    blocks = fetched_rows.reshape((row_count // shard_rows, shard_rows) + fetched_rows.shape[1:])

    def visit_block(held_state, element):
        number, key_block = element
        key_start = number * shard_rows
        dead = jnp.min(block_places(key_start, shard_rows)) > own_high
        held_state = lax.cond(
            dead,
            lambda kept_state: kept_state,
            lambda kept_state: attend(kept_state, key_block, key_start),
            held_state,
        )
        return (held_state, None)

    carried, unused = lax.scan(
        visit_block, carried, (jnp.arange(blocks.shape[0], dtype=jnp.int32), blocks)
    )
    running, totals, accumulated = carried
    attention = accumulated / totals[..., None]
    log_total = running + jnp.log(totals)
    attention_rows = jnp.transpose(attention, (2, 0, 1, 3))
    mixed_low = attention_rows.reshape(token_rows, model_width).astype(jnp.bfloat16)
    attended = jnp.dot(mixed_low, out_weight, preferred_element_type=jnp.float32)
    pre_active = jnp.dot(normed_low, in_weight, preferred_element_type=jnp.float32) + in_bias
    active, gelu_back = jax.vjp(gelu_rows, pre_active)
    active_low = active.astype(jnp.bfloat16)
    result = (
        stream_rows
        + attended
        + jnp.dot(active_low, down_weight, preferred_element_type=jnp.float32)
        + down_bias
    )
    grad_rows = cot_three.reshape(token_rows, model_width)
    down_weight_grad = jnp.dot(active_low.T, grad_rows, preferred_element_type=jnp.float32)
    down_bias_grad = jnp.sum(grad_rows.astype(jnp.float32), axis=0)
    out_weight_grad = jnp.dot(mixed_low.T, grad_rows, preferred_element_type=jnp.float32)
    active_grad = jnp.dot(grad_rows, down_weight.T, preferred_element_type=jnp.float32)
    pre_grad = gelu_back(active_grad)[0].astype(jnp.bfloat16)
    in_weight_grad = jnp.dot(normed_low.T, pre_grad, preferred_element_type=jnp.float32)
    in_bias_grad = jnp.sum(pre_grad.astype(jnp.float32), axis=0)
    mixed_grad = jnp.dot(grad_rows, out_weight.T, preferred_element_type=jnp.float32).astype(
        jnp.bfloat16
    )
    grad_heads = mixed_grad.reshape(shard_rows, windows_here, head_count, HEAD_DIM)
    delta_rows = jnp.sum(grad_heads.astype(jnp.float32) * attention_rows, axis=-1)
    row_delta = jnp.transpose(delta_rows, (1, 2, 0))
    whole_keys = lax.all_gather(key_value, "seq", axis=0, tiled=True)
    blocks = whole_keys.reshape((seq_count, shard_rows) + whole_keys.shape[1:])
    zero_heads = jnp.zeros((shard_rows, windows_here, head_count, HEAD_DIM), jnp.float32)

    def back_block(query_grad, element):
        number, key_block = element
        key_start = number * shard_rows

        def live_block(held_grad):
            scores, key_part, value_part = block_scores(key_block, key_start)
            weighting = jnp.exp(scores - log_total[..., None])
            prob_grad = jnp.einsum(
                "qwhd,kwhd->whqk", grad_heads, value_part, preferred_element_type=jnp.float32
            )
            score_low = (weighting * (prob_grad - row_delta[..., None])).astype(jnp.bfloat16)
            held_grad = held_grad + 0.125 * jnp.einsum(
                "whqk,kwhd->qwhd", score_low, key_part, preferred_element_type=jnp.float32
            )
            key_grad = 0.125 * jnp.einsum(
                "whqk,qwhd->kwhd", score_low, query_low, preferred_element_type=jnp.float32
            )
            value_grad = jnp.einsum(
                "whqk,qwhd->kwhd",
                weighting.astype(jnp.bfloat16),
                grad_heads,
                preferred_element_type=jnp.float32,
            )
            return (
                held_grad,
                jnp.concatenate(
                    [
                        key_grad.reshape(shard_rows, windows_here, model_width),
                        value_grad.reshape(shard_rows, windows_here, model_width),
                    ],
                    axis=-1,
                ),
            )

        def dead_block(held_grad):
            return (held_grad, jnp.zeros((shard_rows, windows_here, 2 * model_width), jnp.float32))

        dead = jnp.min(block_places(key_start, shard_rows)) > own_high
        return lax.cond(dead, dead_block, live_block, query_grad)

    query_grad, key_terms = lax.scan(
        back_block, zero_heads, (jnp.arange(seq_count, dtype=jnp.int32), blocks)
    )
    key_terms = key_terms.reshape((seq_count * shard_rows,) + key_terms.shape[2:])
    summed = lax.psum_scatter(
        key_terms.astype(jnp.bfloat16), "seq", scatter_dimension=0, tiled=True
    ).astype(jnp.float32)
    key_grad = summed[..., :model_width].reshape(shard_rows, windows_here, head_count, HEAD_DIM)
    value_grad = summed[..., model_width:].reshape(shard_rows, windows_here, head_count, HEAD_DIM)
    joined_grad = turn_back((query_grad, key_grad, value_grad))[0].astype(jnp.bfloat16)
    qkv_weight_grad = jnp.dot(normed_low.T, joined_grad, preferred_element_type=jnp.float32)
    normed_grad = jnp.dot(joined_grad, qkv_weight.T, preferred_element_type=jnp.float32) + jnp.dot(
        pre_grad, in_weight.T, preferred_element_type=jnp.float32
    )
    stream_part, norm_gain_grad, norm_bias_grad = norm_back(normed_grad)
    stream_grad = grad_rows.astype(jnp.float32) + stream_part
    result_three = result.reshape(shard_rows, windows_here, model_width)
    grad_three = stream_grad.reshape(shard_rows, windows_here, model_width)
    output = jnp.transpose(result_three, (1, 0, 2)).astype(jnp.bfloat16)
    hidden_grad = jnp.transpose(grad_three, (1, 0, 2))
    shares = (
        lax.psum_scatter(
            norm_gain_grad.astype(jnp.bfloat16), "seq", scatter_dimension=0, tiled=True
        ).astype(jnp.float32),
        lax.psum_scatter(
            norm_bias_grad.astype(jnp.bfloat16), "seq", scatter_dimension=0, tiled=True
        ).astype(jnp.float32),
        lax.psum_scatter(
            qkv_weight_grad.astype(jnp.bfloat16), "seq", scatter_dimension=0, tiled=True
        ).astype(jnp.float32),
        lax.psum_scatter(
            out_weight_grad.astype(jnp.bfloat16), "seq", scatter_dimension=0, tiled=True
        ).astype(jnp.float32),
        lax.psum_scatter(
            in_weight_grad.astype(jnp.bfloat16), "seq", scatter_dimension=0, tiled=True
        ).astype(jnp.float32),
        lax.psum_scatter(
            in_bias_grad.astype(jnp.bfloat16), "seq", scatter_dimension=0, tiled=True
        ).astype(jnp.float32),
        lax.psum_scatter(
            down_weight_grad.astype(jnp.bfloat16), "seq", scatter_dimension=0, tiled=True
        ).astype(jnp.float32),
        lax.psum_scatter(
            down_bias_grad.astype(jnp.bfloat16), "seq", scatter_dimension=0, tiled=True
        ).astype(jnp.float32),
    )
    totals_all = (
        lax.psum(shares[0].astype(jnp.bfloat16), "batch").astype(jnp.float32),
        lax.psum(shares[1].astype(jnp.bfloat16), "batch").astype(jnp.float32),
        lax.psum(shares[2].astype(jnp.bfloat16), "batch").astype(jnp.float32),
        lax.psum(shares[3].astype(jnp.bfloat16), "batch").astype(jnp.float32),
        lax.psum(shares[4].astype(jnp.bfloat16), "batch").astype(jnp.float32),
        lax.psum(shares[5].astype(jnp.bfloat16), "batch").astype(jnp.float32),
        lax.psum(shares[6].astype(jnp.bfloat16), "batch").astype(jnp.float32),
        lax.psum(shares[7].astype(jnp.bfloat16), "batch").astype(jnp.float32),
    )
    return (
        output,
        hidden_grad,
        totals_all[0],
        totals_all[1],
        totals_all[2],
        totals_all[3],
        totals_all[4],
        totals_all[5],
        totals_all[6],
        totals_all[7],
    )


def solution(mesh):
    placed = (
        P("batch", "seq", None),
        P("batch", "seq"),
        P("batch"),
        P("batch"),
        P(),
        P(),
        P(),
        P(),
        P(),
        P(),
        P(),
        P(),
        P(),
        P("batch", "seq", None),
    )
    return jax.shard_map(
        body,
        mesh=mesh,
        in_specs=placed,
        out_specs=(
            P("batch", "seq", None),
            P("batch", "seq", None),
            P("seq"),
            P("seq"),
            P("seq", None),
            P("seq", None),
            P("seq", None),
            P("seq"),
            P("seq", None),
            P("seq"),
        ),
        check_vma=False,
    )
```

profile of v0, /device:TPU:0, one launch (start us, length us, event | category | flops | bytes accessed | tf_op | source)
XLA Modules:
  0.0 1312.2 jit_solution(13740469567836884625)
XLA Ops:
  77.4 138.2 %all-gather.2.cloned.1.call-done = bf16[2048,1,2048]{2,0,1:T(8,128)(2,1)} async-done(((bf16[512,1,2048]{2,0,1:T(8,128)(2,1)}), bf16[2048,1,2048]{2,0,1:T(8,128)(2,1)}) %all-gather.2.cloned.1.call-update) | async-done | bytes 8388624 | tf_op jit(solution)/shard_map/all_gather | solution.py:150
  215.6 11.4 copy.65
  228.6 40.8 %while.31 = (s32[]{:T(128)}, f32[1,16,512]{2,1,0:T(8,128)S(1)}, f32[1,16,512]{2,1,0:T(8,128)S(1)}, f32[1,16,512,64]{2,3,1,0:T(8,128)}, s32[4]{0:T(128)S(1)}, /*i...) while((s32[]{:T(128)}, f32[1,16,512]{2,1,0:T(8,128)S(1)}, ...), condition=%wide.region_9.10_spmd.clone, body=%wide.region_3.9_spmd.clone.sunk | while | flops 1121742336 | bytes 134756688 | solution.py:166
  231.7 28.2 %conditional.6 = (f32[1,16,512]{2,1,0:T(8,128)S(1)}, f32[1,16,512]{2,1,0:T(8,128)S(1)}, f32[1,16,512,64]{2,3,1,0:T(8,128)}) conditional(s32[]{:T(128)} %convert_element_type.244, (s32[]{:T(128)}, s32[]{:T(128)}, s32[1]{0:T(128)}, bf16[4,512,1,2048]{1,3,2,0:T(8,128)(2,1)}, s32[]{:T(128)}, /*index=5*/bf16[512,1,16,64]{0,3,2,1:T(8,128)(2,1)}, ...), branch_computations={%region_5.7_spmd, %region_8.8_spmd} | conditional | flops 1121741312 | bytes 134688832 | solution.py:158
  273.3 93.3 %while.32 = (s32[]{:T(128)}, f32[512,1,16,64]{0,3,2,1:T(8,128)}, bf16[4,512,1,2048]{3,1,0,2:T(8,128)(2,1)}, s32[4]{0:T(128)S(1)}, s32[]{:T(128)}, /*index=5*/bf1...) while((s32[]{:T(128)}, f32[512,1,16,64]{0,3,2,1:T(8,128)}, ...), condition=%wide.region_15.16_spmd.clone, body=%wide.region_11.15_spmd.clone.sunk | while | flops 2733379072 | bytes 161332096 | solution.py:242
  276.8 47.4 %conditional.7 = (f32[512,1,16,64]{0,3,2,1:T(8,128)}, bf16[1,512,1,2048]{1,3,2,0:T(8,128)(2,1)}) conditional(s32[]{:T(128)} %convert_element_type.245, (bf16[4,512,1,2048]{1,3,2,0:T(8,128)(2,1)}, s32[]{:T(128)}, s32[]{:T(128)}, s32[]{:T(128)}, s32[1]{0:T(128)}, /*index=5*/bf16[512,1,16,64]{0,3,2,1:T(8,128)(2,1)}, f32[1,16,512]{2,1,0:T(8,128)S(1)}, ...), branch_computations={%region_13.13_spmd, %region_14.14_spmd} | conditional | flops 2733378048 | bytes 152940656 | solution.py:240
  279.7 9.3 fusion.27
  289.0 9.2 fusion.17
  303.8 11.1 fusion.21
  380.1 14.9 %fusion.69 = (bf16[4096]{0:T(1024)(128)(2,1)S(1)}, bf16[512,4096]{1,0:T(8,128)(2,1)S(1)}) fusion(f32[512,4096]{1,0:T(8,128)S(1)} %fusion.70, f32[4096]{0:T(1024)S(1)} %copy-done.39, bf16[4096,1024]{1,0:T(8,128)(2,1)} %param.33, bf16[1,512,1024]{2,1,0:T(8,128)(2,1)S(1)} %copy-done.13), kind=kOutput, calls=%fused_computation.144 | convolution fusion | flops 4341100544 | bytes 22044672 | tf_op jit(solution)/shard_map/dot_general | solution.py:188
  404.0 13.1 convolution_convert_fusion
  422.8 308.6 %reduce-scatter.6.cloned.1.call-done = bf16[512,1,2048]{2,0,1:T(8,128)(2,1)} async-done(((bf16[2048,1,2048]{2,0,1:T(8,128)(2,1)}), bf16[512,1,2048]{2,0,1:T(8,128)(2,1)}) %reduce-scatter.6.cloned.1.call-update) | async-done | bytes 2097168 | tf_op jit(solution)/shard_map/reduce_scatter | solution.py:246
  750.2 9.9 pad.29
  760.1 10.0 pad.30
  770.1 9.9 pad.33
  780.0 9.9 pad.34
  806.3 12.5 fusion.60
  818.8 105.6 %reduce-scatter.12.cloned.1.call-done = bf16[256,4096]{1,0:T(8,128)(2,1)} async-done(((bf16[1024,4096]{1,0:T(8,128)(2,1)}), bf16[256,4096]{1,0:T(8,128)(2,1)}) %reduce-scatter.12.cloned.1.call-update) | async-done | bytes 2097168 | tf_op jit(solution)/shard_map/reduce_scatter | solution.py:275
  924.5 147.5 %reduce-scatter.14.cloned.1.call-done = bf16[1024,1024]{1,0:T(8,128)(2,1)} async-done(((bf16[4096,1024]{1,0:T(8,128)(2,1)}), bf16[1024,1024]{1,0:T(8,128)(2,1)}) %reduce-scatter.14.cloned.1.call-update) | async-done | bytes 2097168 | tf_op jit(solution)/shard_map/reduce_scatter | solution.py:281
  1072.0 113.8 %reduce-scatter.8.cloned.1.call-done = bf16[256,3072]{1,0:T(8,128)(2,1)} async-done(((bf16[1024,3072]{1,0:T(8,128)(2,1)}), bf16[256,3072]{1,0:T(8,128)(2,1)}) %reduce-scatter.8.cloned.1.call-update) | async-done | bytes 1572880 | tf_op jit(solution)/shard_map/reduce_scatter | solution.py:269
  1185.8 10.6 fusion.71
  1212.0 18.0 %all-reduce.15 = (bf16[1024]{0:T(1024)(128)(2,1)S(1)}, bf16[1024]{0:T(1024)(128)(2,1)S(1)}, bf16[4096]{0:T(1024)(128)(2,1)S(1)}, bf16[1024]{0:T(1024)(128)(2,1)S(1)}) all-reduce(bf16[1024]{0:T(1024)(128)(2,1)S(1)} %get-tuple-element.363, ...), channel_id=3, replica_groups=mesh['batch'=8,'seq'=4] {'seq'}, use_global_device_ids=true, to_apply=%region_20.21.clone | all-reduce | flops 7168 | bytes 28672
  1230.2 12.1 all-reduce.13
  1249.1 46.2 %all-reduce.18.cloned.1.call-done = (bf16[256,3072]{1,0:T(8,128)(2,1)}, bf16[256,1024]{1,0:T(8,128)(2,1)}, bf16[256,4096]{1,0:T(8,128)(2,1)}, bf16[1024,1024]{1,0:T(8,128)(2,1)}) async-done(((bf16[256,3072]{1,0:T(8,128)(2,1)}, bf16[256,1024]{1,0:T(8,128)(2,1)}, bf16[256,4096]{1,0:T(8,128)(2,1)}, bf16[1024,1024]{1,0:T(8,128)(2,1)}), (bf16[256,3072]{1,0:T(8,128)(2,1)}, bf16[256,1024]{1,0:T(8,128)(2,1)}, ...) | async-done | bytes 6291472 | tf_op jit(solution)/shard_map/psum | solution.py:291
  (252 shorter events, 261.6 us)
Async XLA Ops:
  7.2 63.1 %copy-start = (bf16[1024,1024]{1,0:T(8,128)(2,1)S(1)}, bf16[1024,1024]{1,0:T(8,128)(2,1)}, u32[]{:S(2)}) copy-start(bf16[1024,1024]{1,0:T(8,128)(2,1)} %param.30) | copy-start | bytes 6291460
  7.2 208.4 %all-gather.2.cloned.1.call-start = ((), (), s32[]{:S(2)}) async-start(), calls=%async_computation.5 | async-start | bytes 10485760 | tf_op jit(solution)/shard_map/all_gather | solution.py:150
  11.2 10.9 copy-start.30
  13.5 8.7 copy-start.32
  13.5 8.7 copy-start.36
  13.5 8.7 copy-start.38
  24.2 6.4 copy-start.22
  63.0 7.3 copy-start.12
  63.1 668.3 %reduce-scatter.6.cloned.1.call-start = ((), (), s32[]{:S(2)}) async-start(), calls=%async_computation.6 | async-start | bytes 10485760 | tf_op jit(solution)/shard_map/reduce_scatter | solution.py:246
  238.4 5.7 copy-start.1
  298.2 5.6 copy-start.2
  366.7 452.2 %reduce-scatter.10.cloned.1.call-start = ((), (), s32[]{:S(2)}) async-start(), calls=%async_computation.8 | async-start | bytes 2621440 | tf_op jit(solution)/shard_map/reduce_scatter | solution.py:272
  372.8 7.3 copy-start.39
  372.8 551.6 %reduce-scatter.12.cloned.1.call-start = ((), (), s32[]{:S(2)}) async-start(), calls=%async_computation.9 | async-start | bytes 10485760 | tf_op jit(solution)/shard_map/reduce_scatter | solution.py:275
  380.1 14.9 %copy-start.42 = (f32[512,4096]{1,0:T(8,128)}, f32[512,4096]{1,0:T(8,128)S(1)}, u32[]{:S(2)}) copy-start(f32[512,4096]{1,0:T(8,128)S(1)} %fusion.70) | copy-start | bytes 25165828
  380.1 16.9 %copy-start.23 = (bf16[512,1024]{1,0:T(8,128)(2,1)S(1)}, bf16[512,1024]{1,0:T(8,128)(2,1)}, u32[]{:S(2)}) copy-start(bf16[512,1024]{1,0:T(8,128)(2,1)} %copy-done.22) | copy-start | bytes 3145732
  404.0 668.0 %reduce-scatter.14.cloned.1.call-start = ((), (), s32[]{:S(2)}) async-start(), calls=%async_computation.10 | async-start | bytes 10485760 | tf_op jit(solution)/shard_map/reduce_scatter | solution.py:281
  417.2 768.6 %reduce-scatter.8.cloned.1.call-start = ((), (), s32[]{:S(2)}) async-start(), calls=%async_computation.7 | async-start | bytes 7864320 | tf_op jit(solution)/shard_map/reduce_scatter | solution.py:269
  738.4 8.7 copy-start.27
  738.4 8.7 copy-start.29
  806.1 489.2 %all-reduce.18.cloned.1.call-start = ((), (), s32[]{:S(2)}) async-start(), calls=%async_computation.11 | async-start | bytes 12582912 | tf_op jit(solution)/shard_map/psum | solution.py:291
  1185.8 10.8 copy-start.41
  1185.8 12.7 copy-start.40
  1203.6 41.0 %copy-start.35 = (f32[512]{0:T(512)S(1)}, f32[512]{0:T(512)}, u32[]{:S(2)}) copy-start(f32[512]{0:T(512)} %copy-done.34) | copy-start | bytes 6148
  (28 other events, 89.8 us)
Sparse Core Ops, SparseCore 0:
  63.2 152.3 all-gather.1
  366.8 364.5 reduce-scatter.5
  733.7 44.5 reduce-scatter.9
  780.6 143.7 reduce-scatter.11
  926.8 145.1 reduce-scatter.13
  1074.3 111.4 reduce-scatter.7
  1189.8 105.4 all-reduce.17
where the time goes:
time: 1330 us; the launch traced here: 1310 us
  waiting for transfers between devices  860 us (65%)
  local copies, waits for them, and re-layouts  179 us (13%)
  matrix products  147 us (11%)
  other arithmetic  61.9 us (5%)
  blocking collectives  30.1 us (2%)
  between operations  17.6 us (1%)
  loops' own time  16 us (1%)
    reduce_scatter x1, waiting for transfers between devices, body(): lax.psum_scatter(key_terms.astype(jnp.bfloat16), 'seq', scatter_dimension...  309 us
    reduce_scatter x1, waiting for transfers between devices, body(): lax.psum_scatter(down_weight_grad.astype(jnp.bfloat16), 'seq', scatter_di...  148 us
    all_gather x1, waiting for transfers between devices, body(): fetched_rows = lax.all_gather(key_value, 'seq', axis=0, tiled=True)  138 us
    reduce_scatter x1, waiting for transfers between devices, body(): lax.psum_scatter(qkv_weight_grad.astype(jnp.bfloat16), 'seq', scatter_dim...  114 us
    reduce_scatter x1, waiting for transfers between devices, body(): lax.psum_scatter(in_weight_grad.astype(jnp.bfloat16), 'seq', scatter_dime...  106 us
    psum x1, waiting for transfers between devices, body(): lax.psum(shares[2].astype(jnp.bfloat16), 'batch').astype(jnp.float32)  46.2 us
    unnamed x89, local copies, waits for them, and re-layouts  32.7 us
    dynamic_update_slice x8, local copies, waits for them, and re-layouts, body(): lax.scan(back_block, zero_heads, (jnp.arange(seq_count, dtype=jnp.int32),...  28.6 us
  transfers between devices with their start and end apart: 7, of which 6 were waited for; matrix products, arithmetic and copies ran while one was open for 14% of the time, Pallas kernels for 0%

commit v1 on v0

--- a/solution.py
+++ b/solution.py
@@ -1,14 +1,561 @@
+import math
+
 import jax
 import jax.numpy as jnp
+import numpy as np
 from jax import lax
+from jax.experimental import pallas as pl
+from jax.experimental.pallas import tpu as pltpu
 from jax.sharding import PartitionSpec as P
 
 HEAD_DIM = 64
 ROT = 32
-
+PAIR = 2 * HEAD_DIM
 
 EPSILON = 1e-05
 BLOCKED = -1e30
+LOG2E = math.log2(math.e)
+BF16 = jnp.bfloat16
+F32 = jnp.float32
+MIB = 1 << 20
+
+
+def dot_nn(left, right):
+    return lax.dot_general(left, right, (((1,), (0,)), ((), ())), preferred_element_type=F32)
+
+
+def dot_nt(left, right):
+    return lax.dot_general(left, right, (((1,), (1,)), ((), ())), preferred_element_type=F32)
+
+
+def dot_tn(left, right):
+    return lax.dot_general(left, right, (((0,), (0,)), ((), ())), preferred_element_type=F32)
+
+
+def swap_pairs(rows):
+    width = rows.shape[1]
+    lanes = lax.broadcasted_iota(jnp.int32, rows.shape, 1)
+    return jnp.where(lanes % 2 == 0, pltpu.roll(rows, width - 1, 1), pltpu.roll(rows, 1, 1))
+
+
+def trig_tables(length):
+    inverse = 10000.0 ** (-(np.arange(ROT // 2, dtype=np.float32) * np.float32(2.0)) / np.float32(ROT))
+    phases = np.arange(length, dtype=np.float32)[:, None] * inverse.astype(np.float32)[None, :]
+    cosine = np.ones((length, HEAD_DIM), np.float32)
+    sine = np.zeros((length, HEAD_DIM), np.float32)
+    cosine[:, :ROT] = np.repeat(np.cos(phases), 2, axis=1)
+    sine[:, :ROT] = np.repeat(np.sin(phases), 2, axis=1) * np.tile(np.array([-1.0, 1.0], np.float32), ROT // 2)
+    return np.tile(cosine, (1, 2)), np.tile(sine, (1, 2))
+
+
+def prep_kernel(hidden_ref, mark_ref, table_ref, gain_ref, bias_ref, stream_ref, normed_ref, turned_ref):
+    rows = hidden_ref.shape[0]
+    vocab = table_ref.shape[0]
+    onehot = (mark_ref[...] == lax.broadcasted_iota(jnp.int32, (rows, vocab), 1)).astype(F32).astype(BF16)
+    stream = hidden_ref[...].astype(F32) + dot_nn(onehot, table_ref[...])
+    centre = stream - jnp.mean(stream, axis=-1, keepdims=True)
+    spread = jnp.mean(centre * centre, axis=-1, keepdims=True)
+    normed = centre * lax.rsqrt(spread + EPSILON) * gain_ref[...] + bias_ref[...]
+    stream_ref[...] = stream
+    normed_ref[...] = normed.astype(BF16)
+    turned_ref[...] = normed.astype(BF16).T
+
+
+def prepare(hidden, marked, table, gain, bias):
+    rows, width = hidden.shape
+    step = 128
+    return pl.pallas_call(
+        prep_kernel,
+        grid=(rows // step,),
+        in_specs=[
+            pl.BlockSpec((step, width), lambda i: (i, 0)),
+            pl.BlockSpec((step, 1), lambda i: (i, 0)),
+            pl.BlockSpec(table.shape, lambda i: (0, 0)),
+            pl.BlockSpec((1, width), lambda i: (0, 0)),
+            pl.BlockSpec((1, width), lambda i: (0, 0)),
+        ],
+        out_specs=[
+            pl.BlockSpec((step, width), lambda i: (i, 0)),
+            pl.BlockSpec((step, width), lambda i: (i, 0)),
+            pl.BlockSpec((width, step), lambda i: (0, i)),
+        ],
+        out_shape=[
+            jax.ShapeDtypeStruct((rows, width), F32),
+            jax.ShapeDtypeStruct((rows, width), BF16),
+            jax.ShapeDtypeStruct((width, rows), BF16),
+        ],
+        name="prep",
+    )(hidden, marked, table, gain, bias)
+
+
+def heads_kernel(place_ref, normed_ref, cot_ref, wq_ref, wk_ref, wv_ref, wo_ref, cos_ref, sin_ref, *out_refs):
+    normed = normed_ref[...]
+    chunks = len(out_refs)
+    cosine = jnp.concatenate([cos_ref[...]] * chunks, axis=1)
+    sine = jnp.concatenate([sin_ref[...]] * chunks, axis=1)
+
+    def turned(rows):
+        return rows * cosine + swap_pairs(rows) * sine
+
+    parts = (
+        turned(dot_nn(normed, wq_ref[...])).astype(BF16),
+        turned(dot_nn(normed, wk_ref[...])).astype(BF16),
+        dot_nn(normed, wv_ref[...]).astype(BF16),
+        dot_nt(cot_ref[...], wo_ref[...]).astype(BF16),
+    )
+    for chunk in range(chunks):
+        for number, part in enumerate(parts):
+            out_refs[chunk][:, number * PAIR : (number + 1) * PAIR] = part[:, chunk * PAIR : (chunk + 1) * PAIR]
+
+
+def heads_of(owner, normed, cot, qkv_weight, out_weight, cosine, sine, owners):
+    rows, width = normed.shape
+    wide = width // owners
+    chunks = wide // PAIR
+    return pl.pallas_call(
+        heads_kernel,
+        grid_spec=pltpu.PrefetchScalarGridSpec(
+            num_scalar_prefetch=1,
+            grid=(1,),
+            in_specs=[
+                pl.BlockSpec((rows, width), lambda i, o: (0, 0)),
+                pl.BlockSpec((rows, width), lambda i, o: (0, 0)),
+                pl.BlockSpec((width, wide), lambda i, o: (0, o[0])),
+                pl.BlockSpec((width, wide), lambda i, o: (0, owners + o[0])),
+                pl.BlockSpec((width, wide), lambda i, o: (0, 2 * owners + o[0])),
+                pl.BlockSpec((wide, width), lambda i, o: (o[0], 0)),
+                pl.BlockSpec((rows, PAIR), lambda i, o: (0, 0)),
+                pl.BlockSpec((rows, PAIR), lambda i, o: (0, 0)),
+            ],
+            out_specs=[pl.BlockSpec((rows, 4 * PAIR), lambda i, o: (0, 0))] * chunks,
+        ),
+        out_shape=[jax.ShapeDtypeStruct((rows, 4 * PAIR), BF16)] * chunks,
+        name="heads",
+    )(owner, normed, cot, qkv_weight, qkv_weight, qkv_weight, out_weight, cosine, sine)
+
+
+QUERY_ROWS = 256
+KEY_ROWS = 256
+
+
+def attention_kernel(pieces, info_ref, *refs):
+    piece_refs = refs[:pieces]
+    cos_ref, sin_ref = refs[pieces : pieces + 2]
+    out_refs = refs[pieces + 2 : 2 * pieces + 2]
+    held, results, key_turned, value_turned, raised_ref, key_sum, value_sum = refs[2 * pieces + 2 :]
+    me, end = info_ref[0], info_ref[1]
+    rows = piece_refs[0].shape[0]
+    length = rows * pieces
+    for shift in range(pieces):
+        start = pl.multiple_of(lax.rem(me - shift + pieces, pieces) * rows, rows)
+        held[pl.ds(start, rows), :] = piece_refs[shift][...]
+    key_turned[...] = held[:, PAIR : 2 * PAIR].T
+    value_turned[...] = held[:, 2 * PAIR : 3 * PAIR].T
+    key_sum[...] = jnp.zeros_like(key_sum)
+    value_sum[...] = jnp.zeros_like(value_sum)
+    scale = 0.125 * LOG2E
+    halves = lax.broadcasted_iota(jnp.int32, (QUERY_ROWS, PAIR), 1) // HEAD_DIM
+
+    def query_block(number, carry):
+        first = pl.multiple_of(number * QUERY_ROWS, QUERY_ROWS)
+        query_rows = held[pl.ds(first, QUERY_ROWS), 0:PAIR]
+        grad_rows = held[pl.ds(first, QUERY_ROWS), 3 * PAIR : 4 * PAIR]
+        zero = jnp.zeros_like(query_rows)
+        queries = [jnp.where(halves == head, query_rows, zero) for head in range(2)]
+        grads = [jnp.where(halves == head, grad_rows, zero) for head in range(2)]
+        query_places = first + lax.broadcasted_iota(jnp.int32, (1, QUERY_ROWS), 1)
+        lowest = jnp.where(query_places > end, end + 1, 0)
+        blocks = (number + 1) * (QUERY_ROWS // KEY_ROWS) if QUERY_ROWS >= KEY_ROWS else lax.div(
+            number * QUERY_ROWS, KEY_ROWS
+        ) + 1
+
+        def scores_of(block, highest):
+            start = pl.multiple_of(block * KEY_ROWS, KEY_ROWS)
+            keys = held[pl.ds(start, KEY_ROWS), PAIR : 2 * PAIR]
+            key_places = start + lax.broadcasted_iota(jnp.int32, (KEY_ROWS, QUERY_ROWS), 0)
+            seen = (key_places <= query_places) & (key_places >= lowest)
+            after = []
+            for head in range(2):
+                scores = jnp.where(seen, dot_nt(keys, queries[head]) * scale, BLOCKED)
+                raised_ref[head, pl.ds(start, KEY_ROWS), :] = scores
+                after.append(jnp.maximum(highest[head], jnp.max(scores, axis=0, keepdims=True)))
+            return tuple(after)
+
+        start_row = jnp.full((1, QUERY_ROWS), BLOCKED, F32)
+        highest = lax.fori_loop(0, blocks, scores_of, (start_row, start_row))
+
+        def mix(block, carried):
+            start = pl.multiple_of(block * KEY_ROWS, KEY_ROWS)
+            after = []
+            for head in range(2):
+                total, mixed = carried[head]
+                raised = jnp.exp2(raised_ref[head, pl.ds(start, KEY_ROWS), :] - highest[head])
+                raised_ref[head, pl.ds(start, KEY_ROWS), :] = raised
+                values = value_turned[head * HEAD_DIM : (head + 1) * HEAD_DIM, pl.ds(start, KEY_ROWS)]
+                after.append(
+                    (total + jnp.sum(raised, axis=0, keepdims=True), mixed + dot_nn(values, raised.astype(BF16)))
+                )
+            return tuple(after)
+
+        empty = (jnp.zeros((1, QUERY_ROWS), F32), jnp.zeros((HEAD_DIM, QUERY_ROWS), F32))
+        mixes = lax.fori_loop(0, blocks, mix, (empty, empty))
+        inverse = [1.0 / mixes[head][0] for head in range(2)]
+        mixed = jnp.concatenate([mixes[head][1] * inverse[head] for head in range(2)], axis=0)
+        grad_turned = grad_rows.astype(F32).T
+        products = mixed * grad_turned
+        delta = [
+            jnp.sum(products[head * HEAD_DIM : (head + 1) * HEAD_DIM], axis=0, keepdims=True) for head in range(2)
+        ]
+
+        def back(block, carried):
+            start = pl.multiple_of(block * KEY_ROWS, KEY_ROWS)
+            values = held[pl.ds(start, KEY_ROWS), 2 * PAIR : 3 * PAIR]
+            after, key_terms, value_terms = [], [], []
+            for head in range(2):
+                probs = raised_ref[head, pl.ds(start, KEY_ROWS), :] * inverse[head]
+                prob_grad = dot_nt(values, grads[head])
+                score_grad = (probs * (prob_grad - delta[head])).astype(BF16)
+                value_terms.append(dot_nn(probs.astype(BF16), grads[head]))
+                key_terms.append(dot_nn(score_grad, queries[head]))
+                keys = key_turned[head * HEAD_DIM : (head + 1) * HEAD_DIM, pl.ds(start, KEY_ROWS)]
+                after.append(carried[head] + dot_nn(keys, score_grad))
+            value_sum[pl.ds(start, KEY_ROWS), :] += value_terms[0] + value_terms[1]
+            key_sum[pl.ds(start, KEY_ROWS), :] += key_terms[0] + key_terms[1]
+            return tuple(after)
+
+        query_grads = lax.fori_loop(0, blocks, back, (empty[1], empty[1]))
+        query_grad = jnp.concatenate(query_grads, axis=0).T * 0.125
+        cosine = cos_ref[pl.ds(first, QUERY_ROWS), :]
+        sine = sin_ref[pl.ds(first, QUERY_ROWS), :]
+        results[pl.ds(first, QUERY_ROWS), 0:PAIR] = (query_grad * cosine - swap_pairs(query_grad) * sine).astype(BF16)
+        results[pl.ds(first, QUERY_ROWS), 3 * PAIR : 4 * PAIR] = mixed.T.astype(BF16)
+        return carry
+
+    lax.fori_loop(0, length // QUERY_ROWS, query_block, 0)
+    key_grad = key_sum[...] * 0.125
+    results[:, PAIR : 2 * PAIR] = (key_grad * cos_ref[...] - swap_pairs(key_grad) * sin_ref[...]).astype(BF16)
+    results[:, 2 * PAIR : 3 * PAIR] = value_sum[...].astype(BF16)
+    for shift in range(pieces):
+        start = pl.multiple_of(lax.rem(me + shift, pieces) * rows, rows)
+        out_refs[shift][...] = results[pl.ds(start, rows), :]
+
+
+def attention(info, parts, cosine, sine):
+    pieces = len(parts)
+    rows, wide = parts[0].shape
+    length = rows * pieces
+    whole = pl.BlockSpec(memory_space=pltpu.VMEM)
+    blocks = length // QUERY_ROWS
+    pairs_of = 2 * blocks * (blocks + 1) // 2 * QUERY_ROWS * KEY_ROWS
+    return pl.pallas_call(
+        lambda *refs: attention_kernel(pieces, *refs),
+        in_specs=[pl.BlockSpec(memory_space=pltpu.SMEM)] + [whole] * (pieces + 2),
+        out_specs=[whole] * pieces,
+        out_shape=[jax.ShapeDtypeStruct((rows, wide), BF16)] * pieces,
+        scratch_shapes=[
+            pltpu.VMEM((length, wide), BF16),
+            pltpu.VMEM((length, wide), BF16),
+            pltpu.VMEM((PAIR, length), BF16),
+            pltpu.VMEM((PAIR, length), BF16),
+            pltpu.VMEM((2, length, QUERY_ROWS), F32),
+            pltpu.VMEM((length, PAIR), F32),
+            pltpu.VMEM((length, PAIR), F32),
+        ],
+        compiler_params=pltpu.CompilerParams(vmem_limit_bytes=40 * MIB),
+        cost_estimate=pl.CostEstimate(
+            flops=12 * 256 * pairs_of, bytes_accessed=2 * 2 * length * wide * 2, transcendentals=pairs_of
+        ),
+        name="attention",
+    )(info, *parts, cosine, sine)
+
+
+def feed_kernel(
+    cells, normed_ref, turned_ref, cot_ref, in_ref, bias_ref, down_ref, in_grad, down_grad, bias_grad, out_sum, norm_sum
+):
+    step = pl.program_id(0)
+    up = math.sqrt(2.0 / math.pi)
+    weights = in_ref[...]
+    downs = down_ref[...]
+    cot = cot_ref[...]
+    pre = dot_nn(normed_ref[...], weights) + bias_ref[...]
+    square = pre * pre
+    tanh = jnp.tanh(up * pre * (1.0 + 0.044715 * square))
+    half = 0.5 * (1.0 + tanh)
+    active = (pre * half).astype(BF16)
+    slope = half + 0.5 * pre * (1.0 - tanh * tanh) * (up * (1.0 + 3 * 0.044715 * square))
+    pre_grad_full = (dot_nt(cot, downs) * slope).astype(BF16)
+    in_grad[0] = dot_nn(turned_ref[...], pre_grad_full).astype(BF16)
+    down_grad[0] = dot_tn(active, cot).astype(BF16)
+    bias_grad[0] = jnp.sum(pre_grad_full.astype(F32), axis=0, keepdims=True)
+    out_term = dot_nn(active, downs)
+    norm_term = dot_nt(pre_grad_full, weights)
+
+    @pl.when(step == 0)
+    def _():
+        out_sum[...] = out_term
+        norm_sum[...] = norm_term
+
+    @pl.when(step > 0)
+    def _():
+        out_sum[...] += out_term
+        norm_sum[...] += norm_term
+
+
+def feed_half(cells, normed, turned, cot, in_weight, in_bias, down_weight):
+    rows, width = normed.shape
+    tiles = cells.shape[0]
+    hidden_units = in_weight.shape[1]
+    tile = hidden_units // (2 * tiles)
+    return pl.pallas_call(
+        feed_kernel,
+        grid_spec=pltpu.PrefetchScalarGridSpec(
+            num_scalar_prefetch=1,
+            grid=(tiles,),
+            in_specs=[
+                pl.BlockSpec((rows, width), lambda i, c: (0, 0)),
+                pl.BlockSpec((width, rows), lambda i, c: (0, 0)),
+                pl.BlockSpec((rows, width), lambda i, c: (0, 0)),
+                pl.BlockSpec((width, tile), lambda i, c: (0, c[i])),
+                pl.BlockSpec((1, tile), lambda i, c: (0, c[i])),
+                pl.BlockSpec((tile, width), lambda i, c: (c[i], 0)),
+            ],
+            out_specs=[
+                pl.BlockSpec((1, width, tile), lambda i, c: (i, 0, 0)),
+                pl.BlockSpec((1, tile, width), lambda i, c: (i, 0, 0)),
+                pl.BlockSpec((1, 1, tile), lambda i, c: (i, 0, 0)),
+                pl.BlockSpec((rows, width), lambda i, c: (0, 0)),
+                pl.BlockSpec((rows, width), lambda i, c: (0, 0)),
+            ],
+        ),
+        out_shape=[
+            jax.ShapeDtypeStruct((tiles, width, tile), BF16),
+            jax.ShapeDtypeStruct((tiles, tile, width), BF16),
+            jax.ShapeDtypeStruct((tiles, 1, tile), F32),
+            jax.ShapeDtypeStruct((rows, width), F32),
+            jax.ShapeDtypeStruct((rows, width), F32),
+        ],
+        compiler_params=pltpu.CompilerParams(vmem_limit_bytes=56 * MIB),
+        cost_estimate=pl.CostEstimate(
+            flops=12 * rows * width * hidden_units // 2,
+            bytes_accessed=8 * width * hidden_units // 2,
+            transcendentals=rows * hidden_units // 2,
+        ),
+        name="feed",
+    )(cells, normed, turned, cot, in_weight, in_bias, down_weight)
+
+
+def exchange(rows, axis, mask):
+    size = lax.axis_size(axis)
+    return lax.ppermute(rows, axis, [(place, place ^ mask) for place in range(size)])
+
+
+def halves_of(rows, dim, bit):
+    shape = rows.shape[:dim] + (2, rows.shape[dim] // 2) + rows.shape[dim + 1 :]
+    split = rows.reshape(shape)
+    return (
+        lax.dynamic_index_in_dim(split, 1 - bit, dim, keepdims=False),
+        lax.dynamic_index_in_dim(split, bit, dim, keepdims=False),
+    )
+
+
+def added(left, right):
+    return (left.astype(F32) + right.astype(F32)).astype(BF16)
+
+
+def joined(mine, other, dim, bit):
+    low = jnp.where(bit == 0, mine, other)
+    high = jnp.where(bit == 0, other, mine)
+    return jnp.concatenate([low, high], axis=dim)
+
+
+def bits_of(axis):
+    return lax.axis_size(axis).bit_length() - 1
+
+
+def reduce_over(rows, order):
+    place = lax.axis_index("batch")
+    for bit_number in order:
+        bit = (place >> bit_number) & 1
+        sent, kept = halves_of(rows, 2, bit)
+        rows = added(kept, exchange(sent, "batch", 1 << bit_number))
+    place = lax.axis_index("seq")
+    for bit_number in range(bits_of("seq")):
+        bit = (place >> bit_number) & 1
+        shape = rows.shape
+        split = rows.reshape((shape[0], shape[1] // 2, 2) + shape[2:])
+        sent = lax.dynamic_index_in_dim(split, 1 - bit, 2, keepdims=False)
+        kept = lax.dynamic_index_in_dim(split, bit, 2, keepdims=False)
+        rows = added(kept, exchange(sent, "seq", 1 << bit_number))
+    return rows
+
+
+def gather_over(rows, order):
+    place = lax.axis_index("batch")
+    for bit_number in reversed(order):
+        bit = (place >> bit_number) & 1
+        rows = joined(rows, exchange(rows, "batch", 1 << bit_number), 2, bit)
+    return rows
+
+
+def sum_over_devices(sent, kept):
+    rows = added(kept, exchange(sent, "batch", 1))
+    order = list(range(1, bits_of("batch")))
+    middle = rows.shape[2] // 2
+    ends = []
+    for part, bits in ((rows[:, :, :middle], order), (rows[:, :, middle:], order[::-1])):
+        ends.append(gather_over(reduce_over(part, bits), bits))
+    mine = jnp.concatenate(ends, axis=2)[:, 0]
+    other = exchange(mine, "batch", 1)
+    return joined(mine[None], other[None], 0, lax.axis_index("batch") & 1)
+
+
+def fast_body(
+    hidden,
+    token_ids,
+    offsets,
+    end_places,
+    token_table,
+    norm_gain,
+    norm_bias,
+    qkv_weight,
+    out_weight,
+    in_weight,
+    in_bias,
+    down_weight,
+    down_bias,
+    cotangent,
+):
+    width = hidden.shape[2]
+    rows = hidden.shape[1]
+    owners = lax.axis_size("seq")
+    me = lax.axis_index("seq")
+    core = lax.axis_index("batch") & 1
+    length = rows * owners
+    chunks = width // owners // PAIR
+    end = end_places[0]
+
+    places = me * rows + jnp.arange(rows, dtype=jnp.int32)[:, None]
+    marked = token_ids.reshape(rows, 1)
+    marked = jnp.where(places == end, 2, marked)
+    marked = jnp.where(places == end + 1, 1, marked)
+    marked = jnp.where((places == 0) & (offsets[0] == 0), 1, marked)
+    cot = cotangent.reshape(rows, width)
+    stream, normed, turned = prepare(
+        hidden.reshape(rows, width), marked, token_table, norm_gain[None], norm_bias[None]
+    )
+    cosine, sine = (jnp.asarray(table) for table in trig_tables(length))
+    own_cosine = lax.dynamic_slice_in_dim(cosine, me * rows, rows)
+    own_sine = lax.dynamic_slice_in_dim(sine, me * rows, rows)
+
+    parts = [[None] * owners for _ in range(chunks)]
+    for shift in list(range(1, owners)) + [0]:
+        owner = lax.rem(me + shift, owners)
+        blocks = heads_of(owner[None], normed, cot, qkv_weight, out_weight, own_cosine, own_sine, owners)
+        for chunk in range(chunks):
+            parts[chunk][shift] = blocks[chunk]
+
+    def shifted(block, shift):
+        if shift == 0:
+            return block
+        return lax.ppermute(block, "seq", [(place, (place + shift) % owners) for place in range(owners)])
+
+    heads = [[shifted(parts[chunk][shift], shift) for shift in range(owners)] for chunk in range(chunks)]
+
+    cells = 2 * jnp.arange(owners, dtype=jnp.int32)
+    feed = [
+        feed_half(cells + half, normed, turned, cot, in_weight, in_bias[None], down_weight)
+        for half in (1 - core, core)
+    ]
+    tile = in_weight.shape[1] // (2 * owners)
+
+    def in_view(grad):
+        return grad.reshape(owners, owners, width // owners, tile)
+
+    def down_view(grad):
+        return grad.reshape(1, owners, tile, width)
+
+    in_sum = sum_over_devices(in_view(feed[0][0]), in_view(feed[1][0]))
+    down_sum = sum_over_devices(down_view(feed[0][1]), down_view(feed[1][1]))
+    in_weight_grad = jnp.transpose(in_sum, (2, 1, 0, 3)).reshape(width // owners, in_weight.shape[1]).astype(F32)
+    down_weight_grad = down_sum.reshape(2 * tile, width).astype(F32)
+    bias_low = jnp.where(core == 0, feed[1][2], feed[0][2])
+    bias_high = jnp.where(core == 0, feed[0][2], feed[1][2])
+    in_bias_grad = jnp.concatenate([bias_low, bias_high], axis=1).reshape(-1)
+
+    info = jnp.stack([me, end]).astype(jnp.int32)
+    back = []
+    for chunk in range(chunks):
+        results = attention(info, heads[chunk], cosine, sine)
+        back.append([shifted(results[shift], shift) for shift in range(owners)])
+
+    ordered = []
+    for owner in range(owners):
+        ordered.append([])
+        for chunk in range(chunks):
+            stacked = jnp.stack(back[chunk])
+            slot = lax.rem(me - owner + owners, owners)
+            ordered[owner].append(lax.dynamic_index_in_dim(stacked, slot, 0, keepdims=False))
+
+    def columns(part):
+        return [
+            block[:, part * PAIR : (part + 1) * PAIR] for blocks in ordered for block in blocks
+        ]
+
+    joined_grad = jnp.concatenate(columns(0) + columns(1) + columns(2), axis=1)
+    mixed = jnp.concatenate(columns(3), axis=1)
+
+    qkv_weight_grad = dot_nn(turned, joined_grad).astype(BF16)
+    out_weight_grad = dot_tn(mixed, cot).astype(BF16)
+    normed_grad = dot_nt(joined_grad, qkv_weight) + feed[0][4] + feed[1][4]
+
+    def core_halves(grad):
+        split = grad.reshape(1, owners, 2, grad.shape[0] // (2 * owners), grad.shape[1])
+        return (
+            lax.dynamic_index_in_dim(split, 1 - core, 2, keepdims=False),
+            lax.dynamic_index_in_dim(split, core, 2, keepdims=False),
+        )
+
+    qkv_sum = sum_over_devices(*core_halves(qkv_weight_grad))
+    out_sum = sum_over_devices(*core_halves(out_weight_grad))
+    qkv_weight_grad = qkv_sum.reshape(width // owners, -1).astype(F32)
+    out_weight_grad = out_sum.reshape(width // owners, -1).astype(F32)
+
+    output = stream + dot_nn(mixed, out_weight) + feed[0][3] + feed[1][3] + down_bias[None]
+    centre = stream - jnp.mean(stream, axis=-1, keepdims=True)
+    spread = jnp.mean(centre * centre, axis=-1, keepdims=True)
+    inverse = lax.rsqrt(spread + EPSILON)
+    hat = centre * inverse
+    gained = normed_grad * norm_gain[None]
+    stream_part = inverse * (
+        gained
+        - jnp.mean(gained, axis=-1, keepdims=True)
+        - hat * jnp.mean(gained * hat, axis=-1, keepdims=True)
+    )
+    hidden_grad = cot.astype(F32) + stream_part
+    small = jnp.concatenate(
+        [
+            in_bias_grad.reshape(owners, -1),
+            jnp.sum(cot.astype(F32), axis=0).reshape(owners, -1),
+            jnp.sum(normed_grad * hat, axis=0).reshape(owners, -1),
+            jnp.sum(normed_grad, axis=0).reshape(owners, -1),
+        ],
+        axis=1,
+    )
+    small = lax.dynamic_index_in_dim(lax.psum(small, ("batch", "seq")), me, 0, keepdims=False)
+    few = width // owners
+    many = in_bias.shape[0] // owners
+    return (
+        output.astype(BF16)[None],
+        hidden_grad[None],
+        small[many + few : many + 2 * few],
+        small[many + 2 * few :],
+        qkv_weight_grad,
+        out_weight_grad,
+        in_weight_grad,
+        small[:many],
+        down_weight_grad,
+        small[many : many + few],
+    )
 
 
 def rotate(vectors, cosine_table, sine_table):
@@ -47,7 +594,7 @@
     return jax.nn.gelu(pre_active, approximate=True)
 
 
-def body(
+def plain_body(
     hidden,
     token_ids,
     offsets,
@@ -326,6 +873,15 @@
         P(),
         P("batch", "seq", None),
     )
+
+    def body(*arrays):
+        hidden = arrays[0]
+        owners = mesh.shape["seq"]
+        wide = hidden.shape[2] // owners
+        if hidden.shape[0] == 1 and wide % PAIR == 0:
+            return fast_body(*arrays)
+        return plain_body(*arrays)
+
     return jax.shard_map(
         body,
         mesh=mesh,

time: 1330 us -> 538 us (0.40)
  waiting for transfers between devices: 860 us -> 152 us
  Pallas kernels: 0 us -> 162 us
  local copies, waits for them, and re-layouts: 179 us -> 28.3 us
  matrix products: 147 us -> 16.1 us
  starting transfers between devices: 0.87 us -> 89.9 us
  other arithmetic: 61.9 us -> 41.2 us
  loops' own time: 16 us -> 0 us
  between operations: 17.6 us -> 3.7 us
    reduce_scatter x5 -> x0, waiting for transfers between devices: 675 us -> none  [the longest x1 309 us: body(): lax.psum_scatter(key_terms.astype(jnp.bfloat16), 'seq', scatter_dimension...]
    pallas_call x0 -> x9, Pallas kernels: none -> 162 us  [the longest x2 93.1 us: attention(): pl.pallas_call(lambda *refs: attention_kernel(pieces, *refs), in_specs=[p...]
    ppermute x0 -> x68, waiting for transfers between devices: none -> 152 us  [the longest x56 122 us: exchange(): lax.ppermute(rows, axis, [(place, place ^ mask) for place in range(size)])]
    all_gather x1 -> x0, waiting for transfers between devices: 138 us -> none  [body(): fetched_rows = lax.all_gather(key_value, 'seq', axis=0, tiled=True)]
    dot_general x20 -> x4, matrix products: 147 us -> 16.1 us  [the longest x2 7.62 us: dot_nn(): lax.dot_general(left, right, (((1,), (0,)), ((), ())), preferred_element_...]
    ppermute x0 -> x68, starting transfers between devices: none -> 89.9 us  [the longest x56 69.4 us: exchange(): lax.ppermute(rows, axis, [(place, place ^ mask) for place in range(size)])]
    psum x1 -> x0, waiting for transfers between devices: 46.2 us -> none  [body(): lax.psum(shares[2].astype(jnp.bfloat16), 'batch').astype(jnp.float32)]
    pad x4 -> x0, local copies, waits for them, and re-layouts: 39.6 us -> none  [the longest x2 19.8 us: rotate(): even_part = vectors[..., 0:ROT:2]]
  transfers between devices with their start and end apart: 7 -> 68, of which waited for: 6 -> 30; matrix products, arithmetic and copies ran while one was open for 14% -> 12% of each run, Pallas kernels for 0% -> 29%
where the time goes in v1:
time: 538 us; the launch traced here: 533 us
  Pallas kernels  162 us (30%)
  waiting for transfers between devices  152 us (28%)
  starting transfers between devices  89.9 us (17%)
  other arithmetic  41.2 us (8%)
  blocking collectives  40.2 us (7%)
  local copies, waits for them, and re-layouts  28.3 us (5%)
  matrix products  16.1 us (3%)
    ppermute x56, waiting for transfers between devices, exchange(): lax.ppermute(rows, axis, [(place, place ^ mask) for place in range(size)])  122 us
    pallas_call x2, Pallas kernels, attention(): pl.pallas_call(lambda *refs: attention_kernel(pieces, *refs), in_specs=[p...  93.1 us
    ppermute x56, starting transfers between devices, exchange(): lax.ppermute(rows, axis, [(place, place ^ mask) for place in range(size)])  69.4 us
    pallas_call x2, Pallas kernels, feed_half(): pl.pallas_call(feed_kernel, grid_spec=pltpu.PrefetchScalarGridSpec(num_sc...  45.7 us
    psum x1, blocking collectives, fast_body(): lax.psum(small, ('batch', 'seq'))  40.2 us
    ppermute x12, waiting for transfers between devices, shifted(): lax.ppermute(block, 'seq', [(place, (place + shift) % owners) for place i...  30.6 us
    convert_element_type x36, other arithmetic, added(): return (left.astype(F32) + right.astype(F32)).astype(BF16)  20.8 us
    ppermute x12, starting transfers between devices, shifted(): lax.ppermute(block, 'seq', [(place, (place + shift) % owners) for place i...  20.4 us
  transfers between devices with their start and end apart: 68, of which 30 were waited for; matrix products, arithmetic and copies ran while one was open for 12% of the time, Pallas kernels for 29%

profile of v1, /device:TPU:0, one launch (start us, length us, event | category | flops | bytes accessed | tf_op | source)
XLA Modules:
  0.0 533.3 jit_solution(18155978479548624458)
XLA Ops:
  5.5 4.6 prep.1
  10.0 4.6 heads.5
  17.6 4.5 heads.6
  24.7 4.6 heads.7
  32.9 22.9 %feed.2 = (bf16[4,1024,512]{2,1,0:T(8,128)(2,1)}, bf16[4,512,1024]{2,1,0:T(8,128)(2,1)}, f32[4,1,512]{2,1,0:T(1,128)}, f32[512,1024]{1,0:T(8,128)}, f32[512,1024]{1,0:T(8,128)}) custom-call(s32[4]{0:T(128)} %fusion.35.cells, bf16[512,1024]{1,0:T(8,128)(2,1)} %get-tuple-element.40.normed_ref, bf16[1024,512]{1,0:T(8,128)(2,1)} %get-tuple-element.57.turned_ref, ...), custom_call_target="tpu_custom_call" | custom-call | flops 12884901888 | bytes 16777216 | tf_op jit(solution)/shard_map/feed/pallas_call | solution.py:309
  55.8 22.8 %feed.3 = (bf16[4,1024,512]{2,1,0:T(8,128)(2,1)}, bf16[4,512,1024]{2,1,0:T(8,128)(2,1)}, f32[4,1,512]{2,1,0:T(1,128)}, f32[512,1024]{1,0:T(8,128)}, f32[512,1024]{1,0:T(8,128)}) custom-call(s32[4]{0:T(128)} %fusion.34.cells, bf16[512,1024]{1,0:T(8,128)(2,1)} %get-tuple-element.40.normed_ref, bf16[1024,512]{1,0:T(8,128)(2,1)} %get-tuple-element.57.turned_ref, ...), custom_call_target="tpu_custom_call" | custom-call | flops 12884901888 | bytes 16777216 | tf_op jit(solution)/shard_map/feed/pallas_call | solution.py:309
  79.4 4.5 heads.4
  90.5 46.6 %attention.3 = (bf16[512,512]{1,0:T(8,128)(2,1)S(1)}, bf16[512,512]{1,0:T(8,128)(2,1)S(1)}, bf16[512,512]{1,0:T(8,128)(2,1)S(1)}, bf16[512,512]{1,0:T(8,128)(2,1)S(1)}) custom-call(s32[2]{0:T(128)S(1)} %pad_add_fusion.refs_0_, bf16[512,512]{1,0:T(8,128)(2,1)S(1)} %copy-done.3, bf16[512,512]{1,0:T(8,128)(2,1)S(1)} %collective-permute-done.6.refs_2_, ...), custom_call_target="tpu_custom_call" | custom-call | flops 14495514624 | bytes 8388608 | tf_op jit(solution)/shard_map/attention/pallas_call | solution.py:250
  142.1 46.5 %attention.2 = (bf16[512,512]{1,0:T(8,128)(2,1)S(1)}, bf16[512,512]{1,0:T(8,128)(2,1)S(1)}, bf16[512,512]{1,0:T(8,128)(2,1)S(1)}, bf16[512,512]{1,0:T(8,128)(2,1)S(1)}) custom-call(s32[2]{0:T(128)S(1)} %pad_add_fusion.refs_0_, bf16[512,512]{1,0:T(8,128)(2,1)S(1)} %copy-done.2, bf16[512,512]{1,0:T(8,128)(2,1)S(1)} %collective-permute-done.refs_2_, ...), custom_call_target="tpu_custom_call" | custom-call | flops 14495514624 | bytes 8388608 | tf_op jit(solution)/shard_map/attention/pallas_call | solution.py:250
  193.7 11.6 %collective-permute-done.3 = bf16[512,512]{1,0:T(8,128)(2,1)S(1)} collective-permute-done((bf16[512,512]{1,0:T(8,128)(2,1)S(1)}, bf16[512,512]{1,0:T(8,128)(2,1)S(1)}, u32[]{:S(2)}, u32[]{:S(2)}) %collective-permute-start.3) | collective-permute-done | bytes 524320 | tf_op jit(solution)/shard_map/ppermute | solution.py:460
  205.4 18.9 %collective-permute-done.4 = bf16[512,512]{1,0:T(8,128)(2,1)S(1)} collective-permute-done((bf16[512,512]{1,0:T(8,128)(2,1)S(1)}, bf16[512,512]{1,0:T(8,128)(2,1)S(1)}, u32[]{:S(2)}, u32[]{:S(2)}) %collective-permute-start.4) | collective-permute-done | bytes 524320 | tf_op jit(solution)/shard_map/ppermute | solution.py:460
  237.0 7.2 %multiply_reduce_fusion = (f32[1024]{0:T(1024)S(1)}, f32[512]{0:T(512)S(1)}, f32[512]{0:T(512)S(1)}, f32[1024]{0:T(1024)S(1)}, f32[512,1024]{1,0:T(8,128)S(1)}) fusion(f32[512,1024]{1,0:T(8,128)S(1)} %copy-done.6, f32[512]{0:T(512)S(1)} %add_rsqrt_fusion, f32[512]{0:T(512)S(1)} %broadcast_multiply_fusion.2, f32[1024]{0:T(1024)S(1)} %copy-done.10, ...), kind=kOutput, calls=%fused_computation.26 | convolution fusion | flops 3226989568 | bytes 17846272 | tf_op jit(solution)/shard_map/dot_general | solution.py:28
  266.8 10.9 %collective-permute-start.29 = (bf16[1,2,16,1024]{3,2,1,0:T(8,128)(2,1)S(1)}, bf16[1,2,16,1024]{3,2,1,0:T(8,128)(2,1)S(1)}, u32[]{:S(2)}, u32[]{:S(2)}) collective-permute-start(bf16[1,2,16,1024]{3,2,1,0:T(8,128)(2,1)S(1)} %dynamic-slice_bitcast_fusion.33), channel_id=1, source_target_pairs={{0,1},{1,0},{2,3},{3,2},{4,5},{5,4},{6,7},{7,6},{8,9},{9,8},{10,11... | collective-permute-start | bytes 196616 | tf_op jit(solution)/shard_map/ppermute | solution.py:349
  298.0 40.2 %psum.7 = f32[4,1792]{1,0:T(4,128)S(1)} all-reduce(f32[4,1792]{1,0:T(4,128)S(1)} %pad_maximum_fusion.16), channel_id=1, replica_groups=mesh['batch'=8,'seq'=4] {'batch','seq'}, use_global_device_ids=true, to_apply=%region_7.8 | all-reduce | flops 7168 | bytes 57344 | tf_op jit(solution)/shard_map/psum | solution.py:544
  341.7 5.7 %fusion = bf16[1,4,512,1024]{3,2,1,0:T(8,128)(2,1)S(1)} fusion(bf16[1,4,512,1024]{3,2,1,0:T(8,128)(2,1)} %collective-permute-done.54, bf16[4,512,1024]{2,1,0:T(8,128)(2,1)} %get-tuple-element.66), kind=kLoop, calls=%fused_computation.1 | loop fusion | flops 8388608 | bytes 12582912 | tf_op jit(solution)/shard_map/convert_element_type | solution.py:362
  362.4 28.8 %collective-permute-done.13 = bf16[1,4,32,3072]{3,2,1,0:T(8,128)(2,1)S(1)} collective-permute-done((bf16[1,4,32,3072]{3,2,1,0:T(8,128)(2,1)S(1)}, bf16[1,4,32,3072]{3,2,1,0:T(8,128)(2,1)S(1)}, u32[]{:S(2)}, u32[]{:S(2)}) %collective-permute-start.13) | collective-permute-done | bytes 786464 | tf_op jit(solution)/shard_map/ppermute | solution.py:349
  393.6 20.2 %collective-permute-done.19 = bf16[1,4,32,3072]{3,2,1,0:T(8,128)(2,1)S(1)} collective-permute-done((bf16[1,4,32,3072]{3,2,1,0:T(8,128)(2,1)S(1)}, bf16[1,4,32,3072]{3,2,1,0:T(8,128)(2,1)S(1)}, u32[]{:S(2)}, u32[]{:S(2)}) %collective-permute-start.19) | collective-permute-done | bytes 786464 | tf_op jit(solution)/shard_map/ppermute | solution.py:349
  427.0 5.3 collective-permute-done.15
  432.7 5.3 collective-permute-done.21
  439.6 4.7 collective-permute-done.16
  445.1 5.4 %collective-permute-done.22 = bf16[1,1,16,3072]{3,2,1,0:T(8,128)(2,1)S(1)} collective-permute-done((bf16[1,1,16,3072]{3,2,1,0:T(8,128)(2,1)S(1)}, bf16[1,1,16,3072]{3,2,1,0:T(8,128)(2,1)S(1)}, u32[]{:S(2)}, u32[]{:S(2)}) %collective-permute-start.22) | collective-permute-done | bytes 98336 | tf_op jit(solution)/shard_map/ppermute | solution.py:349
  476.2 11.5 %collective-permute-done.58 = bf16[1,1,64,1024]{3,2,1,0:T(8,128)(2,1)S(1)} collective-permute-done((bf16[1,1,64,1024]{3,2,1,0:T(8,128)(2,1)S(1)}, bf16[1,1,64,1024]{3,2,1,0:T(8,128)(2,1)S(1)}, u32[]{:S(2)}, u32[]{:S(2)}) %collective-permute-start.58) | collective-permute-done | bytes 131104 | tf_op jit(solution)/shard_map/ppermute | solution.py:349
  522.2 5.2 copy.47
  527.5 5.6 %copy.51 = f32[256,4096]{1,0:T(8,128)} copy(f32[256,4096]{0,1:T(8,128)} %bitcast.287) | data formatting | bytes 8388608
  (337 shorter events, 181.4 us)
Async XLA Ops:
  14.6 71.5 %collective-permute-start.6 = (bf16[512,512]{1,0:T(8,128)(2,1)}, bf16[512,512]{1,0:T(8,128)(2,1)S(1)}, u32[]{:S(2)}, u32[]{:S(2)}) collective-permute-start(bf16[512,512]{1,0:T(8,128)(2,1)} %get-tuple-element.50), channel_id=1, source_target_pairs={{0,1},{1,2},{2,3},{3,0},{4,5},{5,6},{6,7},{7,4},{8,9},{9,10},{10,1... | collective-permute-start | bytes 1572872 | tf_op jit(solution)/shard_map/ppermute | solution.py:460
  22.1 67.3 %collective-permute-start.7 = (bf16[512,512]{1,0:T(8,128)(2,1)}, bf16[512,512]{1,0:T(8,128)(2,1)}, u32[]{:S(2)}, u32[]{:S(2)}) collective-permute-start(bf16[512,512]{1,0:T(8,128)(2,1)} %get-tuple-element.51), channel_id=1, source_target_pairs={{0,2},{1,3},{2,0},{3,1},{4,6},{5,7},{6,4},{7,5},{8,10},{9,11},{10,... | collective-permute-start | bytes 1572872 | tf_op jit(solution)/shard_map/ppermute | solution.py:460
  29.3 60.1 %collective-permute-start.8 = (bf16[512,512]{1,0:T(8,128)(2,1)}, bf16[512,512]{1,0:T(8,128)(2,1)}, u32[]{:S(2)}, u32[]{:S(2)}) collective-permute-start(bf16[512,512]{1,0:T(8,128)(2,1)} %get-tuple-element.52), channel_id=1, source_target_pairs={{0,3},{1,0},{2,1},{3,2},{4,7},{5,4},{6,5},{7,6},{8,11},{9,8},{10,9... | collective-permute-start | bytes 1572872 | tf_op jit(solution)/shard_map/ppermute | solution.py:460
  30.6 108.5 %collective-permute-start = (bf16[512,512]{1,0:T(8,128)(2,1)}, bf16[512,512]{1,0:T(8,128)(2,1)S(1)}, u32[]{:S(2)}, u32[]{:S(2)}) collective-permute-start(bf16[512,512]{1,0:T(8,128)(2,1)} %get-tuple-element.42), channel_id=1, source_target_pairs={{0,1},{1,2},{2,3},{3,0},{4,5},{5,6},{6,7},{7,4},{8,9},{9,10},{10,1... | collective-permute-start | bytes 1572872 | tf_op jit(solution)/shard_map/ppermute | solution.py:460
  31.6 110.5 %collective-permute-start.1 = (bf16[512,512]{1,0:T(8,128)(2,1)}, bf16[512,512]{1,0:T(8,128)(2,1)}, u32[]{:S(2)}, u32[]{:S(2)}) collective-permute-start(bf16[512,512]{1,0:T(8,128)(2,1)} %get-tuple-element.43), channel_id=1, source_target_pairs={{0,2},{1,3},{2,0},{3,1},{4,6},{5,7},{6,4},{7,5},{8,10},{9,11},{10,... | collective-permute-start | bytes 1572872 | tf_op jit(solution)/shard_map/ppermute | solution.py:460
  86.0 56.0 %collective-permute-start.2 = (bf16[512,512]{1,0:T(8,128)(2,1)}, bf16[512,512]{1,0:T(8,128)(2,1)S(1)}, u32[]{:S(2)}, u32[]{:S(2)}) collective-permute-start(bf16[512,512]{1,0:T(8,128)(2,1)} %get-tuple-element.44), channel_id=1, source_target_pairs={{0,3},{1,0},{2,1},{3,2},{4,7},{5,4},{6,5},{7,6},{8,11},{9,8},{10,9... | collective-permute-start | bytes 1572872 | tf_op jit(solution)/shard_map/ppermute | solution.py:460
  137.1 52.6 %collective-permute-start.9 = (bf16[512,512]{1,0:T(8,128)(2,1)S(1)}, bf16[512,512]{1,0:T(8,128)(2,1)S(1)}, u32[]{:S(2)}, u32[]{:S(2)}) collective-permute-start(bf16[512,512]{1,0:T(8,128)(2,1)S(1)} %get-tuple-element.54), channel_id=1, source_target_pairs={{0,1},{1,2},{2,3},{3,0},{4,5},{5,6},{6,7},{7,4},{8,9},{9,10},{10,1... | collective-permute-start | bytes 1572872 | tf_op jit(solution)/shard_map/ppermute | solution.py:460
  137.7 55.2 %collective-permute-start.10 = (bf16[512,512]{1,0:T(8,128)(2,1)S(1)}, bf16[512,512]{1,0:T(8,128)(2,1)S(1)}, u32[]{:S(2)}, u32[]{:S(2)}) collective-permute-start(bf16[512,512]{1,0:T(8,128)(2,1)S(1)} %get-tuple-element.55), channel_id=1, source_target_pairs={{0,2},{1,3},{2,0},{3,1},{4,6},{5,7},{6,4},{7,5},{8,10},{9,11},{10,... | collective-permute-start | bytes 1572872 | tf_op jit(solution)/shard_map/ppermute | solution.py:460
  139.2 53.8 %collective-permute-start.11 = (bf16[512,512]{1,0:T(8,128)(2,1)S(1)}, bf16[512,512]{1,0:T(8,128)(2,1)S(1)}, u32[]{:S(2)}, u32[]{:S(2)}) collective-permute-start(bf16[512,512]{1,0:T(8,128)(2,1)S(1)} %get-tuple-element.56), channel_id=1, source_target_pairs={{0,3},{1,0},{2,1},{3,2},{4,7},{5,4},{6,5},{7,6},{8,11},{9,8},{10,9... | collective-permute-start | bytes 1572872 | tf_op jit(solution)/shard_map/ppermute | solution.py:460
  188.7 35.6 %collective-permute-start.4 = (bf16[512,512]{1,0:T(8,128)(2,1)S(1)}, bf16[512,512]{1,0:T(8,128)(2,1)S(1)}, u32[]{:S(2)}, u32[]{:S(2)}) collective-permute-start(bf16[512,512]{1,0:T(8,128)(2,1)S(1)} %get-tuple-element.47), channel_id=1, source_target_pairs={{0,2},{1,3},{2,0},{3,1},{4,6},{5,7},{6,4},{7,5},{8,10},{9,11},{10,... | collective-permute-start | bytes 1572872 | tf_op jit(solution)/shard_map/ppermute | solution.py:460
  189.7 34.6 %collective-permute-start.5 = (bf16[512,512]{1,0:T(8,128)(2,1)S(1)}, bf16[512,512]{1,0:T(8,128)(2,1)S(1)}, u32[]{:S(2)}, u32[]{:S(2)}) collective-permute-start(bf16[512,512]{1,0:T(8,128)(2,1)S(1)} %get-tuple-element.48), channel_id=1, source_target_pairs={{0,3},{1,0},{2,1},{3,2},{4,7},{5,4},{6,5},{7,6},{8,11},{9,8},{10,9... | collective-permute-start | bytes 1572872 | tf_op jit(solution)/shard_map/ppermute | solution.py:460
  192.9 148.9 %collective-permute-start.54 = (bf16[1,4,512,1024]{3,2,1,0:T(8,128)(2,1)}, bf16[1,4,512,1024]{3,2,1,0:T(8,128)(2,1)}, u32[]{:S(2)}, u32[]{:S(2)}) collective-permute-start(bf16[1,4,512,1024]{3,2,1,0:T(8,128)(2,1)} %bitcast.108), channel_id=1, source_target_pairs={{0,4},{4,0},{8,12},{12,8},{16,20},{20,16},{24,28},{28,24},{1,5},{5... | collective-permute-start | bytes 12582920 | tf_op jit(solution)/shard_map/ppermute | solution.py:349
  193.0 163.1 %collective-permute-start.40 = (bf16[4,4,256,512]{3,2,1,0:T(8,128)(2,1)}, bf16[4,4,256,512]{3,2,1,0:T(8,128)(2,1)}, u32[]{:S(2)}, u32[]{:S(2)}) collective-permute-start(bf16[4,4,256,512]{3,2,1,0:T(8,128)(2,1)} %bitcast.82), channel_id=1, source_target_pairs={{0,4},{4,0},{8,12},{12,8},{16,20},{20,16},{24,28},{28,24},{1,5},{5... | collective-permute-start | bytes 12582920 | tf_op jit(solution)/shard_map/ppermute | solution.py:349
  236.9 115.1 %collective-permute-start.12 = (bf16[1,4,128,3072]{3,2,1,0:T(8,128)(2,1)S(1)}, bf16[1,4,128,3072]{3,2,1,0:T(8,128)(2,1)}, u32[]{:S(2)}, u32[]{:S(2)}) collective-permute-start(bf16[1,4,128,3072]{3,2,1,0:T(8,128)(2,1)S(1)} %dynamic-slice_bitcast_fusion), channel_id=1, source_target_pairs={{0,4},{4,0},{8,12},{12,8},{16,20},{20,16},{24,28},{28,24},{1,5},{5... | collective-permute-start | bytes 9437192 | tf_op jit(solution)/shard_map/ppermute | solution.py:349
  298.0 41.5 %collective-permute-start.39 = (bf16[1,128,1024]{2,1,0:T(8,128)(2,1)}, bf16[1,128,1024]{2,1,0:T(8,128)(2,1)}, u32[]{:S(2)}, u32[]{:S(2)}) collective-permute-start(bf16[1,128,1024]{2,1,0:T(8,128)(2,1)} %fusion.37), channel_id=1, source_target_pairs={{0,4},{4,0},{8,12},{12,8},{16,20},{20,16},{24,28},{28,24},{1,5},{5... | collective-permute-start | bytes 786440 | tf_op jit(solution)/shard_map/ppermute | solution.py:349
  348.0 66.5 %collective-permute-start.55 = (bf16[1,4,128,1024]{3,2,1,0:T(8,128)(2,1)S(1)}, bf16[1,4,128,1024]{3,2,1,0:T(8,128)(2,1)}, u32[]{:S(2)}, u32[]{:S(2)}) collective-permute-start(bf16[1,4,128,1024]{3,2,1,0:T(8,128)(2,1)S(1)} %dynamic-slice_bitcast_fusion.2), channel_id=1, source_target_pairs={{0,8},{4,12},{8,0},{12,4},{16,24},{20,28},{24,16},{28,20},{1,9},{5... | collective-permute-start | bytes 3145736 | tf_op jit(solution)/shard_map/ppermute | solution.py:349
  350.4 67.4 %collective-permute-start.61 = (bf16[1,4,128,1024]{3,2,1,0:T(8,128)(2,1)S(1)}, bf16[1,4,128,1024]{3,2,1,0:T(8,128)(2,1)S(1)}, u32[]{:S(2)}, u32[]{:S(2)}) collective-permute-start(bf16[1,4,128,1024]{3,2,1,0:T(8,128)(2,1)S(1)} %dynamic-slice_bitcast_fusion.1), channel_id=1, source_target_pairs={{0,16},{4,20},{8,24},{12,28},{16,0},{20,4},{24,8},{28,12},{1,17},{... | collective-permute-start | bytes 3145736 | tf_op jit(solution)/shard_map/ppermute | solution.py:349
  355.5 35.7 %collective-permute-start.13 = (bf16[1,4,32,3072]{3,2,1,0:T(8,128)(2,1)S(1)}, bf16[1,4,32,3072]{3,2,1,0:T(8,128)(2,1)S(1)}, u32[]{:S(2)}, u32[]{:S(2)}) collective-permute-start(bf16[1,4,32,3072]{3,2,1,0:T(8,128)(2,1)S(1)} %dynamic-slice_bitcast_fusion.7), channel_id=1, source_target_pairs={{0,8},{4,12},{8,0},{12,4},{16,24},{20,28},{24,16},{28,20},{1,9},{5... | collective-permute-start | bytes 2359304 | tf_op jit(solution)/shard_map/ppermute | solution.py:349
  361.3 57.3 %collective-permute-start.41 = (bf16[4,4,64,512]{3,2,1,0:T(8,128)(2,1)S(1)}, bf16[4,4,64,512]{3,2,1,0:T(8,128)(2,1)S(1)}, u32[]{:S(2)}, u32[]{:S(2)}) collective-permute-start(bf16[4,4,64,512]{3,2,1,0:T(8,128)(2,1)S(1)} %dynamic-slice_bitcast_fusion.4), channel_id=1, source_target_pairs={{0,8},{4,12},{8,0},{12,4},{16,24},{20,28},{24,16},{28,20},{1,9},{5... | collective-permute-start | bytes 3145736 | tf_op jit(solution)/shard_map/ppermute | solution.py:349
  362.0 58.8 %collective-permute-start.47 = (bf16[4,4,64,512]{3,2,1,0:T(8,128)(2,1)S(1)}, bf16[4,4,64,512]{3,2,1,0:T(8,128)(2,1)S(1)}, u32[]{:S(2)}, u32[]{:S(2)}) collective-permute-start(bf16[4,4,64,512]{3,2,1,0:T(8,128)(2,1)S(1)} %dynamic-slice_bitcast_fusion.3), channel_id=1, source_target_pairs={{0,16},{4,20},{8,24},{12,28},{16,0},{20,4},{24,8},{28,12},{1,17},{... | collective-permute-start | bytes 3145736 | tf_op jit(solution)/shard_map/ppermute | solution.py:349
  417.8 34.3 %collective-permute-start.56 = (bf16[1,4,64,1024]{3,2,1,0:T(8,128)(2,1)S(1)}, bf16[1,4,64,1024]{3,2,1,0:T(8,128)(2,1)S(1)}, u32[]{:S(2)}, u32[]{:S(2)}) collective-permute-start(bf16[1,4,64,1024]{3,2,1,0:T(8,128)(2,1)S(1)} %dynamic-slice_bitcast_fusion.9), channel_id=1, source_target_pairs={{0,16},{4,20},{8,24},{12,28},{16,0},{20,4},{24,8},{28,12},{1,17},{... | collective-permute-start | bytes 1572872 | tf_op jit(solution)/shard_map/ppermute | solution.py:349
  418.7 34.1 %collective-permute-start.62 = (bf16[1,4,64,1024]{3,2,1,0:T(8,128)(2,1)S(1)}, bf16[1,4,64,1024]{3,2,1,0:T(8,128)(2,1)S(1)}, u32[]{:S(2)}, u32[]{:S(2)}) collective-permute-start(bf16[1,4,64,1024]{3,2,1,0:T(8,128)(2,1)S(1)} %dynamic-slice_bitcast_fusion.8), channel_id=1, source_target_pairs={{0,8},{4,12},{8,0},{12,4},{16,24},{20,28},{24,16},{28,20},{1,9},{5... | collective-permute-start | bytes 1572872 | tf_op jit(solution)/shard_map/ppermute | solution.py:349
  420.8 32.3 %collective-permute-start.42 = (bf16[4,4,32,512]{3,2,1,0:T(8,128)(2,1)S(1)}, bf16[4,4,32,512]{3,2,1,0:T(8,128)(2,1)S(1)}, u32[]{:S(2)}, u32[]{:S(2)}) collective-permute-start(bf16[4,4,32,512]{3,2,1,0:T(8,128)(2,1)S(1)} %dynamic-slice_bitcast_fusion.11), channel_id=1, source_target_pairs={{0,16},{4,20},{8,24},{12,28},{16,0},{20,4},{24,8},{28,12},{1,17},{... | collective-permute-start | bytes 1572872 | tf_op jit(solution)/shard_map/ppermute | solution.py:349
  469.4 44.0 %collective-permute-start.25 = (bf16[1,128,3072]{2,1,0:T(8,128)(2,1)S(1)}, bf16[1,128,3072]{2,1,0:T(8,128)(2,1)S(1)}, u32[]{:S(2)}, u32[]{:S(2)}) collective-permute-start(bf16[1,128,3072]{2,1,0:T(8,128)(2,1)S(1)} %fusion.38), channel_id=1, source_target_pairs={{0,4},{4,0},{8,12},{12,8},{16,20},{20,16},{24,28},{28,24},{1,5},{5... | collective-permute-start | bytes 2359304 | tf_op jit(solution)/shard_map/ppermute | solution.py:349
  (66 other events, 696.6 us)

commit v2 on v1

--- a/solution.py
+++ b/solution.py
@@ -134,8 +134,8 @@
     )(owner, normed, cot, qkv_weight, qkv_weight, qkv_weight, out_weight, cosine, sine)
 
 
-QUERY_ROWS = 256
-KEY_ROWS = 256
+QUERY_ROWS = 512
+KEY_ROWS = 512
 
 
 def attention_kernel(pieces, info_ref, *refs):
@@ -165,9 +165,7 @@
         grads = [jnp.where(halves == head, grad_rows, zero) for head in range(2)]
         query_places = first + lax.broadcasted_iota(jnp.int32, (1, QUERY_ROWS), 1)
         lowest = jnp.where(query_places > end, end + 1, 0)
-        blocks = (number + 1) * (QUERY_ROWS // KEY_ROWS) if QUERY_ROWS >= KEY_ROWS else lax.div(
-            number * QUERY_ROWS, KEY_ROWS
-        ) + 1
+        blocks = (number + 1) * (QUERY_ROWS // KEY_ROWS)
 
         def scores_of(block, highest):
             start = pl.multiple_of(block * KEY_ROWS, KEY_ROWS)
@@ -269,11 +267,21 @@
     )(info, *parts, cosine, sine)
 
 
-def feed_kernel(
-    cells, normed_ref, turned_ref, cot_ref, in_ref, bias_ref, down_ref, in_grad, down_grad, bias_grad, out_sum, norm_sum
-):
+def feed_kernel(first, *refs):
+    normed_ref, turned_ref, cot_ref, in_ref, bias_ref, down_ref = refs[1:7]
+    in_grad, down_grad, bias_grad, out_sum, norm_sum = refs[-5:]
     step = pl.program_id(0)
     up = math.sqrt(2.0 / math.pi)
+
+    @pl.when(step == 0)
+    def _():
+        if first:
+            out_sum[...] = jnp.zeros_like(out_sum)
+            norm_sum[...] = jnp.zeros_like(norm_sum)
+        else:
+            out_sum[...] = refs[7][...]
+            norm_sum[...] = refs[8][...]
+
     weights = in_ref[...]
     downs = down_ref[...]
     cot = cot_ref[...]
@@ -283,65 +291,195 @@
     half = 0.5 * (1.0 + tanh)
     active = (pre * half).astype(BF16)
     slope = half + 0.5 * pre * (1.0 - tanh * tanh) * (up * (1.0 + 3 * 0.044715 * square))
-    pre_grad_full = (dot_nt(cot, downs) * slope).astype(BF16)
-    in_grad[0] = dot_nn(turned_ref[...], pre_grad_full).astype(BF16)
-    down_grad[0] = dot_tn(active, cot).astype(BF16)
-    bias_grad[0] = jnp.sum(pre_grad_full.astype(F32), axis=0, keepdims=True)
-    out_term = dot_nn(active, downs)
-    norm_term = dot_nt(pre_grad_full, weights)
-
-    @pl.when(step == 0)
-    def _():
-        out_sum[...] = out_term
-        norm_sum[...] = norm_term
-
-    @pl.when(step > 0)
-    def _():
-        out_sum[...] += out_term
-        norm_sum[...] += norm_term
-
-
-def feed_half(cells, normed, turned, cot, in_weight, in_bias, down_weight):
+    pre_grad = (dot_nt(cot, downs) * slope).astype(BF16)
+    pieces, owners, kept, tile = in_grad.shape
+    term = dot_nn(turned_ref[...], pre_grad).astype(BF16)
+    for owner in range(owners):
+        for piece in range(pieces):
+            start = (owner * pieces + piece) * kept
+            in_grad[piece, owner] = term[start : start + kept]
+    term = dot_tn(active, cot).astype(BF16)
+    kept = tile // pieces
+    for group in range(term.shape[1] // tile):
+        for piece in range(pieces):
+            down_grad[piece, 0, group * kept : (group + 1) * kept] = term[
+                piece * kept : (piece + 1) * kept, group * tile : (group + 1) * tile
+            ]
+    bias_grad[0] = jnp.sum(pre_grad.astype(F32), axis=0, keepdims=True)
+    out_sum[...] += dot_nn(active, downs)
+    norm_sum[...] += dot_nt(pre_grad, weights)
+
+
+def feed_half(cells, normed, turned, cot, in_weight, in_bias, down_weight, pieces, sums=()):
     rows, width = normed.shape
-    tiles = cells.shape[0]
+    owners = cells.shape[0]
     hidden_units = in_weight.shape[1]
-    tile = hidden_units // (2 * tiles)
+    tile = hidden_units // (2 * owners)
+    kept = width // owners // pieces
+    tall = owners * kept
+    wide = tile // pieces * (width // tile)
+    fixed = pl.BlockSpec((rows, width), lambda i, c: (0, 0))
     return pl.pallas_call(
-        feed_kernel,
+        lambda *refs: feed_kernel(not sums, *refs),
         grid_spec=pltpu.PrefetchScalarGridSpec(
             num_scalar_prefetch=1,
-            grid=(tiles,),
+            grid=(owners,),
             in_specs=[
-                pl.BlockSpec((rows, width), lambda i, c: (0, 0)),
+                fixed,
                 pl.BlockSpec((width, rows), lambda i, c: (0, 0)),
-                pl.BlockSpec((rows, width), lambda i, c: (0, 0)),
+                fixed,
                 pl.BlockSpec((width, tile), lambda i, c: (0, c[i])),
                 pl.BlockSpec((1, tile), lambda i, c: (0, c[i])),
                 pl.BlockSpec((tile, width), lambda i, c: (c[i], 0)),
-            ],
+            ]
+            + [fixed] * len(sums),
             out_specs=[
-                pl.BlockSpec((1, width, tile), lambda i, c: (i, 0, 0)),
-                pl.BlockSpec((1, tile, width), lambda i, c: (i, 0, 0)),
+                pl.BlockSpec((pieces, owners, kept, tile), lambda i, c: (0, 0, i, 0)),
+                pl.BlockSpec((pieces, 1, wide, tile), lambda i, c: (0, i, 0, 0)),
                 pl.BlockSpec((1, 1, tile), lambda i, c: (i, 0, 0)),
-                pl.BlockSpec((rows, width), lambda i, c: (0, 0)),
-                pl.BlockSpec((rows, width), lambda i, c: (0, 0)),
+                fixed,
+                fixed,
             ],
         ),
         out_shape=[
-            jax.ShapeDtypeStruct((tiles, width, tile), BF16),
-            jax.ShapeDtypeStruct((tiles, tile, width), BF16),
-            jax.ShapeDtypeStruct((tiles, 1, tile), F32),
+            jax.ShapeDtypeStruct((pieces, owners, tall, tile), BF16),
+            jax.ShapeDtypeStruct((pieces, owners, wide, tile), BF16),
+            jax.ShapeDtypeStruct((owners, 1, tile), F32),
             jax.ShapeDtypeStruct((rows, width), F32),
             jax.ShapeDtypeStruct((rows, width), F32),
         ],
-        compiler_params=pltpu.CompilerParams(vmem_limit_bytes=56 * MIB),
+        compiler_params=pltpu.CompilerParams(vmem_limit_bytes=60 * MIB),
         cost_estimate=pl.CostEstimate(
             flops=12 * rows * width * hidden_units // 2,
             bytes_accessed=8 * width * hidden_units // 2,
             transcendentals=rows * hidden_units // 2,
         ),
         name="feed",
-    )(cells, normed, turned, cot, in_weight, in_bias, down_weight)
+    )(cells, normed, turned, cot, in_weight, in_bias, down_weight, *sums)
+
+
+def place_columns(me_ref, piece_refs, held):
+    owners = len(piece_refs)
+    for shift in range(owners):
+        owner = lax.rem(me_ref[0] - shift + owners, owners)
+        start = pl.multiple_of(owner * PAIR, PAIR)
+        for part in range(4):
+            held[part, :, pl.ds(start, PAIR)] = piece_refs[shift][:, part * PAIR : (part + 1) * PAIR]
+
+
+def weight_kernel(pieces, me_ref, turned_ref, cot_ref, *refs):
+    owners = len(refs) - 2
+    grad_ref, held = refs[-2:]
+    place_columns(me_ref, refs[:owners], held)
+    kept = PAIR // pieces
+    turned = turned_ref[...]
+    for part in range(3):
+        term = dot_nn(turned, held[part]).astype(BF16)
+        for owner in range(owners):
+            for core in range(2):
+                for piece in range(pieces):
+                    start = ((owner * 2 + core) * pieces + piece) * kept
+                    grad_ref[core, piece, owner, part * kept : (part + 1) * kept] = term[start : start + kept]
+    term = dot_tn(held[3], cot_ref[...]).astype(BF16)
+    half = term.shape[1] // 2
+    for owner in range(owners):
+        for core in range(2):
+            for piece in range(pieces):
+                start = (owner * pieces + piece) * kept
+                grad_ref[core, piece, owner, 3 * kept :] = term[
+                    start : start + kept, core * half : (core + 1) * half
+                ]
+
+
+def weight_grads(me, turned, cot, parts, pieces):
+    owners = len(parts)
+    rows, width = cot.shape
+    kept = PAIR // pieces
+    whole = pl.BlockSpec(memory_space=pltpu.VMEM)
+    return pl.pallas_call(
+        lambda *refs: weight_kernel(pieces, *refs),
+        in_specs=[pl.BlockSpec(memory_space=pltpu.SMEM)] + [whole] * (2 + owners),
+        out_specs=whole,
+        out_shape=jax.ShapeDtypeStruct((2, pieces, owners, 4 * kept, owners * PAIR), BF16),
+        scratch_shapes=[pltpu.VMEM((4, rows, owners * PAIR), BF16)],
+        compiler_params=pltpu.CompilerParams(vmem_limit_bytes=40 * MIB),
+        cost_estimate=pl.CostEstimate(
+            flops=8 * rows * width * owners * PAIR, bytes_accessed=12 * MIB, transcendentals=0
+        ),
+        name="weight_grads",
+    )(me[None], turned, cot, *parts)
+
+
+def sums_kernel(last, owners, me_ref, *refs):
+    piece_refs, refs = refs[:owners], refs[owners:]
+    weight_refs, refs = refs[: 3 * owners], refs[3 * owners :]
+    out_weight_refs, refs = refs[:owners], refs[owners:]
+    out_in, norm_in = refs[:2]
+    held = refs[-1]
+    place_columns(me_ref, piece_refs, held)
+    norm = norm_in[...]
+    for part in range(3):
+        weights = jnp.concatenate([ref[...] for ref in weight_refs[part * owners : (part + 1) * owners]], axis=1)
+        norm = norm + dot_nt(held[part], weights)
+    weights = jnp.concatenate([ref[...] for ref in out_weight_refs], axis=0)
+    out = out_in[...] + dot_nn(held[3], weights)
+    if not last:
+        out_ref, norm_ref = refs[2:4]
+        out_ref[...] = out
+        norm_ref[...] = norm
+        return
+    stream_ref, cot_ref, gain_ref, down_bias_ref, out_ref, hidden_ref, gain_grad, bias_grad, cot_sum = refs[2:-1]
+    stream = stream_ref[...]
+    cot = cot_ref[...].astype(F32)
+    out_ref[...] = (stream + out + down_bias_ref[...]).astype(BF16)
+    centre = stream - jnp.mean(stream, axis=-1, keepdims=True)
+    spread = jnp.mean(centre * centre, axis=-1, keepdims=True)
+    inverse = lax.rsqrt(spread + EPSILON)
+    hat = centre * inverse
+    gained = norm * gain_ref[...]
+    hidden_ref[...] = cot + inverse * (
+        gained
+        - jnp.mean(gained, axis=-1, keepdims=True)
+        - hat * jnp.mean(gained * hat, axis=-1, keepdims=True)
+    )
+    gain_grad[...] = jnp.sum(norm * hat, axis=0, keepdims=True)
+    bias_grad[...] = jnp.sum(norm, axis=0, keepdims=True)
+    cot_sum[...] = jnp.sum(cot, axis=0, keepdims=True)
+
+
+def sums_of(me, chunk, chunks, parts, qkv_weight, out_weight, sums, final=()):
+    owners = len(parts)
+    rows = parts[0].shape[0]
+    width = qkv_weight.shape[0]
+    whole = pl.BlockSpec(memory_space=pltpu.VMEM)
+    last = bool(final)
+
+    def columns(part, owner):
+        at = (part * owners + owner) * chunks + chunk
+        return pl.BlockSpec((width, PAIR), lambda i: (0, at))
+
+    def weight_rows(owner):
+        return pl.BlockSpec((PAIR, width), lambda i: (owner * chunks + chunk, 0))
+
+    full = jax.ShapeDtypeStruct((rows, width), F32)
+    row = jax.ShapeDtypeStruct((1, width), F32)
+    return pl.pallas_call(
+        lambda *refs: sums_kernel(last, owners, *refs),
+        grid=(1,),
+        in_specs=[pl.BlockSpec(memory_space=pltpu.SMEM)]
+        + [whole] * owners
+        + [columns(part, owner) for part in range(3) for owner in range(owners)]
+        + [weight_rows(owner) for owner in range(owners)]
+        + [whole] * (2 + len(final)),
+        out_specs=[whole] * (5 if last else 2),
+        out_shape=[jax.ShapeDtypeStruct((rows, width), BF16), full, row, row, row] if last else [full, full],
+        scratch_shapes=[pltpu.VMEM((4, rows, owners * PAIR), BF16)],
+        compiler_params=pltpu.CompilerParams(vmem_limit_bytes=56 * MIB),
+        cost_estimate=pl.CostEstimate(
+            flops=8 * rows * width * owners * PAIR, bytes_accessed=16 * MIB, transcendentals=0
+        ),
+        name="sums",
+    )(me[None], *parts, *([qkv_weight] * (3 * owners)), *([out_weight] * owners), *sums, *final)
 
 
 def exchange(rows, axis, mask):
@@ -349,64 +487,116 @@
     return lax.ppermute(rows, axis, [(place, place ^ mask) for place in range(size)])
 
 
-def halves_of(rows, dim, bit):
-    shape = rows.shape[:dim] + (2, rows.shape[dim] // 2) + rows.shape[dim + 1 :]
-    split = rows.reshape(shape)
-    return (
-        lax.dynamic_index_in_dim(split, 1 - bit, dim, keepdims=False),
-        lax.dynamic_index_in_dim(split, bit, dim, keepdims=False),
-    )
-
-
 def added(left, right):
     return (left.astype(F32) + right.astype(F32)).astype(BF16)
 
 
-def joined(mine, other, dim, bit):
+def joined(mine, other, bit):
     low = jnp.where(bit == 0, mine, other)
     high = jnp.where(bit == 0, other, mine)
-    return jnp.concatenate([low, high], axis=dim)
+    return jnp.stack([low, high])
 
 
 def bits_of(axis):
     return lax.axis_size(axis).bit_length() - 1
 
 
-def reduce_over(rows, order):
-    place = lax.axis_index("batch")
-    for bit_number in order:
-        bit = (place >> bit_number) & 1
-        sent, kept = halves_of(rows, 2, bit)
-        rows = added(kept, exchange(sent, "batch", 1 << bit_number))
-    place = lax.axis_index("seq")
-    for bit_number in range(bits_of("seq")):
-        bit = (place >> bit_number) & 1
-        shape = rows.shape
-        split = rows.reshape((shape[0], shape[1] // 2, 2) + shape[2:])
-        sent = lax.dynamic_index_in_dim(split, 1 - bit, 2, keepdims=False)
-        kept = lax.dynamic_index_in_dim(split, bit, 2, keepdims=False)
-        rows = added(kept, exchange(sent, "seq", 1 << bit_number))
+def picked(rows, index):
+    return lax.dynamic_index_in_dim(rows, index, 0, keepdims=False)
+
+
+class DeviceSum:
+    def __init__(self):
+        place = lax.axis_index("batch")
+        self.bits = [(place >> number) & 1 for number in range(bits_of("batch"))]
+        place = lax.axis_index("seq")
+        self.seq_bits = [(place >> number) & 1 for number in range(bits_of("seq"))]
+        order = list(range(1, len(self.bits)))
+        self.orders = (order, order[::-1])
+
+    def send_core(self, arrays):
+        self.arrived = [exchange(array, "batch", 1) for array in arrays]
+
+    def take_core(self, kept):
+        self.ends = []
+        depth = len(self.orders[0])
+        for half, order in enumerate(self.orders):
+            bit = self.bits[order[0]]
+
+            def side(index):
+                terms = []
+                for mine, other in zip(kept, self.arrived):
+                    shape = (2, 2, mine.shape[0] // 4) + mine.shape[1:]
+                    terms.append(
+                        added(picked(mine.reshape(shape)[half], index), picked(other.reshape(shape)[half], index))
+                    )
+                return terms[0] if len(terms) == 1 else jnp.concatenate(terms, axis=2)
+
+            self.ends.append((side(1 - bit), side(bit)))
+        self.level = 0
+        return self
+
+    def send(self):
+        self.arrived = [
+            exchange(end[0], "batch", 1 << order[self.level]) for end, order in zip(self.ends, self.orders)
+        ]
+
+    def take(self):
+        ends = []
+        self.level += 1
+        for (_, kept), arrived, order in zip(self.ends, self.arrived, self.orders):
+            total = added(kept, arrived)
+            if self.level < len(order):
+                shape = (2, total.shape[0] // 2) + total.shape[1:]
+                bit = self.bits[order[self.level]]
+                ends.append((picked(total.reshape(shape), 1 - bit), picked(total.reshape(shape), bit)))
+            else:
+                ends.append(total[0])
+        self.ends = ends
+        if self.level == len(self.orders[0]):
+            self.split_seq(jnp.concatenate(ends, axis=1), 0)
+
+    def split_seq(self, rows, number):
+        self.level = number
+        split = rows.reshape((rows.shape[0] // 2, 2) + rows.shape[1:])
+        bit = self.seq_bits[number]
+        self.ends = tuple(
+            lax.dynamic_index_in_dim(split, index, 1, keepdims=False) for index in (1 - bit, bit)
+        )
+
+    def send_seq(self):
+        self.arrived = exchange(self.ends[0], "seq", 1 << self.level)
+
+    def take_seq(self):
+        total = added(self.ends[1], self.arrived)
+        if self.level + 1 < len(self.seq_bits):
+            self.split_seq(total, self.level + 1)
+        else:
+            rows = total[0]
+            middle = rows.shape[0] // 2
+            self.ends = [rows[:middle], rows[middle:]]
+
+    def gather(self, level):
+        ends = []
+        for rows, order in zip(self.ends, self.orders):
+            number = order[len(order) - 1 - level]
+            ends.append(joined(rows, exchange(rows, "batch", 1 << number), self.bits[number]))
+        self.ends = ends
+
+    def gather_core(self):
+        mine = jnp.stack(self.ends)
+        return joined(mine, exchange(mine, "batch", 1), self.bits[0])
+
+
+def all_sum(rows):
+    for axis in ("batch", "seq"):
+        for number in range(bits_of(axis)):
+            rows = rows + exchange(rows, axis, 1 << number)
     return rows
 
 
-def gather_over(rows, order):
-    place = lax.axis_index("batch")
-    for bit_number in reversed(order):
-        bit = (place >> bit_number) & 1
-        rows = joined(rows, exchange(rows, "batch", 1 << bit_number), 2, bit)
-    return rows
-
-
-def sum_over_devices(sent, kept):
-    rows = added(kept, exchange(sent, "batch", 1))
-    order = list(range(1, bits_of("batch")))
-    middle = rows.shape[2] // 2
-    ends = []
-    for part, bits in ((rows[:, :, :middle], order), (rows[:, :, middle:], order[::-1])):
-        ends.append(gather_over(reduce_over(part, bits), bits))
-    mine = jnp.concatenate(ends, axis=2)[:, 0]
-    other = exchange(mine, "batch", 1)
-    return joined(mine[None], other[None], 0, lax.axis_index("batch") & 1)
+def tied(*groups):
+    return lax.optimization_barrier(groups)
 
 
 def fast_body(
@@ -428,10 +618,12 @@
     width = hidden.shape[2]
     rows = hidden.shape[1]
     owners = lax.axis_size("seq")
+    pieces = lax.axis_size("batch")
     me = lax.axis_index("seq")
     core = lax.axis_index("batch") & 1
     length = rows * owners
-    chunks = width // owners // PAIR
+    own_rows = width // owners
+    chunks = own_rows // PAIR
     end = end_places[0]
 
     places = me * rows + jnp.arange(rows, dtype=jnp.int32)[:, None]
@@ -448,104 +640,106 @@
     own_sine = lax.dynamic_slice_in_dim(sine, me * rows, rows)
 
     parts = [[None] * owners for _ in range(chunks)]
-    for shift in list(range(1, owners)) + [0]:
+    far_first = sorted(range(1, owners), key=lambda shift: abs(2 * shift - owners)) + [0]
+    for shift in far_first:
         owner = lax.rem(me + shift, owners)
         blocks = heads_of(owner[None], normed, cot, qkv_weight, out_weight, own_cosine, own_sine, owners)
         for chunk in range(chunks):
             parts[chunk][shift] = blocks[chunk]
 
-    def shifted(block, shift):
-        if shift == 0:
-            return block
-        return lax.ppermute(block, "seq", [(place, (place + shift) % owners) for place in range(owners)])
-
-    heads = [[shifted(parts[chunk][shift], shift) for shift in range(owners)] for chunk in range(chunks)]
+    def shifted(blocks):
+        around = [blocks[0]]
+        for shift in range(1, owners):
+            around.append(
+                lax.ppermute(blocks[shift], "seq", [(place, (place + shift) % owners) for place in range(owners)])
+            )
+        return around
+
+    heads = [shifted(parts[0])]
+    for chunk in range(1, chunks):
+        parts[chunk], _ = tied(parts[chunk], parts[0])
+        heads.append(shifted(parts[chunk]))
 
     cells = 2 * jnp.arange(owners, dtype=jnp.int32)
-    feed = [
-        feed_half(cells + half, normed, turned, cot, in_weight, in_bias[None], down_weight)
-        for half in (1 - core, core)
-    ]
-    tile = in_weight.shape[1] // (2 * owners)
-
-    def in_view(grad):
-        return grad.reshape(owners, owners, width // owners, tile)
-
-    def down_view(grad):
-        return grad.reshape(1, owners, tile, width)
-
-    in_sum = sum_over_devices(in_view(feed[0][0]), in_view(feed[1][0]))
-    down_sum = sum_over_devices(down_view(feed[0][1]), down_view(feed[1][1]))
-    in_weight_grad = jnp.transpose(in_sum, (2, 1, 0, 3)).reshape(width // owners, in_weight.shape[1]).astype(F32)
-    down_weight_grad = down_sum.reshape(2 * tile, width).astype(F32)
-    bias_low = jnp.where(core == 0, feed[1][2], feed[0][2])
-    bias_high = jnp.where(core == 0, feed[0][2], feed[1][2])
-    in_bias_grad = jnp.concatenate([bias_low, bias_high], axis=1).reshape(-1)
+    feed_args = (normed, turned, cot, in_weight, in_bias[None], down_weight, pieces)
+    away = feed_half(cells + 1 - core, *feed_args)
+    here = feed_half(cells + core, *feed_args, sums=tuple(away[3:]))
+    bias_low = jnp.where(core == 0, here[2], away[2])
+    bias_high = jnp.where(core == 0, away[2], here[2])
+    in_bias_grad = jnp.concatenate([bias_low, bias_high], axis=1)
+    feed_sum = DeviceSum()
+    feed_sum.send_core(away[:2])
+    feed_sum.take_core(here[:2])
+    out_total, norm_total = here[3:]
 
     info = jnp.stack([me, end]).astype(jnp.int32)
     back = []
     for chunk in range(chunks):
+        heads[chunk], feed_sum.ends = tied(heads[chunk], feed_sum.ends)
+        feed_sum.send()
         results = attention(info, heads[chunk], cosine, sine)
-        back.append([shifted(results[shift], shift) for shift in range(owners)])
-
-    ordered = []
-    for owner in range(owners):
-        ordered.append([])
-        for chunk in range(chunks):
-            stacked = jnp.stack(back[chunk])
-            slot = lax.rem(me - owner + owners, owners)
-            ordered[owner].append(lax.dynamic_index_in_dim(stacked, slot, 0, keepdims=False))
-
-    def columns(part):
-        return [
-            block[:, part * PAIR : (part + 1) * PAIR] for blocks in ordered for block in blocks
-        ]
-
-    joined_grad = jnp.concatenate(columns(0) + columns(1) + columns(2), axis=1)
-    mixed = jnp.concatenate(columns(3), axis=1)
-
-    qkv_weight_grad = dot_nn(turned, joined_grad).astype(BF16)
-    out_weight_grad = dot_tn(mixed, cot).astype(BF16)
-    normed_grad = dot_nt(joined_grad, qkv_weight) + feed[0][4] + feed[1][4]
-
-    def core_halves(grad):
-        split = grad.reshape(1, owners, 2, grad.shape[0] // (2 * owners), grad.shape[1])
-        return (
-            lax.dynamic_index_in_dim(split, 1 - core, 2, keepdims=False),
-            lax.dynamic_index_in_dim(split, core, 2, keepdims=False),
-        )
-
-    qkv_sum = sum_over_devices(*core_halves(qkv_weight_grad))
-    out_sum = sum_over_devices(*core_halves(out_weight_grad))
-    qkv_weight_grad = qkv_sum.reshape(width // owners, -1).astype(F32)
-    out_weight_grad = out_sum.reshape(width // owners, -1).astype(F32)
-
-    output = stream + dot_nn(mixed, out_weight) + feed[0][3] + feed[1][3] + down_bias[None]
-    centre = stream - jnp.mean(stream, axis=-1, keepdims=True)
-    spread = jnp.mean(centre * centre, axis=-1, keepdims=True)
-    inverse = lax.rsqrt(spread + EPSILON)
-    hat = centre * inverse
-    gained = normed_grad * norm_gain[None]
-    stream_part = inverse * (
-        gained
-        - jnp.mean(gained, axis=-1, keepdims=True)
-        - hat * jnp.mean(gained * hat, axis=-1, keepdims=True)
-    )
-    hidden_grad = cot.astype(F32) + stream_part
+        back.append(shifted(results))
+        results, feed_sum.arrived = tied(results, feed_sum.arrived)
+        feed_sum.take()
+
+    grads = []
+    for chunk in range(chunks):
+        last = chunk == chunks - 1
+        back[chunk], feed_sum.ends = tied(back[chunk], feed_sum.ends)
+        feed_sum.send_seq()
+        grad = weight_grads(me, turned, cot, back[chunk], pieces)
+        grads.append(DeviceSum())
+        grads[chunk].send_core([picked(grad, 1 - core)])
+        final = (stream, cot, norm_gain[None], down_bias[None]) if last else ()
+        totals = sums_of(me, chunk, chunks, back[chunk], qkv_weight, out_weight, (out_total, norm_total), final)
+        if not last:
+            out_total, norm_total = totals
+        grads[chunk].take_core([picked(grad, core)])
+        grads[chunk].send()
+        feed_sum.take_seq()
+    output, hidden_grad, gain_grad, bias_grad, cot_sum = totals
+
+    for grad in grads:
+        for level in range(1, len(grad.orders[0])):
+            grad.take()
+            grad.send()
+        grad.take()
+        for _ in grad.seq_bits:
+            grad.send_seq()
+            grad.take_seq()
     small = jnp.concatenate(
         [
             in_bias_grad.reshape(owners, -1),
-            jnp.sum(cot.astype(F32), axis=0).reshape(owners, -1),
-            jnp.sum(normed_grad * hat, axis=0).reshape(owners, -1),
-            jnp.sum(normed_grad, axis=0).reshape(owners, -1),
+            cot_sum.reshape(owners, -1),
+            gain_grad.reshape(owners, -1),
+            bias_grad.reshape(owners, -1),
         ],
         axis=1,
     )
-    small = lax.dynamic_index_in_dim(lax.psum(small, ("batch", "seq")), me, 0, keepdims=False)
-    few = width // owners
+    small = picked(all_sum(small), me)
+    for total in [feed_sum] + grads:
+        for level in range(len(total.orders[0])):
+            total.gather(level)
+
+    tile = in_weight.shape[1] // (2 * owners)
+    total = feed_sum.gather_core()
+    total = total.reshape((2, pieces) + total.shape[-2:])
+    tall = owners * (own_rows // pieces)
+    in_weight_grad = total[:, :, :tall].reshape(2, pieces, owners, own_rows // pieces, tile)
+    in_weight_grad = jnp.transpose(in_weight_grad, (1, 3, 2, 0, 4)).reshape(own_rows, -1).astype(F32)
+    down_weight_grad = total[:, :, tall:].reshape(2, pieces, width // tile, tile // pieces, tile)
+    down_weight_grad = jnp.transpose(down_weight_grad, (0, 1, 3, 2, 4)).reshape(2 * tile, width).astype(F32)
+    kept = PAIR // pieces
+    totals = jnp.stack([grad.gather_core() for grad in grads])
+    totals = totals.reshape((chunks, 2, pieces, 4, kept) + totals.shape[-1:])
+    qkv_weight_grad = totals[:, :, :, :3].reshape(chunks, 2, pieces, 3, kept, owners, PAIR)
+    qkv_weight_grad = jnp.transpose(qkv_weight_grad, (1, 2, 4, 3, 5, 0, 6)).reshape(own_rows, -1).astype(F32)
+    out_weight_grad = jnp.transpose(totals[:, :, :, 3], (0, 2, 3, 1, 4)).reshape(own_rows, width).astype(F32)
+
+    few = own_rows
     many = in_bias.shape[0] // owners
     return (
-        output.astype(BF16)[None],
+        output[None],
         hidden_grad[None],
         small[many + few : many + 2 * few],
         small[many + 2 * few :],
@@ -878,7 +1072,8 @@
         hidden = arrays[0]
         owners = mesh.shape["seq"]
         wide = hidden.shape[2] // owners
-        if hidden.shape[0] == 1 and wide % PAIR == 0:
+        pieces = mesh.shape["batch"]
+        if hidden.shape[0] == 1 and wide % PAIR == 0 and wide // 2 >= 16 * pieces and pieces >= 4:
             return fast_body(*arrays)
         return plain_body(*arrays)
 

time: 538 us -> 451 us (0.84)
  blocking collectives: 40.2 us -> 0 us
  local copies, waits for them, and re-layouts: 28.3 us -> 59.7 us
  waiting for transfers between devices: 152 us -> 124 us
  matrix products: 16.1 us -> 0 us
  other arithmetic: 41.2 us -> 28.3 us
  starting transfers between devices: 89.9 us -> 77.4 us
  Pallas kernels: 162 us -> 150 us
    psum x1 -> x0, blocking collectives: 40.2 us -> none  [fast_body(): lax.psum(small, ('batch', 'seq'))]
    pallas_call x2, Pallas kernels: 93.1 us -> 58.5 us  [attention(): pl.pallas_call(lambda *refs: attention_kernel(pieces, *refs), in_specs=[p...]
    ppermute x12, waiting for transfers between devices: 30.6 us -> 5.82 us  [shifted(): lax.ppermute(blocks[shift], 'seq', [(place, (place + shift) % owners) for...]
    pallas_call x2 -> x6, Pallas kernels: 45.7 us -> 68.1 us  [the longest x2 44.8 us: feed_half(): pl.pallas_call(lambda *refs: feed_kernel(not sums, *refs), grid_spec=pltp...]
    convert_element_type x1 -> x7, local copies, waits for them, and re-layouts: 5.25 us -> 26.9 us  [the longest x2 11.9 us: fast_body(): jnp.transpose(in_weight_grad, (1, 3, 2, 0, 4)).reshape(own_rows, -1)]
    dot_general x4 -> x0, matrix products: 16.1 us -> none  [the longest x2 7.62 us: dot_nn(): lax.dot_general(left, right, (((1,), (0,)), ((), ())), preferred_element_...]
    ppermute x56 -> x42, starting transfers between devices: 69.4 us -> 58.2 us  [exchange(): lax.ppermute(rows, axis, [(place, place ^ mask) for place in range(size)])]
    convert_element_type x36 -> x26, other arithmetic: 20.8 us -> 11.7 us  [added(): return (left.astype(F32) + right.astype(F32)).astype(BF16)]
  transfers between devices with their start and end apart: 68 -> 54, of which waited for: 30 -> 30; matrix products, arithmetic and copies ran while one was open for 12% -> 14% of each run, Pallas kernels for 29% -> 28%
where the time goes in v2:
time: 451 us; the launch traced here: 443 us
  Pallas kernels  150 us (33%)
  waiting for transfers between devices  124 us (27%)
  starting transfers between devices  77.4 us (17%)
  local copies, waits for them, and re-layouts  59.7 us (13%)
  other arithmetic  28.3 us (6%)
    ppermute x42, waiting for transfers between devices, exchange(): lax.ppermute(rows, axis, [(place, place ^ mask) for place in range(size)])  119 us
    pallas_call x2, Pallas kernels, attention(): pl.pallas_call(lambda *refs: attention_kernel(pieces, *refs), in_specs=[p...  58.5 us
    ppermute x42, starting transfers between devices, exchange(): lax.ppermute(rows, axis, [(place, place ^ mask) for place in range(size)])  58.2 us
    pallas_call x2, Pallas kernels, feed_half(): pl.pallas_call(lambda *refs: feed_kernel(not sums, *refs), grid_spec=pltp...  44.8 us
    ppermute x12, starting transfers between devices, shifted(): lax.ppermute(blocks[shift], 'seq', [(place, (place + shift) % owners) for...  19.1 us
    pallas_call x4, Pallas kernels, heads_of(): pl.pallas_call(heads_kernel, grid_spec=pltpu.PrefetchScalarGridSpec(num_s...  18.4 us
    pallas_call x2, Pallas kernels, sums_of(): pl.pallas_call(lambda *refs: sums_kernel(last, owners, *refs), grid=(1,),...  18.2 us
    unnamed x74, local copies, waits for them, and re-layouts  15.5 us
  transfers between devices with their start and end apart: 54, of which 30 were waited for; matrix products, arithmetic and copies ran while one was open for 14% of the time, Pallas kernels for 28%

profile of v2, /device:TPU:0, one launch (start us, length us, event | category | flops | bytes accessed | tf_op | source)
XLA Modules:
  0.0 442.9 jit_solution(10982273717166677400)
XLA Ops:
  4.1 4.6 %prep.1 = (f32[512,1024]{1,0:T(8,128)}, bf16[512,1024]{1,0:T(8,128)(2,1)}, bf16[1024,512]{1,0:T(8,128)(2,1)}) custom-call(bf16[512,1024]{1,0:T(8,128)(2,1)} %bitcast.302, s32[512,1]{1,0:T(8,128)} %select_select_fusion.mark_ref, bf16[32,1024]{1,0:T(8,128)(2,1)} %table_ref.1, f32[1,1024]{1,0:T(1,128)} %bitcast.305, f32[1,1024]{1,0:T(1,128)} %bitcast.307), custom_call_target="tpu_custom_call" | custom-call | tf_op jit(solution)/shard_map/prep/pallas_call | solution.py:67
  8.7 21.8 %feed.2 = (bf16[8,4,128,512]{3,2,1,0:T(8,128)(2,1)}, bf16[8,4,128,512]{3,2,1,0:T(8,128)(2,1)}, f32[4,1,512]{2,1,0:T(1,128)}, f32[512,1024]{1,0:T(8,128)}, f32[512,1024]{1,0:T(8,128)}) custom-call(s32[4]{0:T(128)} %get-tuple-element.237.refs_0_, bf16[512,1024]{1,0:T(8,128)(2,1)} %get-tuple-element.82.normed_ref.refs_1_, ...), custom_call_target="tpu_custom_call" | custom-call | flops 12884901888 | bytes 16777216 | tf_op jit(solution)/shard_map/feed/pallas_call | solution.py:322
  32.0 4.6 %heads.5 = (bf16[512,512]{1,0:T(8,128)(2,1)}, bf16[512,512]{1,0:T(8,128)(2,1)}) custom-call(s32[1]{0:T(128)} %bitcast.9.place_ref, bf16[512,1024]{1,0:T(8,128)(2,1)} %get-tuple-element.82.normed_ref.refs_1_, bf16[512,1024]{1,0:T(8,128)(2,1)} %bitcast.244, bf16[1024,3072]{1,0:T(8,128)(2,1)} %refs_16_.3, bf16[1024,3072]{1,0:T(8,128)(2,1)} %refs_16_.3, ...), custom_call_target="tpu_custom_call" | custom-call | tf_op jit(solution)/shard_map/heads/pallas_call | solution.py:115
  39.6 4.6 %heads.6 = (bf16[512,512]{1,0:T(8,128)(2,1)}, bf16[512,512]{1,0:T(8,128)(2,1)}) custom-call(s32[1]{0:T(128)} %bitcast.10.place_ref, bf16[512,1024]{1,0:T(8,128)(2,1)} %get-tuple-element.82.normed_ref.refs_1_, bf16[512,1024]{1,0:T(8,128)(2,1)} %bitcast.245, bf16[1024,3072]{1,0:T(8,128)(2,1)} %refs_16_.3, bf16[1024,3072]{1,0:T(8,128)(2,1)} %refs_16_.3, ...), custom_call_target="tpu_custom_call" | custom-call | tf_op jit(solution)/shard_map/heads/pallas_call | solution.py:115
  46.8 4.6 %heads.7 = (bf16[512,512]{1,0:T(8,128)(2,1)}, bf16[512,512]{1,0:T(8,128)(2,1)}) custom-call(s32[1]{0:T(128)} %bitcast.11.place_ref, bf16[512,1024]{1,0:T(8,128)(2,1)} %get-tuple-element.82.normed_ref.refs_1_, bf16[512,1024]{1,0:T(8,128)(2,1)} %bitcast.246, bf16[1024,3072]{1,0:T(8,128)(2,1)} %refs_16_.3, bf16[1024,3072]{1,0:T(8,128)(2,1)} %refs_16_.3, ...), custom_call_target="tpu_custom_call" | custom-call | tf_op jit(solution)/shard_map/heads/pallas_call | solution.py:115
  52.9 4.5 %heads.4 = (bf16[512,512]{1,0:T(8,128)(2,1)}, bf16[512,512]{1,0:T(8,128)(2,1)}) custom-call(s32[1]{0:T(128)} %bitcast.1.place_ref, bf16[512,1024]{1,0:T(8,128)(2,1)} %get-tuple-element.82.normed_ref.refs_1_, bf16[512,1024]{1,0:T(8,128)(2,1)} %bitcast.247, bf16[1024,3072]{1,0:T(8,128)(2,1)} %refs_16_.3, bf16[1024,3072]{1,0:T(8,128)(2,1)} %refs_16_.3, ...), custom_call_target="tpu_custom_call" | custom-call | tf_op jit(solution)/shard_map/heads/pallas_call | solution.py:115
  57.5 23.0 %feed.3 = (bf16[8,4,128,512]{3,2,1,0:T(8,128)(2,1)}, bf16[8,4,128,512]{3,2,1,0:T(8,128)(2,1)}, f32[4,1,512]{2,1,0:T(1,128)}, f32[512,1024]{1,0:T(8,128)}, f32[512,1024]{1,0:T(8,128)}) custom-call(s32[4]{0:T(128)} %get-tuple-element.238.refs_0_, bf16[512,1024]{1,0:T(8,128)(2,1)} %get-tuple-element.82.normed_ref.refs_1_, ...), custom_call_target="tpu_custom_call" | custom-call | flops 12884901888 | bytes 16777216 | tf_op jit(solution)/shard_map/feed/pallas_call | solution.py:322
  108.4 29.2 %attention.2 = (bf16[512,512]{1,0:T(8,128)(2,1)S(1)}, bf16[512,512]{1,0:T(8,128)(2,1)S(1)}, bf16[512,512]{1,0:T(8,128)(2,1)S(1)}, bf16[512,512]{1,0:T(8,128)(2,1)S(1)}) custom-call(s32[2]{0:T(128)S(1)} %pad_add_fusion.refs_0_, bf16[512,512]{1,0:T(8,128)(2,1)S(1)} %copy-done.23, bf16[512,512]{1,0:T(8,128)(2,1)S(1)} %collective-permute-done.3.refs_2_, ...), custom_call_target="tpu_custom_call" | custom-call | flops 16106127360 | bytes 8388608 | tf_op jit(solution)/shard_map/attention/pallas_call | solution.py:248
  137.6 8.5 %collective-permute-done.8 = bf16[2,4,256,512]{3,2,1,0:T(8,128)(2,1)} collective-permute-done((bf16[2,4,256,512]{3,2,1,0:T(8,128)(2,1)}, bf16[2,4,256,512]{3,2,1,0:T(8,128)(2,1)}, u32[]{:S(2)}, u32[]{:S(2)}) %collective-permute-start.8) | collective-permute-done | bytes 2097184 | tf_op jit(solution)/shard_map/ppermute | solution.py:487
  159.3 29.4 %attention.3 = (bf16[512,512]{1,0:T(8,128)(2,1)S(1)}, bf16[512,512]{1,0:T(8,128)(2,1)S(1)}, bf16[512,512]{1,0:T(8,128)(2,1)S(1)}, bf16[512,512]{1,0:T(8,128)(2,1)S(1)}) custom-call(s32[2]{0:T(128)S(1)} %pad_add_fusion.refs_0_, bf16[512,512]{1,0:T(8,128)(2,1)S(1)} %copy-done.20, bf16[512,512]{1,0:T(8,128)(2,1)} %collective-permute-done.refs_2_, ...), custom_call_target="tpu_custom_call" | custom-call | flops 16106127360 | bytes 8388608 | tf_op jit(solution)/shard_map/attention/pallas_call | solution.py:248
  193.2 13.1 %collective-permute-start.18 = (bf16[2,512,512]{2,1,0:T(8,128)(2,1)}, bf16[2,512,512]{2,1,0:T(8,128)(2,1)}, u32[]{:S(2)}, u32[]{:S(2)}) collective-permute-start(bf16[2,512,512]{2,1,0:T(8,128)(2,1)} %get-tuple-element.131), channel_id=1, source_target_pairs={{0,1},{1,0},{2,3},{3,2},{4,5},{5,4},{6,7},{7,6},{8,9},{9,8},{10,11... | collective-permute-start | bytes 3145736 | tf_op jit(solution)/shard_map/ppermute | solution.py:487
  217.8 8.3 %sums.2 = (f32[512,1024]{1,0:T(8,128)}, f32[512,1024]{1,0:T(8,128)}) custom-call(s32[1]{0:T(128)} %bitcast.refs_0_, bf16[512,512]{1,0:T(8,128)(2,1)} %copy-done.6, bf16[512,512]{1,0:T(8,128)(2,1)} %copy-done.7, bf16[512,512]{1,0:T(8,128)(2,1)} %copy-done.8, bf16[512,512]{1,0:T(8,128)(2,1)} %copy-done.16, bf16[1024,3072]{1,0:T(8,128)(2,1)} %refs_16_.3, ...), custom_call_target="tpu_custom_call" | custom-call | flops 2147483648 | bytes 16777216 | tf_op jit(solution)/shard_map/sums/pallas_call | solution.py:466
  226.1 26.5 %collective-permute-done.18 = bf16[2,512,512]{2,1,0:T(8,128)(2,1)} collective-permute-done((bf16[2,512,512]{2,1,0:T(8,128)(2,1)}, bf16[2,512,512]{2,1,0:T(8,128)(2,1)}, u32[]{:S(2)}, u32[]{:S(2)}) %collective-permute-start.18) | collective-permute-done | bytes 1048608 | tf_op jit(solution)/shard_map/ppermute | solution.py:487
  255.2 5.8 %collective-permute-done.12.refs_4_.refs_6_ = bf16[512,512]{1,0:T(8,128)(2,1)S(1)} collective-permute-done((bf16[512,512]{1,0:T(8,128)(2,1)}, bf16[512,512]{1,0:T(8,128)(2,1)S(1)}, u32[]{:S(2)}, u32[]{:S(2)}) %collective-permute-start.12) | collective-permute-done | bytes 524320 | tf_op jit(solution)/shard_map/ppermute | solution.py:654
  261.8 9.9 %sums.3 = (bf16[512,1024]{1,0:T(8,128)(2,1)}, f32[512,1024]{1,0:T(8,128)}, f32[1,1024]{1,0:T(1,128)}, f32[1,1024]{1,0:T(1,128)}, f32[1,1024]{1,0:T(1,128)}) custom-call(s32[1]{0:T(128)} %bitcast.refs_0_, bf16[512,512]{1,0:T(8,128)(2,1)} %copy-done.4, bf16[512,512]{1,0:T(8,128)(2,1)} %copy-done.10, bf16[512,512]{1,0:T(8,128)(2,1)} %copy-done.12, ...), custom_call_target="tpu_custom_call" | custom-call | flops 2147483648 | bytes 16777216 | tf_op jit(solution)/shard_map/sums/pallas_call | solution.py:466
  294.0 10.0 %collective-permute-done.48 = bf16[1,512,512]{2,1,0:T(8,128)(2,1)S(1)} collective-permute-done((bf16[1,512,512]{2,1,0:T(8,128)(2,1)}, bf16[1,512,512]{2,1,0:T(8,128)(2,1)S(1)}, u32[]{:S(2)}, u32[]{:S(2)}) %collective-permute-start.48) | collective-permute-done | bytes 524320 | tf_op jit(solution)/shard_map/ppermute | solution.py:487
  318.5 9.8 %collective-permute-done.50 = bf16[2,256,512]{2,1,0:T(8,128)(2,1)S(1)} collective-permute-done((bf16[2,256,512]{2,1,0:T(8,128)(2,1)S(1)}, bf16[2,256,512]{2,1,0:T(8,128)(2,1)S(1)}, u32[]{:S(2)}, u32[]{:S(2)}) %collective-permute-start.50) | collective-permute-done | bytes 524320 | tf_op jit(solution)/shard_map/ppermute | solution.py:487
  330.2 8.0 %collective-permute-done.27 = bf16[2,4,64,512]{3,2,1,0:T(8,128)(2,1)S(1)} collective-permute-done((bf16[2,4,64,512]{3,2,1,0:T(8,128)(2,1)S(1)}, bf16[2,4,64,512]{3,2,1,0:T(8,128)(2,1)S(1)}, u32[]{:S(2)}, u32[]{:S(2)}) %collective-permute-start.27) | collective-permute-done | bytes 524320 | tf_op jit(solution)/shard_map/ppermute | solution.py:487
  339.8 5.1 %collective-permute-done.28 = bf16[1,4,64,512]{3,2,1,0:T(8,128)(2,1)S(1)} collective-permute-done((bf16[1,4,64,512]{3,2,1,0:T(8,128)(2,1)S(1)}, bf16[1,4,64,512]{3,2,1,0:T(8,128)(2,1)S(1)}, u32[]{:S(2)}, u32[]{:S(2)}) %collective-permute-start.28) | collective-permute-done | bytes 262176 | tf_op jit(solution)/shard_map/ppermute | solution.py:487
  346.1 7.4 %collective-permute-done.29 = bf16[2,128,512]{2,1,0:T(8,128)(2,1)S(1)} collective-permute-done((bf16[2,128,512]{2,1,0:T(8,128)(2,1)S(1)}, bf16[2,128,512]{2,1,0:T(8,128)(2,1)S(1)}, u32[]{:S(2)}, u32[]{:S(2)}) %collective-permute-start.29) | collective-permute-done | bytes 262176 | tf_op jit(solution)/shard_map/ppermute | solution.py:487
  353.9 6.0 %collective-permute-done.30 = bf16[1,128,512]{2,1,0:T(8,128)(2,1)S(1)} collective-permute-done((bf16[1,128,512]{2,1,0:T(8,128)(2,1)S(1)}, bf16[1,128,512]{2,1,0:T(8,128)(2,1)S(1)}, u32[]{:S(2)}, u32[]{:S(2)}) %collective-permute-start.30) | collective-permute-done | bytes 131104 | tf_op jit(solution)/shard_map/ppermute | solution.py:487
  385.6 4.7 %collective-permute-done.41 = bf16[2,128,512]{2,1,0:T(8,128)(2,1)S(1)} collective-permute-done((bf16[2,128,512]{2,1,0:T(8,128)(2,1)S(1)}, bf16[2,128,512]{2,1,0:T(8,128)(2,1)S(1)}, u32[]{:S(2)}, u32[]{:S(2)}) %collective-permute-start.41) | collective-permute-done | bytes 262176 | tf_op jit(solution)/shard_map/ppermute | solution.py:487
  416.9 5.3 %copy.36 = f32[8,32,4,2,512]{4,3,2,1,0:T(2,128)} copy(f32[8,32,4,2,512]{4,1,2,0,3:T(8,128)S(1)} %convert_bitcast_fusion.1) | data formatting | bytes 8388608 | tf_op jit(solution)/shard_map/convert_element_type | solution.py:729
  422.2 6.6 %reshape.373 = f32[256,4096]{1,0:T(8,128)} reshape(f32[8,32,4,2,512]{4,3,2,1,0:T(2,128)} %copy.36) | data formatting | bytes 8388608 | tf_op jit(solution)/shard_map/convert_element_type | solution.py:729
  (288 shorter events, 178.0 us)
Async XLA Ops:
  30.5 53.9 %collective-permute-start.6 = (bf16[8,4,128,512]{3,2,1,0:T(8,128)(2,1)}, bf16[8,4,128,512]{3,2,1,0:T(8,128)(2,1)}, u32[]{:S(2)}, u32[]{:S(2)}) collective-permute-start(bf16[8,4,128,512]{3,2,1,0:T(8,128)(2,1)} %get-tuple-element.99), channel_id=1, source_target_pairs={{0,4},{4,0},{8,12},{12,8},{16,20},{20,16},{24,28},{28,24},{1,5},{5... | collective-permute-start | bytes 12582920 | tf_op jit(solution)/shard_map/ppermute | solution.py:487
  31.0 56.6 %collective-permute-start.7 = (bf16[8,4,128,512]{3,2,1,0:T(8,128)(2,1)}, bf16[8,4,128,512]{3,2,1,0:T(8,128)(2,1)}, u32[]{:S(2)}, u32[]{:S(2)}) collective-permute-start(bf16[8,4,128,512]{3,2,1,0:T(8,128)(2,1)} %get-tuple-element.101), channel_id=1, source_target_pairs={{0,4},{4,0},{8,12},{12,8},{16,20},{20,16},{24,28},{28,24},{1,5},{5... | collective-permute-start | bytes 12582920 | tf_op jit(solution)/shard_map/ppermute | solution.py:487
  36.6 61.6 %collective-permute-start.3 = (bf16[512,512]{1,0:T(8,128)(2,1)}, bf16[512,512]{1,0:T(8,128)(2,1)S(1)}, u32[]{:S(2)}, u32[]{:S(2)}) collective-permute-start(bf16[512,512]{1,0:T(8,128)(2,1)} %get-tuple-element.88), channel_id=1, source_target_pairs={{0,1},{1,2},{2,3},{3,0},{4,5},{5,6},{6,7},{7,4},{8,9},{9,10},{10,1... | collective-permute-start | bytes 1572872 | tf_op jit(solution)/shard_map/ppermute | solution.py:654
  44.2 54.0 %collective-permute-start.4 = (bf16[512,512]{1,0:T(8,128)(2,1)}, bf16[512,512]{1,0:T(8,128)(2,1)S(1)}, u32[]{:S(2)}, u32[]{:S(2)}) collective-permute-start(bf16[512,512]{1,0:T(8,128)(2,1)} %get-tuple-element.89), channel_id=1, source_target_pairs={{0,2},{1,3},{2,0},{3,1},{4,6},{5,7},{6,4},{7,5},{8,10},{9,11},{10,... | collective-permute-start | bytes 1572872 | tf_op jit(solution)/shard_map/ppermute | solution.py:654
  51.4 47.6 %collective-permute-start.5 = (bf16[512,512]{1,0:T(8,128)(2,1)}, bf16[512,512]{1,0:T(8,128)(2,1)}, u32[]{:S(2)}, u32[]{:S(2)}) collective-permute-start(bf16[512,512]{1,0:T(8,128)(2,1)} %get-tuple-element.90), channel_id=1, source_target_pairs={{0,3},{1,0},{2,1},{3,2},{4,7},{5,4},{6,5},{7,6},{8,11},{9,8},{10,9... | collective-permute-start | bytes 1572872 | tf_op jit(solution)/shard_map/ppermute | solution.py:654
  99.0 47.1 %collective-permute-start.8 = (bf16[2,4,256,512]{3,2,1,0:T(8,128)(2,1)}, bf16[2,4,256,512]{3,2,1,0:T(8,128)(2,1)}, u32[]{:S(2)}, u32[]{:S(2)}) collective-permute-start(bf16[2,4,256,512]{3,2,1,0:T(8,128)(2,1)} %pad_maximum_fusion.1), channel_id=1, source_target_pairs={{0,8},{4,12},{8,0},{12,4},{16,24},{20,28},{24,16},{28,20},{1,9},{5... | collective-permute-start | bytes 6291464 | tf_op jit(solution)/shard_map/ppermute | solution.py:487
  100.5 46.8 %collective-permute-start.9 = (bf16[2,4,256,512]{3,2,1,0:T(8,128)(2,1)}, bf16[2,4,256,512]{3,2,1,0:T(8,128)(2,1)}, u32[]{:S(2)}, u32[]{:S(2)}) collective-permute-start(bf16[2,4,256,512]{3,2,1,0:T(8,128)(2,1)} %pad_maximum_fusion.3), channel_id=1, source_target_pairs={{0,16},{4,20},{8,24},{12,28},{16,0},{20,4},{24,8},{28,12},{1,17},{... | collective-permute-start | bytes 6291464 | tf_op jit(solution)/shard_map/ppermute | solution.py:487
  102.0 52.0 %collective-permute-start = (bf16[512,512]{1,0:T(8,128)(2,1)}, bf16[512,512]{1,0:T(8,128)(2,1)}, u32[]{:S(2)}, u32[]{:S(2)}) collective-permute-start(bf16[512,512]{1,0:T(8,128)(2,1)} %get-tuple-element.92), channel_id=1, source_target_pairs={{0,1},{1,2},{2,3},{3,0},{4,5},{5,6},{6,7},{7,4},{8,9},{9,10},{10,1... | collective-permute-start | bytes 1572872 | tf_op jit(solution)/shard_map/ppermute | solution.py:654
  102.6 54.1 %collective-permute-start.1 = (bf16[512,512]{1,0:T(8,128)(2,1)}, bf16[512,512]{1,0:T(8,128)(2,1)}, u32[]{:S(2)}, u32[]{:S(2)}) collective-permute-start(bf16[512,512]{1,0:T(8,128)(2,1)} %get-tuple-element.93), channel_id=1, source_target_pairs={{0,2},{1,3},{2,0},{3,1},{4,6},{5,7},{6,4},{7,5},{8,10},{9,11},{10,... | collective-permute-start | bytes 1572872 | tf_op jit(solution)/shard_map/ppermute | solution.py:654
  103.0 53.7 %collective-permute-start.2 = (bf16[512,512]{1,0:T(8,128)(2,1)}, bf16[512,512]{1,0:T(8,128)(2,1)}, u32[]{:S(2)}, u32[]{:S(2)}) collective-permute-start(bf16[512,512]{1,0:T(8,128)(2,1)} %get-tuple-element.94), channel_id=1, source_target_pairs={{0,3},{1,0},{2,1},{3,2},{4,7},{5,4},{6,5},{7,6},{8,11},{9,8},{10,9... | collective-permute-start | bytes 1572872 | tf_op jit(solution)/shard_map/ppermute | solution.py:654
  146.1 45.5 %collective-permute-start.13 = (bf16[512,512]{1,0:T(8,128)(2,1)S(1)}, bf16[512,512]{1,0:T(8,128)(2,1)S(1)}, u32[]{:S(2)}, u32[]{:S(2)}) collective-permute-start(bf16[512,512]{1,0:T(8,128)(2,1)S(1)} %get-tuple-element.108), channel_id=1, source_target_pairs={{0,1},{1,2},{2,3},{3,0},{4,5},{5,6},{6,7},{7,4},{8,9},{9,10},{10,1... | collective-permute-start | bytes 1572872 | tf_op jit(solution)/shard_map/ppermute | solution.py:654
  147.3 44.3 %collective-permute-start.14 = (bf16[512,512]{1,0:T(8,128)(2,1)S(1)}, bf16[512,512]{1,0:T(8,128)(2,1)S(1)}, u32[]{:S(2)}, u32[]{:S(2)}) collective-permute-start(bf16[512,512]{1,0:T(8,128)(2,1)S(1)} %get-tuple-element.109), channel_id=1, source_target_pairs={{0,2},{1,3},{2,0},{3,1},{4,6},{5,7},{6,4},{7,5},{8,10},{9,11},{10,... | collective-permute-start | bytes 1572872 | tf_op jit(solution)/shard_map/ppermute | solution.py:654
  154.0 38.4 %collective-permute-start.15 = (bf16[512,512]{1,0:T(8,128)(2,1)S(1)}, bf16[512,512]{1,0:T(8,128)(2,1)S(1)}, u32[]{:S(2)}, u32[]{:S(2)}) collective-permute-start(bf16[512,512]{1,0:T(8,128)(2,1)S(1)} %get-tuple-element.110), channel_id=1, source_target_pairs={{0,3},{1,0},{2,1},{3,2},{4,7},{5,4},{6,5},{7,6},{8,11},{9,8},{10,9... | collective-permute-start | bytes 1572872 | tf_op jit(solution)/shard_map/ppermute | solution.py:654
  156.7 32.0 %collective-permute-start.16 = (bf16[1,4,256,512]{3,2,1,0:T(8,128)(2,1)S(1)}, bf16[1,4,256,512]{3,2,1,0:T(8,128)(2,1)S(1)}, u32[]{:S(2)}, u32[]{:S(2)}) collective-permute-start(bf16[1,4,256,512]{3,2,1,0:T(8,128)(2,1)S(1)} %get-tuple-element.125), channel_id=1, source_target_pairs={{0,16},{4,20},{8,24},{12,28},{16,0},{20,4},{24,8},{28,12},{1,17},{... | collective-permute-start | bytes 3145736 | tf_op jit(solution)/shard_map/ppermute | solution.py:487
  158.2 30.5 %collective-permute-start.17 = (bf16[1,4,256,512]{3,2,1,0:T(8,128)(2,1)S(1)}, bf16[1,4,256,512]{3,2,1,0:T(8,128)(2,1)S(1)}, u32[]{:S(2)}, u32[]{:S(2)}) collective-permute-start(bf16[1,4,256,512]{3,2,1,0:T(8,128)(2,1)S(1)} %get-tuple-element.126), channel_id=1, source_target_pairs={{0,8},{4,12},{8,0},{12,4},{16,24},{20,28},{24,16},{28,20},{1,9},{5... | collective-permute-start | bytes 3145736 | tf_op jit(solution)/shard_map/ppermute | solution.py:487
  193.2 59.4 %collective-permute-start.18 = (bf16[2,512,512]{2,1,0:T(8,128)(2,1)}, bf16[2,512,512]{2,1,0:T(8,128)(2,1)}, u32[]{:S(2)}, u32[]{:S(2)}) collective-permute-start(bf16[2,512,512]{2,1,0:T(8,128)(2,1)} %get-tuple-element.131), channel_id=1, source_target_pairs={{0,1},{1,0},{2,3},{3,2},{4,5},{5,4},{6,7},{7,6},{8,9},{9,8},{10,11... | collective-permute-start | bytes 3145736 | tf_op jit(solution)/shard_map/ppermute | solution.py:487
  206.4 48.8 %collective-permute-start.10 = (bf16[512,512]{1,0:T(8,128)(2,1)}, bf16[512,512]{1,0:T(8,128)(2,1)S(1)}, u32[]{:S(2)}, u32[]{:S(2)}) collective-permute-start(bf16[512,512]{1,0:T(8,128)(2,1)} %copy-done.26), channel_id=1, source_target_pairs={{0,1},{1,2},{2,3},{3,0},{4,5},{5,6},{6,7},{7,4},{8,9},{9,10},{10,1... | collective-permute-start | bytes 1572872 | tf_op jit(solution)/shard_map/ppermute | solution.py:654
  206.5 48.7 %collective-permute-start.11 = (bf16[512,512]{1,0:T(8,128)(2,1)}, bf16[512,512]{1,0:T(8,128)(2,1)S(1)}, u32[]{:S(2)}, u32[]{:S(2)}) collective-permute-start(bf16[512,512]{1,0:T(8,128)(2,1)} %copy-done.25), channel_id=1, source_target_pairs={{0,2},{1,3},{2,0},{3,1},{4,6},{5,7},{6,4},{7,5},{8,10},{9,11},{10,... | collective-permute-start | bytes 1572872 | tf_op jit(solution)/shard_map/ppermute | solution.py:654
  207.0 54.0 %collective-permute-start.12 = (bf16[512,512]{1,0:T(8,128)(2,1)}, bf16[512,512]{1,0:T(8,128)(2,1)S(1)}, u32[]{:S(2)}, u32[]{:S(2)}) collective-permute-start(bf16[512,512]{1,0:T(8,128)(2,1)} %copy-done.24), channel_id=1, source_target_pairs={{0,3},{1,0},{2,1},{3,2},{4,7},{5,4},{6,5},{7,6},{8,11},{9,8},{10,9... | collective-permute-start | bytes 1572872 | tf_op jit(solution)/shard_map/ppermute | solution.py:654
  217.8 97.9 %collective-permute-start.24 = (bf16[8,4,64,512]{3,2,1,0:T(8,128)(2,1)}, bf16[8,4,64,512]{3,2,1,0:T(8,128)(2,1)S(1)}, u32[]{:S(2)}, u32[]{:S(2)}) collective-permute-start(bf16[8,4,64,512]{3,2,1,0:T(8,128)(2,1)} %dynamic-slice_bitcast_fusion.1), channel_id=1, source_target_pairs={{0,4},{4,0},{8,12},{12,8},{16,20},{20,16},{24,28},{28,24},{1,5},{5... | collective-permute-start | bytes 6291464 | tf_op jit(solution)/shard_map/ppermute | solution.py:487
  276.4 27.6 %collective-permute-start.48 = (bf16[1,512,512]{2,1,0:T(8,128)(2,1)}, bf16[1,512,512]{2,1,0:T(8,128)(2,1)S(1)}, u32[]{:S(2)}, u32[]{:S(2)}) collective-permute-start(bf16[1,512,512]{2,1,0:T(8,128)(2,1)} %get-tuple-element.153), channel_id=1, source_target_pairs={{0,2},{1,3},{2,0},{3,1},{4,6},{5,7},{6,4},{7,5},{8,10},{9,11},{10,... | collective-permute-start | bytes 1572872 | tf_op jit(solution)/shard_map/ppermute | solution.py:487
  307.9 45.9 %collective-permute-start.36 = (bf16[8,4,64,512]{3,2,1,0:T(8,128)(2,1)S(1)}, bf16[8,4,64,512]{3,2,1,0:T(8,128)(2,1)S(1)}, u32[]{:S(2)}, u32[]{:S(2)}) collective-permute-start(bf16[8,4,64,512]{3,2,1,0:T(8,128)(2,1)S(1)} %dynamic-slice_bitcast_fusion), channel_id=1, source_target_pairs={{0,4},{4,0},{8,12},{12,8},{16,20},{20,16},{24,28},{28,24},{1,5},{5... | collective-permute-start | bytes 6291464 | tf_op jit(solution)/shard_map/ppermute | solution.py:487
  316.3 22.0 %collective-permute-start.27 = (bf16[2,4,64,512]{3,2,1,0:T(8,128)(2,1)S(1)}, bf16[2,4,64,512]{3,2,1,0:T(8,128)(2,1)S(1)}, u32[]{:S(2)}, u32[]{:S(2)}) collective-permute-start(bf16[2,4,64,512]{3,2,1,0:T(8,128)(2,1)S(1)} %fusion.20), channel_id=1, source_target_pairs={{0,16},{4,20},{8,24},{12,28},{16,0},{20,4},{24,8},{28,12},{1,17},{... | collective-permute-start | bytes 1572872 | tf_op jit(solution)/shard_map/ppermute | solution.py:487
  346.0 59.1 %collective-permute-start.53 = (bf16[2,2,2,256,512]{4,3,2,1,0:T(8,128)(2,1)S(1)}, bf16[2,2,2,256,512]{4,3,2,1,0:T(8,128)(2,1)S(1)}, u32[]{:S(2)}, u32[]{:S(2)}) collective-permute-start(bf16[2,2,2,256,512]{4,3,2,1,0:T(8,128)(2,1)S(1)} %pad_maximum_fusion.5), channel_id=1, source_target_pairs={{0,4},{4,0},{8,12},{12,8},{16,20},{20,16},{24,28},{28,24},{1,5},{5... | collective-permute-start | bytes 6291464 | tf_op jit(solution)/shard_map/ppermute | solution.py:487
  (64 other events, 621.5 us)

commit v3 on v1

--- a/solution.py
+++ b/solution.py
@@ -18,6 +18,8 @@
 BF16 = jnp.bfloat16
 F32 = jnp.float32
 MIB = 1 << 20
+SHORT = pl.CostEstimate(flops=1000, bytes_accessed=1000, transcendentals=0)
+LONG = pl.CostEstimate(flops=10**11, bytes_accessed=1000, transcendentals=0)
 
 
 def dot_nn(left, right):
@@ -46,6 +48,14 @@
     cosine[:, :ROT] = np.repeat(np.cos(phases), 2, axis=1)
     sine[:, :ROT] = np.repeat(np.sin(phases), 2, axis=1) * np.tile(np.array([-1.0, 1.0], np.float32), ROT // 2)
     return np.tile(cosine, (1, 2)), np.tile(sine, (1, 2))
+
+
+def whole(array):
+    shape = array.shape
+    return pl.BlockSpec(shape, lambda i: (0,) * len(shape))
+
+
+SCALARS = pl.BlockSpec(memory_space=pltpu.SMEM)
 
 
 def prep_kernel(hidden_ref, mark_ref, table_ref, gain_ref, bias_ref, stream_ref, normed_ref, turned_ref):
@@ -84,13 +94,15 @@
             jax.ShapeDtypeStruct((rows, width), BF16),
             jax.ShapeDtypeStruct((width, rows), BF16),
         ],
+        cost_estimate=SHORT,
         name="prep",
     )(hidden, marked, table, gain, bias)
 
 
-def heads_kernel(place_ref, normed_ref, cot_ref, wq_ref, wk_ref, wv_ref, wo_ref, cos_ref, sin_ref, *out_refs):
+def heads_kernel(owners_ref, normed_ref, cot_ref, wq_ref, wk_ref, wv_ref, wo_ref, cos_ref, sin_ref, *out_refs):
     normed = normed_ref[...]
-    chunks = len(out_refs)
+    shifts = pl.num_programs(0)
+    chunks = wq_ref.shape[1] // PAIR
     cosine = jnp.concatenate([cos_ref[...]] * chunks, axis=1)
     sine = jnp.concatenate([sin_ref[...]] * chunks, axis=1)
 
@@ -103,46 +115,53 @@
         dot_nn(normed, wv_ref[...]).astype(BF16),
         dot_nt(cot_ref[...], wo_ref[...]).astype(BF16),
     )
-    for chunk in range(chunks):
-        for number, part in enumerate(parts):
-            out_refs[chunk][:, number * PAIR : (number + 1) * PAIR] = part[:, chunk * PAIR : (chunk + 1) * PAIR]
-
-
-def heads_of(owner, normed, cot, qkv_weight, out_weight, cosine, sine, owners):
+    for number, out_ref in enumerate(out_refs):
+        shift, chunk = divmod(number, chunks)
+
+        @pl.when(pl.program_id(0) == shift)
+        def _():
+            for at, part in enumerate(parts):
+                out_ref[:, at * PAIR : (at + 1) * PAIR] = part[:, chunk * PAIR : (chunk + 1) * PAIR]
+
+
+def heads_of(order, normed, cot, qkv_weight, out_weight, cosine, sine):
     rows, width = normed.shape
+    owners = order.shape[0]
     wide = width // owners
     chunks = wide // PAIR
-    return pl.pallas_call(
+    fixed = pl.BlockSpec((rows, width), lambda i, o: (0, 0))
+    table = pl.BlockSpec((rows, PAIR), lambda i, o: (0, 0))
+
+    def columns(part):
+        return pl.BlockSpec((width, wide), lambda i, o: (0, part * owners + o[i]))
+
+    blocks = pl.pallas_call(
         heads_kernel,
         grid_spec=pltpu.PrefetchScalarGridSpec(
             num_scalar_prefetch=1,
-            grid=(1,),
-            in_specs=[
-                pl.BlockSpec((rows, width), lambda i, o: (0, 0)),
-                pl.BlockSpec((rows, width), lambda i, o: (0, 0)),
-                pl.BlockSpec((width, wide), lambda i, o: (0, o[0])),
-                pl.BlockSpec((width, wide), lambda i, o: (0, owners + o[0])),
-                pl.BlockSpec((width, wide), lambda i, o: (0, 2 * owners + o[0])),
-                pl.BlockSpec((wide, width), lambda i, o: (o[0], 0)),
-                pl.BlockSpec((rows, PAIR), lambda i, o: (0, 0)),
-                pl.BlockSpec((rows, PAIR), lambda i, o: (0, 0)),
-            ],
-            out_specs=[pl.BlockSpec((rows, 4 * PAIR), lambda i, o: (0, 0))] * chunks,
+            grid=(owners,),
+            in_specs=[fixed, fixed]
+            + [columns(part) for part in range(3)]
+            + [pl.BlockSpec((wide, width), lambda i, o: (o[i], 0)), table, table],
+            out_specs=[pl.BlockSpec((rows, 4 * PAIR), lambda i, o: (0, 0))] * (owners * chunks),
         ),
-        out_shape=[jax.ShapeDtypeStruct((rows, 4 * PAIR), BF16)] * chunks,
+        out_shape=[jax.ShapeDtypeStruct((rows, 4 * PAIR), BF16)] * (owners * chunks),
+        compiler_params=pltpu.CompilerParams(vmem_limit_bytes=60 * MIB),
+        cost_estimate=SHORT,
         name="heads",
-    )(owner, normed, cot, qkv_weight, qkv_weight, qkv_weight, out_weight, cosine, sine)
-
-
-QUERY_ROWS = 256
-KEY_ROWS = 256
+    )(order, normed, cot, qkv_weight, qkv_weight, qkv_weight, out_weight, cosine, sine)
+    return [[blocks[shift * chunks + chunk] for shift in range(owners)] for chunk in range(chunks)]
+
+
+QUERY_ROWS = 512
+KEY_ROWS = QUERY_ROWS
 
 
 def attention_kernel(pieces, info_ref, *refs):
     piece_refs = refs[:pieces]
     cos_ref, sin_ref = refs[pieces : pieces + 2]
-    out_refs = refs[pieces + 2 : 2 * pieces + 2]
-    held, results, key_turned, value_turned, raised_ref, key_sum, value_sum = refs[2 * pieces + 2 :]
+    out_refs = refs[pieces + 2 : -9]
+    held, results, key_turned, value_turned, doubled, score_ref, raised_ref, key_sum, value_sum = refs[-9:]
     me, end = info_ref[0], info_ref[1]
     rows = piece_refs[0].shape[0]
     length = rows * pieces
@@ -151,10 +170,17 @@
         held[pl.ds(start, rows), :] = piece_refs[shift][...]
     key_turned[...] = held[:, PAIR : 2 * PAIR].T
     value_turned[...] = held[:, 2 * PAIR : 3 * PAIR].T
+    for head in range(2):
+        keys = held[:, PAIR + head * HEAD_DIM : PAIR + (head + 1) * HEAD_DIM]
+        doubled[head] = jnp.concatenate([keys, keys], axis=1)
     key_sum[...] = jnp.zeros_like(key_sum)
     value_sum[...] = jnp.zeros_like(value_sum)
     scale = 0.125 * LOG2E
     halves = lax.broadcasted_iota(jnp.int32, (QUERY_ROWS, PAIR), 1) // HEAD_DIM
+    causal = lax.broadcasted_iota(jnp.int32, (KEY_ROWS, QUERY_ROWS), 0) <= lax.broadcasted_iota(
+        jnp.int32, (KEY_ROWS, QUERY_ROWS), 1
+    )
+    key_steps = lax.broadcasted_iota(jnp.int32, (KEY_ROWS, QUERY_ROWS), 0)
 
     def query_block(number, carry):
         first = pl.multiple_of(number * QUERY_ROWS, QUERY_ROWS)
@@ -162,60 +188,79 @@
         grad_rows = held[pl.ds(first, QUERY_ROWS), 3 * PAIR : 4 * PAIR]
         zero = jnp.zeros_like(query_rows)
         queries = [jnp.where(halves == head, query_rows, zero) for head in range(2)]
-        grads = [jnp.where(halves == head, grad_rows, zero) for head in range(2)]
+        scaled = query_rows.astype(F32) * scale
+        large = scaled.astype(BF16)
+        small = (scaled - large.astype(F32)).astype(BF16)
+        pairs = [
+            jnp.concatenate(
+                [part[:, head * HEAD_DIM : (head + 1) * HEAD_DIM] for part in (large, small)], axis=1
+            )
+            for head in range(2)
+        ]
         query_places = first + lax.broadcasted_iota(jnp.int32, (1, QUERY_ROWS), 1)
         lowest = jnp.where(query_places > end, end + 1, 0)
-        blocks = (number + 1) * (QUERY_ROWS // KEY_ROWS) if QUERY_ROWS >= KEY_ROWS else lax.div(
-            number * QUERY_ROWS, KEY_ROWS
-        ) + 1
-
-        def scores_of(block, highest):
+
+        def scores_of(block, highest, diagonal, parted):
             start = pl.multiple_of(block * KEY_ROWS, KEY_ROWS)
-            keys = held[pl.ds(start, KEY_ROWS), PAIR : 2 * PAIR]
-            key_places = start + lax.broadcasted_iota(jnp.int32, (KEY_ROWS, QUERY_ROWS), 0)
-            seen = (key_places <= query_places) & (key_places >= lowest)
             after = []
             for head in range(2):
-                scores = jnp.where(seen, dot_nt(keys, queries[head]) * scale, BLOCKED)
-                raised_ref[head, pl.ds(start, KEY_ROWS), :] = scores
+                scores = dot_nt(doubled[head, pl.ds(start, KEY_ROWS), :], pairs[head])
+                if diagonal:
+                    scores = jnp.where(causal, scores, BLOCKED)
+                if parted:
+                    scores = jnp.where(key_steps >= lowest - start, scores, BLOCKED)
+                score_ref[head, pl.ds(start, KEY_ROWS), :] = scores
                 after.append(jnp.maximum(highest[head], jnp.max(scores, axis=0, keepdims=True)))
             return tuple(after)
 
+        def any_scores(block, highest, diagonal=False):
+            parted = (first + QUERY_ROWS - 1 > end) & (block * KEY_ROWS <= end)
+            return lax.cond(
+                parted,
+                lambda held_rows: scores_of(block, held_rows, diagonal, True),
+                lambda held_rows: scores_of(block, held_rows, diagonal, False),
+                highest,
+            )
+
         start_row = jnp.full((1, QUERY_ROWS), BLOCKED, F32)
-        highest = lax.fori_loop(0, blocks, scores_of, (start_row, start_row))
+        highest = lax.fori_loop(0, number, any_scores, (start_row, start_row))
+        highest = any_scores(number, highest, True)
 
         def mix(block, carried):
             start = pl.multiple_of(block * KEY_ROWS, KEY_ROWS)
             after = []
             for head in range(2):
                 total, mixed = carried[head]
-                raised = jnp.exp2(raised_ref[head, pl.ds(start, KEY_ROWS), :] - highest[head])
-                raised_ref[head, pl.ds(start, KEY_ROWS), :] = raised
+                raised = jnp.exp2(score_ref[head, pl.ds(start, KEY_ROWS), :] - highest[head])
+                rounded = raised.astype(BF16)
+                raised_ref[head, pl.ds(start, KEY_ROWS), :] = rounded
                 values = value_turned[head * HEAD_DIM : (head + 1) * HEAD_DIM, pl.ds(start, KEY_ROWS)]
-                after.append(
-                    (total + jnp.sum(raised, axis=0, keepdims=True), mixed + dot_nn(values, raised.astype(BF16)))
-                )
+                after.append((total + jnp.sum(raised, axis=0, keepdims=True), mixed + dot_nn(values, rounded)))
             return tuple(after)
 
         empty = (jnp.zeros((1, QUERY_ROWS), F32), jnp.zeros((HEAD_DIM, QUERY_ROWS), F32))
-        mixes = lax.fori_loop(0, blocks, mix, (empty, empty))
+        mixes = lax.fori_loop(0, number + 1, mix, (empty, empty))
         inverse = [1.0 / mixes[head][0] for head in range(2)]
         mixed = jnp.concatenate([mixes[head][1] * inverse[head] for head in range(2)], axis=0)
-        grad_turned = grad_rows.astype(F32).T
-        products = mixed * grad_turned
+        turned = grad_rows.astype(F32).T
+        turned = jnp.concatenate(
+            [turned[head * HEAD_DIM : (head + 1) * HEAD_DIM] * inverse[head] for head in range(2)], axis=0
+        )
+        products = mixed * turned
         delta = [
             jnp.sum(products[head * HEAD_DIM : (head + 1) * HEAD_DIM], axis=0, keepdims=True) for head in range(2)
         ]
+        divided = turned.T.astype(BF16)
+        grads = [jnp.where(halves == head, divided, zero) for head in range(2)]
 
         def back(block, carried):
             start = pl.multiple_of(block * KEY_ROWS, KEY_ROWS)
             values = held[pl.ds(start, KEY_ROWS), 2 * PAIR : 3 * PAIR]
             after, key_terms, value_terms = [], [], []
             for head in range(2):
-                probs = raised_ref[head, pl.ds(start, KEY_ROWS), :] * inverse[head]
-                prob_grad = dot_nt(values, grads[head])
-                score_grad = (probs * (prob_grad - delta[head])).astype(BF16)
-                value_terms.append(dot_nn(probs.astype(BF16), grads[head]))
+                raised = raised_ref[head, pl.ds(start, KEY_ROWS), :]
+                score_grad = raised * (dot_nt(values, grads[head]) - delta[head]).astype(BF16)
+                value_terms.append(dot_nn(raised, grads[head]))
                 key_terms.append(dot_nn(score_grad, queries[head]))
                 keys = key_turned[head * HEAD_DIM : (head + 1) * HEAD_DIM, pl.ds(start, KEY_ROWS)]
                 after.append(carried[head] + dot_nn(keys, score_grad))
@@ -223,7 +268,7 @@
             key_sum[pl.ds(start, KEY_ROWS), :] += key_terms[0] + key_terms[1]
             return tuple(after)
 
-        query_grads = lax.fori_loop(0, blocks, back, (empty[1], empty[1]))
+        query_grads = lax.fori_loop(0, number + 1, back, (empty[1], empty[1]))
         query_grad = jnp.concatenate(query_grads, axis=0).T * 0.125
         cosine = cos_ref[pl.ds(first, QUERY_ROWS), :]
         sine = sin_ref[pl.ds(first, QUERY_ROWS), :]
@@ -242,38 +287,45 @@
 
 def attention(info, parts, cosine, sine):
     pieces = len(parts)
-    rows, wide = parts[0].shape
+    rows = parts[0].shape[0]
     length = rows * pieces
-    whole = pl.BlockSpec(memory_space=pltpu.VMEM)
-    blocks = length // QUERY_ROWS
-    pairs_of = 2 * blocks * (blocks + 1) // 2 * QUERY_ROWS * KEY_ROWS
+    arrays = (*parts, cosine, sine)
+    shapes = [jax.ShapeDtypeStruct((rows, 4 * PAIR), BF16)] * pieces
     return pl.pallas_call(
         lambda *refs: attention_kernel(pieces, *refs),
-        in_specs=[pl.BlockSpec(memory_space=pltpu.SMEM)] + [whole] * (pieces + 2),
-        out_specs=[whole] * pieces,
-        out_shape=[jax.ShapeDtypeStruct((rows, wide), BF16)] * pieces,
+        grid=(1,),
+        in_specs=[SCALARS] + [whole(array) for array in arrays],
+        out_specs=[whole(shape) for shape in shapes],
+        out_shape=shapes,
         scratch_shapes=[
-            pltpu.VMEM((length, wide), BF16),
-            pltpu.VMEM((length, wide), BF16),
+            pltpu.VMEM((length, 4 * PAIR), BF16),
+            pltpu.VMEM((length, 4 * PAIR), BF16),
             pltpu.VMEM((PAIR, length), BF16),
             pltpu.VMEM((PAIR, length), BF16),
+            pltpu.VMEM((2, length, PAIR), BF16),
             pltpu.VMEM((2, length, QUERY_ROWS), F32),
+            pltpu.VMEM((2, length, QUERY_ROWS), BF16),
             pltpu.VMEM((length, PAIR), F32),
             pltpu.VMEM((length, PAIR), F32),
         ],
-        compiler_params=pltpu.CompilerParams(vmem_limit_bytes=40 * MIB),
-        cost_estimate=pl.CostEstimate(
-            flops=12 * 256 * pairs_of, bytes_accessed=2 * 2 * length * wide * 2, transcendentals=pairs_of
-        ),
+        compiler_params=pltpu.CompilerParams(vmem_limit_bytes=60 * MIB),
+        cost_estimate=SHORT,
         name="attention",
-    )(info, *parts, cosine, sine)
-
-
-def feed_kernel(
-    cells, normed_ref, turned_ref, cot_ref, in_ref, bias_ref, down_ref, in_grad, down_grad, bias_grad, out_sum, norm_sum
-):
+    )(info, *arrays)
+
+
+def feed_kernel(cells_ref, normed_ref, turned_ref, cot_ref, in_ref, bias_ref, down_ref, *out_refs):
+    sides = (out_refs[0:2], out_refs[2:4])
+    bias_grad, out_sum, norm_sum = out_refs[4:]
     step = pl.program_id(0)
+    steps = pl.num_programs(0) // 2
     up = math.sqrt(2.0 / math.pi)
+
+    @pl.when(step == 0)
+    def _():
+        out_sum[...] = jnp.zeros_like(out_sum)
+        norm_sum[...] = jnp.zeros_like(norm_sum)
+
     weights = in_ref[...]
     downs = down_ref[...]
     cot = cot_ref[...]
@@ -283,65 +335,276 @@
     half = 0.5 * (1.0 + tanh)
     active = (pre * half).astype(BF16)
     slope = half + 0.5 * pre * (1.0 - tanh * tanh) * (up * (1.0 + 3 * 0.044715 * square))
-    pre_grad_full = (dot_nt(cot, downs) * slope).astype(BF16)
-    in_grad[0] = dot_nn(turned_ref[...], pre_grad_full).astype(BF16)
-    down_grad[0] = dot_tn(active, cot).astype(BF16)
-    bias_grad[0] = jnp.sum(pre_grad_full.astype(F32), axis=0, keepdims=True)
-    out_term = dot_nn(active, downs)
-    norm_term = dot_nt(pre_grad_full, weights)
-
-    @pl.when(step == 0)
-    def _():
-        out_sum[...] = out_term
-        norm_sum[...] = norm_term
-
-    @pl.when(step > 0)
-    def _():
-        out_sum[...] += out_term
-        norm_sum[...] += norm_term
-
-
-def feed_half(cells, normed, turned, cot, in_weight, in_bias, down_weight):
+    pre_grad = (dot_nt(cot, downs) * slope).astype(BF16)
+    in_term = dot_nn(turned_ref[...], pre_grad).astype(BF16)
+    down_term = dot_tn(active, cot).astype(BF16)
+    for side, (in_grad, down_grad) in enumerate(sides):
+
+        @pl.when((step >= steps) == bool(side))
+        def _():
+            pieces, owners, kept, tile = in_grad.shape
+            for owner in range(owners):
+                for piece in range(pieces):
+                    start = (owner * pieces + piece) * kept
+                    in_grad[piece, owner] = in_term[start : start + kept]
+            kept = tile // pieces
+            for group in range(down_term.shape[1] // tile):
+                for piece in range(pieces):
+                    down_grad[piece, 0, group * kept : (group + 1) * kept] = down_term[
+                        piece * kept : (piece + 1) * kept, group * tile : (group + 1) * tile
+                    ]
+
+    bias_grad[0] = jnp.sum(pre_grad.astype(F32), axis=0, keepdims=True)
+    out_sum[...] += dot_nn(active, downs)
+    norm_sum[...] += dot_nt(pre_grad, weights)
+
+
+def feed_forward(cells, normed, turned, cot, in_weight, in_bias, down_weight, pieces):
     rows, width = normed.shape
-    tiles = cells.shape[0]
+    steps = cells.shape[0]
+    owners = steps // 2
     hidden_units = in_weight.shape[1]
-    tile = hidden_units // (2 * tiles)
-    return pl.pallas_call(
+    tile = hidden_units // steps
+    kept = width // owners // pieces
+    tall = owners * kept
+    wide = tile // pieces * (width // tile)
+    fixed = pl.BlockSpec((rows, width), lambda i, c: (0, 0))
+
+    def first(i):
+        return jnp.minimum(i, owners - 1)
+
+    def second(i):
+        return jnp.maximum(i - owners, 0)
+
+    def sides_of(turn):
+        return [
+            pl.BlockSpec((pieces, owners, kept, tile), lambda i, c: (0, 0, turn(i), 0)),
+            pl.BlockSpec((pieces, 1, wide, tile), lambda i, c: (0, turn(i), 0, 0)),
+        ]
+
+    grads = [
+        jax.ShapeDtypeStruct((pieces, owners, tall, tile), BF16),
+        jax.ShapeDtypeStruct((pieces, owners, wide, tile), BF16),
+    ]
+    full = jax.ShapeDtypeStruct((rows, width), F32)
+    results = pl.pallas_call(
         feed_kernel,
         grid_spec=pltpu.PrefetchScalarGridSpec(
             num_scalar_prefetch=1,
-            grid=(tiles,),
+            grid=(steps,),
             in_specs=[
-                pl.BlockSpec((rows, width), lambda i, c: (0, 0)),
+                fixed,
                 pl.BlockSpec((width, rows), lambda i, c: (0, 0)),
-                pl.BlockSpec((rows, width), lambda i, c: (0, 0)),
+                fixed,
                 pl.BlockSpec((width, tile), lambda i, c: (0, c[i])),
                 pl.BlockSpec((1, tile), lambda i, c: (0, c[i])),
                 pl.BlockSpec((tile, width), lambda i, c: (c[i], 0)),
             ],
-            out_specs=[
-                pl.BlockSpec((1, width, tile), lambda i, c: (i, 0, 0)),
-                pl.BlockSpec((1, tile, width), lambda i, c: (i, 0, 0)),
-                pl.BlockSpec((1, 1, tile), lambda i, c: (i, 0, 0)),
-                pl.BlockSpec((rows, width), lambda i, c: (0, 0)),
-                pl.BlockSpec((rows, width), lambda i, c: (0, 0)),
-            ],
+            out_specs=sides_of(first)
+            + sides_of(second)
+            + [pl.BlockSpec((1, 1, tile), lambda i, c: (i, 0, 0)), fixed, fixed],
         ),
-        out_shape=[
-            jax.ShapeDtypeStruct((tiles, width, tile), BF16),
-            jax.ShapeDtypeStruct((tiles, tile, width), BF16),
-            jax.ShapeDtypeStruct((tiles, 1, tile), F32),
-            jax.ShapeDtypeStruct((rows, width), F32),
-            jax.ShapeDtypeStruct((rows, width), F32),
-        ],
-        compiler_params=pltpu.CompilerParams(vmem_limit_bytes=56 * MIB),
-        cost_estimate=pl.CostEstimate(
-            flops=12 * rows * width * hidden_units // 2,
-            bytes_accessed=8 * width * hidden_units // 2,
-            transcendentals=rows * hidden_units // 2,
-        ),
+        out_shape=grads + grads + [jax.ShapeDtypeStruct((steps, 1, tile), F32), full, full],
+        compiler_params=pltpu.CompilerParams(vmem_limit_bytes=60 * MIB),
+        cost_estimate=SHORT,
         name="feed",
     )(cells, normed, turned, cot, in_weight, in_bias, down_weight)
+    return results[:2], results[2:4], *results[4:]
+
+
+def place_columns(me_ref, piece_refs, held):
+    owners = len(piece_refs)
+    for shift in range(owners):
+        owner = lax.rem(me_ref[0] - shift + owners, owners)
+        start = pl.multiple_of(owner * PAIR, PAIR)
+        for part in range(4):
+            held[part, :, pl.ds(start, PAIR)] = piece_refs[shift][:, part * PAIR : (part + 1) * PAIR]
+
+
+def weight_kernel(pieces, info_ref, turned_ref, cot_ref, *refs):
+    owners = len(refs) - 4
+    kept_ref, sent_ref, held, grad = refs[-4:]
+    place_columns(info_ref, refs[:owners], held)
+    kept = PAIR // pieces
+    turned = turned_ref[...]
+    for part in range(3):
+        grad[...] = dot_nn(turned, held[part]).astype(BF16)
+        for side, ref in enumerate((kept_ref, sent_ref)):
+            core = info_ref[1] ^ side
+            for owner in range(owners):
+                for piece in range(pieces):
+                    start = pl.multiple_of(((owner * 2 + core) * pieces + piece) * kept, kept)
+                    ref[piece, owner, part * kept : (part + 1) * kept] = grad[pl.ds(start, kept), :]
+    term = dot_tn(held[3], cot_ref[...]).astype(BF16)
+    rows, half = term.shape[0], term.shape[1] // 2
+    for core in range(2):
+        grad[core * rows : (core + 1) * rows, :] = term[:, core * half : (core + 1) * half]
+    for side, ref in enumerate((kept_ref, sent_ref)):
+        core = info_ref[1] ^ side
+        for owner in range(owners):
+            for piece in range(pieces):
+                start = pl.multiple_of(core * rows + (owner * pieces + piece) * kept, kept)
+                ref[piece, owner, 3 * kept :] = grad[pl.ds(start, kept), :]
+
+
+def weight_grads(info, turned, cot, parts, pieces):
+    owners = len(parts)
+    rows, width = cot.shape
+    kept = PAIR // pieces
+    arrays = (turned, cot, *parts)
+    shape = jax.ShapeDtypeStruct((pieces, owners, 4 * kept, owners * PAIR), BF16)
+    return pl.pallas_call(
+        lambda *refs: weight_kernel(pieces, *refs),
+        grid=(1,),
+        in_specs=[SCALARS] + [whole(array) for array in arrays],
+        out_specs=[whole(shape)] * 2,
+        out_shape=[shape] * 2,
+        scratch_shapes=[pltpu.VMEM((4, rows, owners * PAIR), BF16), pltpu.VMEM((width, owners * PAIR), BF16)],
+        compiler_params=pltpu.CompilerParams(vmem_limit_bytes=60 * MIB),
+        cost_estimate=SHORT,
+        name="weight_grads",
+    )(info, *arrays)
+
+
+def sums_kernel(last, owners, me_ref, *refs):
+    piece_refs, refs = refs[:owners], refs[owners:]
+    weight_refs, refs = refs[: 3 * owners], refs[3 * owners :]
+    out_weight_refs, refs = refs[:owners], refs[owners:]
+    out_in, norm_in = refs[:2]
+    held = refs[-1]
+    place_columns(me_ref, piece_refs, held)
+    norm = norm_in[...]
+    for part in range(3):
+        weights = jnp.concatenate([ref[...] for ref in weight_refs[part * owners : (part + 1) * owners]], axis=1)
+        norm = norm + dot_nt(held[part], weights)
+    weights = jnp.concatenate([ref[...] for ref in out_weight_refs], axis=0)
+    out = out_in[...] + dot_nn(held[3], weights)
+    if not last:
+        out_ref, norm_ref = refs[2:4]
+        out_ref[...] = out
+        norm_ref[...] = norm
+        return
+    stream_ref, cot_ref, gain_ref, down_bias_ref, out_ref, hidden_ref, gain_grad, bias_grad = refs[2:-1]
+    stream = stream_ref[...]
+    cot = cot_ref[...].astype(F32)
+    out_ref[...] = (stream + out + down_bias_ref[...]).astype(BF16)
+    centre = stream - jnp.mean(stream, axis=-1, keepdims=True)
+    spread = jnp.mean(centre * centre, axis=-1, keepdims=True)
+    inverse = lax.rsqrt(spread + EPSILON)
+    hat = centre * inverse
+    gained = norm * gain_ref[...]
+    hidden_ref[...] = cot + inverse * (
+        gained
+        - jnp.mean(gained, axis=-1, keepdims=True)
+        - hat * jnp.mean(gained * hat, axis=-1, keepdims=True)
+    )
+    gain_grad[...] = jnp.sum(norm * hat, axis=0, keepdims=True)
+    bias_grad[...] = jnp.sum(norm, axis=0, keepdims=True)
+
+
+def sums_of(info, chunk, chunks, parts, qkv_weight, out_weight, sums, final=()):
+    owners = len(parts)
+    rows = parts[0].shape[0]
+    width = qkv_weight.shape[0]
+    last = bool(final)
+
+    def columns(part, owner):
+        at = (part * owners + owner) * chunks + chunk
+        return pl.BlockSpec((width, PAIR), lambda i: (0, at))
+
+    def weight_rows(owner):
+        return pl.BlockSpec((PAIR, width), lambda i: (owner * chunks + chunk, 0))
+
+    full = jax.ShapeDtypeStruct((rows, width), F32)
+    row = jax.ShapeDtypeStruct((1, width), F32)
+    shapes = [jax.ShapeDtypeStruct((rows, width), BF16), full, row, row] if last else [full, full]
+    return pl.pallas_call(
+        lambda *refs: sums_kernel(last, owners, *refs),
+        grid=(1,),
+        in_specs=[SCALARS]
+        + [whole(part) for part in parts]
+        + [columns(part, owner) for part in range(3) for owner in range(owners)]
+        + [weight_rows(owner) for owner in range(owners)]
+        + [whole(array) for array in (*sums, *final)],
+        out_specs=[whole(shape) for shape in shapes],
+        out_shape=shapes,
+        scratch_shapes=[pltpu.VMEM((4, rows, owners * PAIR), BF16)],
+        compiler_params=pltpu.CompilerParams(vmem_limit_bytes=60 * MIB),
+        cost_estimate=SHORT,
+        name="sums",
+    )(info, *parts, *([qkv_weight] * (3 * owners)), *([out_weight] * owners), *sums, *final)
+
+
+def feed_place_kernel(sums_ref, in_ref, down_ref):
+    devices, total, tile = sums_ref.shape
+    kept = 2 * in_ref.shape[0] // devices
+    tiles = in_ref.shape[1] // (2 * tile)
+    rows = down_ref.shape[0] // 2
+    down_kept = 2 * rows // devices
+    for device in range(devices):
+        core, chip = device & 1, device >> 1
+        rows_of = slice(chip * kept, (chip + 1) * kept)
+        for number in range(tiles):
+            column = (2 * number + core) * tile
+            in_ref[rows_of, column : column + tile] = sums_ref[device, number * kept : (number + 1) * kept].astype(F32)
+        start = core * rows + chip * down_kept
+        for group in range(down_ref.shape[1] // tile):
+            at = tiles * kept + group * down_kept
+            down_ref[start : start + down_kept, group * tile : (group + 1) * tile] = sums_ref[
+                device, at : at + down_kept
+            ].astype(F32)
+
+
+def place_feed(sums, in_shape, down_shape):
+    shapes = [jax.ShapeDtypeStruct(in_shape, F32), jax.ShapeDtypeStruct(down_shape, F32)]
+    return pl.pallas_call(
+        feed_place_kernel,
+        grid=(1,),
+        in_specs=[whole(sums)],
+        out_specs=[whole(shape) for shape in shapes],
+        out_shape=shapes,
+        compiler_params=pltpu.CompilerParams(vmem_limit_bytes=60 * MIB),
+        cost_estimate=SHORT,
+        name="place_feed",
+    )(sums)
+
+
+def heads_place_kernel(info_ref, mine_ref, other_ref, qkv_ref, out_ref):
+    core, place = info_ref[0], info_ref[1]
+    masks, total, wide = mine_ref.shape
+    own_rows, width = out_ref.shape
+    kept = own_rows // 2 // masks
+    chunks = total // (4 * kept)
+    owners = wide // PAIR
+    for source, ref in enumerate((mine_ref, other_ref)):
+        at_core = core if source == 0 else 1 - core
+        columns = pl.ds(pl.multiple_of(at_core * (width // 2), width // 2), width // 2)
+        for mask in range(masks):
+            piece = place ^ mask
+            rows = pl.ds(pl.multiple_of(at_core * (own_rows // 2) + piece * kept, kept), kept)
+            for chunk in range(chunks):
+                at = chunk * 4 * kept
+                for part in range(3):
+                    block = ref[mask, at + part * kept : at + (part + 1) * kept].astype(F32)
+                    for owner in range(owners):
+                        column = part * width + (owner * chunks + chunk) * PAIR
+                        qkv_ref[rows, column : column + PAIR] = block[:, owner * PAIR : (owner + 1) * PAIR]
+                out_rows = pl.ds(pl.multiple_of(chunk * PAIR + piece * kept, kept), kept)
+                out_ref[out_rows, columns] = ref[mask, at + 3 * kept : at + 4 * kept].astype(F32)
+
+
+def place_heads(info, mine, other, own_rows, width):
+    shapes = [jax.ShapeDtypeStruct((own_rows, 3 * width), F32), jax.ShapeDtypeStruct((own_rows, width), F32)]
+    return pl.pallas_call(
+        heads_place_kernel,
+        grid=(1,),
+        in_specs=[SCALARS, whole(mine), whole(other)],
+        out_specs=[whole(shape) for shape in shapes],
+        out_shape=shapes,
+        compiler_params=pltpu.CompilerParams(vmem_limit_bytes=60 * MIB),
+        cost_estimate=SHORT,
+        name="place_heads",
+    )(info, mine, other)
 
 
 def exchange(rows, axis, mask):
@@ -349,64 +612,87 @@
     return lax.ppermute(rows, axis, [(place, place ^ mask) for place in range(size)])
 
 
-def halves_of(rows, dim, bit):
-    shape = rows.shape[:dim] + (2, rows.shape[dim] // 2) + rows.shape[dim + 1 :]
-    split = rows.reshape(shape)
-    return (
-        lax.dynamic_index_in_dim(split, 1 - bit, dim, keepdims=False),
-        lax.dynamic_index_in_dim(split, bit, dim, keepdims=False),
-    )
-
-
-def added(left, right):
-    return (left.astype(F32) + right.astype(F32)).astype(BF16)
-
-
-def joined(mine, other, dim, bit):
-    low = jnp.where(bit == 0, mine, other)
-    high = jnp.where(bit == 0, other, mine)
-    return jnp.concatenate([low, high], axis=dim)
-
-
-def bits_of(axis):
-    return lax.axis_size(axis).bit_length() - 1
-
-
-def reduce_over(rows, order):
-    place = lax.axis_index("batch")
-    for bit_number in order:
-        bit = (place >> bit_number) & 1
-        sent, kept = halves_of(rows, 2, bit)
-        rows = added(kept, exchange(sent, "batch", 1 << bit_number))
-    place = lax.axis_index("seq")
-    for bit_number in range(bits_of("seq")):
-        bit = (place >> bit_number) & 1
-        shape = rows.shape
-        split = rows.reshape((shape[0], shape[1] // 2, 2) + shape[2:])
-        sent = lax.dynamic_index_in_dim(split, 1 - bit, 2, keepdims=False)
-        kept = lax.dynamic_index_in_dim(split, bit, 2, keepdims=False)
-        rows = added(kept, exchange(sent, "seq", 1 << bit_number))
-    return rows
-
-
-def gather_over(rows, order):
-    place = lax.axis_index("batch")
-    for bit_number in reversed(order):
-        bit = (place >> bit_number) & 1
-        rows = joined(rows, exchange(rows, "batch", 1 << bit_number), 2, bit)
-    return rows
-
-
-def sum_over_devices(sent, kept):
-    rows = added(kept, exchange(sent, "batch", 1))
-    order = list(range(1, bits_of("batch")))
-    middle = rows.shape[2] // 2
-    ends = []
-    for part, bits in ((rows[:, :, :middle], order), (rows[:, :, middle:], order[::-1])):
-        ends.append(gather_over(reduce_over(part, bits), bits))
-    mine = jnp.concatenate(ends, axis=2)[:, 0]
-    other = exchange(mine, "batch", 1)
-    return joined(mine[None], other[None], 0, lax.axis_index("batch") & 1)
+def around(rows, shift):
+    owners = lax.axis_size("seq")
+    return lax.ppermute(rows, "seq", [(place, (place + shift) % owners) for place in range(owners)])
+
+
+def total_of(*terms):
+    return sum(term.astype(F32) for term in terms).astype(BF16)
+
+
+def picked(rows, index, dim=0):
+    return lax.dynamic_index_in_dim(rows, index, dim, keepdims=False)
+
+
+def add_kernel(places, bits_ref, *refs):
+    outs = refs[len(refs) - len(places) :]
+    for out_ref, terms in zip(outs, places):
+        at = 0
+        for left, right in terms:
+            rows = refs[left].shape[-2]
+            total = refs[left][...].astype(F32) + refs[right][...].astype(F32)
+            out_ref[..., at : at + rows, :] = total.reshape(out_ref.shape[:-2] + total.shape[-2:]).astype(BF16)
+            at += rows
+
+
+def add_pieces(kept, arrived):
+    pieces, owners = kept[0].shape[:2]
+    arrays = [array for pair in zip(kept, arrived) for array in pair]
+    rows = sum(array.shape[2] for array in kept)
+    columns = kept[0].shape[3]
+    return pl.pallas_call(
+        lambda *refs: add_kernel([[(0, 1), (2, 3)]], None, *refs),
+        grid=(pieces,),
+        in_specs=[pl.BlockSpec((1,) + array.shape[1:], lambda i: (i, 0, 0, 0)) for array in arrays],
+        out_specs=pl.BlockSpec((1, owners, rows, columns), lambda i: (i, 0, 0, 0)),
+        out_shape=jax.ShapeDtypeStruct((pieces, owners, rows, columns), BF16),
+        compiler_params=pltpu.CompilerParams(vmem_limit_bytes=60 * MIB),
+        cost_estimate=SHORT,
+        name="add_pieces",
+    )(*arrays)
+
+
+def add_for_chips(chip, kept, arrived):
+    specs, places, arrays = [], [], []
+    chips, owners = kept[0].shape[:2]
+    for mask in range(chips):
+        terms = []
+        for mine, other in zip(kept, arrived):
+            terms.append((len(arrays), len(arrays) + 1))
+            arrays += [mine, other]
+            specs += [pl.BlockSpec((1,) + mine.shape[1:], lambda i, c, mask=mask: (c[0] ^ mask, 0, 0, 0))] * 2
+        places.append(terms)
+    rows = sum(array.shape[2] for array in kept)
+    out = jax.ShapeDtypeStruct((owners, rows, kept[0].shape[3]), BF16)
+    return pl.pallas_call(
+        lambda *refs: add_kernel(places, *refs),
+        grid_spec=pltpu.PrefetchScalarGridSpec(
+            num_scalar_prefetch=1,
+            grid=(1,),
+            in_specs=specs,
+            out_specs=[pl.BlockSpec(out.shape, lambda i, c: (0, 0, 0))] * chips,
+        ),
+        out_shape=[out] * chips,
+        cost_estimate=SHORT,
+        name="add_for_chips",
+    )(chip[None], *arrays)
+
+
+class Order:
+    token = None
+
+    def __call__(self, value):
+        if self.token is None:
+            return value
+        return lax.optimization_barrier((value, self.token))[0]
+
+    def done(self, token):
+        self.token = token
+        return token
+
+    def also(self, *tokens):
+        self.token = (self.token, tokens)
 
 
 def fast_body(
@@ -428,10 +714,12 @@
     width = hidden.shape[2]
     rows = hidden.shape[1]
     owners = lax.axis_size("seq")
+    pieces = lax.axis_size("batch")
     me = lax.axis_index("seq")
     core = lax.axis_index("batch") & 1
     length = rows * owners
-    chunks = width // owners // PAIR
+    own_rows = width // owners
+    chunks = own_rows // PAIR
     end = end_places[0]
 
     places = me * rows + jnp.arange(rows, dtype=jnp.int32)[:, None]
@@ -446,106 +734,129 @@
     cosine, sine = (jnp.asarray(table) for table in trig_tables(length))
     own_cosine = lax.dynamic_slice_in_dim(cosine, me * rows, rows)
     own_sine = lax.dynamic_slice_in_dim(sine, me * rows, rows)
-
-    parts = [[None] * owners for _ in range(chunks)]
-    for shift in list(range(1, owners)) + [0]:
-        owner = lax.rem(me + shift, owners)
-        blocks = heads_of(owner[None], normed, cot, qkv_weight, out_weight, own_cosine, own_sine, owners)
-        for chunk in range(chunks):
-            parts[chunk][shift] = blocks[chunk]
-
-    def shifted(block, shift):
-        if shift == 0:
-            return block
-        return lax.ppermute(block, "seq", [(place, (place + shift) % owners) for place in range(owners)])
-
-    heads = [[shifted(parts[chunk][shift], shift) for shift in range(owners)] for chunk in range(chunks)]
-
+    place = lax.axis_index("batch")
+    info = jnp.stack([me, core]).astype(jnp.int32)
+    spots = jnp.stack([me, end]).astype(jnp.int32)
+    order = Order()
+
+    def moved(blocks, shifts=(2, 1, 3)):
+        return {shift: around(blocks[shift], shift) for shift in shifts}
+
+    def gathered(blocks, arrived):
+        return [blocks[0]] + [arrived[shift] for shift in range(1, owners)]
+
+    def back(rows):
+        return [exchange(rows, "batch", mask) for mask in (2, 4, 6)]
+
+    shifts = lax.rem(me + jnp.arange(owners, dtype=jnp.int32), owners)
+    heads = order.done(heads_of(shifts, normed, cot, qkv_weight, out_weight, own_cosine, own_sine))
+
+    arrived = moved(order(heads[0]))
     cells = 2 * jnp.arange(owners, dtype=jnp.int32)
-    feed = [
-        feed_half(cells + half, normed, turned, cot, in_weight, in_bias[None], down_weight)
-        for half in (1 - core, core)
-    ]
-    tile = in_weight.shape[1] // (2 * owners)
-
-    def in_view(grad):
-        return grad.reshape(owners, owners, width // owners, tile)
-
-    def down_view(grad):
-        return grad.reshape(1, owners, tile, width)
-
-    in_sum = sum_over_devices(in_view(feed[0][0]), in_view(feed[1][0]))
-    down_sum = sum_over_devices(down_view(feed[0][1]), down_view(feed[1][1]))
-    in_weight_grad = jnp.transpose(in_sum, (2, 1, 0, 3)).reshape(width // owners, in_weight.shape[1]).astype(F32)
-    down_weight_grad = down_sum.reshape(2 * tile, width).astype(F32)
-    bias_low = jnp.where(core == 0, feed[1][2], feed[0][2])
-    bias_high = jnp.where(core == 0, feed[0][2], feed[1][2])
-    in_bias_grad = jnp.concatenate([bias_low, bias_high], axis=1).reshape(-1)
-
-    info = jnp.stack([me, end]).astype(jnp.int32)
-    back = []
-    for chunk in range(chunks):
-        results = attention(info, heads[chunk], cosine, sine)
-        back.append([shifted(results[shift], shift) for shift in range(owners)])
-
-    ordered = []
-    for owner in range(owners):
-        ordered.append([])
-        for chunk in range(chunks):
-            stacked = jnp.stack(back[chunk])
-            slot = lax.rem(me - owner + owners, owners)
-            ordered[owner].append(lax.dynamic_index_in_dim(stacked, slot, 0, keepdims=False))
-
-    def columns(part):
-        return [
-            block[:, part * PAIR : (part + 1) * PAIR] for blocks in ordered for block in blocks
-        ]
-
-    joined_grad = jnp.concatenate(columns(0) + columns(1) + columns(2), axis=1)
-    mixed = jnp.concatenate(columns(3), axis=1)
-
-    qkv_weight_grad = dot_nn(turned, joined_grad).astype(BF16)
-    out_weight_grad = dot_tn(mixed, cot).astype(BF16)
-    normed_grad = dot_nt(joined_grad, qkv_weight) + feed[0][4] + feed[1][4]
-
-    def core_halves(grad):
-        split = grad.reshape(1, owners, 2, grad.shape[0] // (2 * owners), grad.shape[1])
-        return (
-            lax.dynamic_index_in_dim(split, 1 - core, 2, keepdims=False),
-            lax.dynamic_index_in_dim(split, core, 2, keepdims=False),
+    cells = jnp.concatenate([cells + 1 - core, cells + core])
+    away, here, in_bias_grad, out_sum, norm_sum = order.done(
+        feed_forward(cells, order(normed), turned, cot, in_weight, in_bias[None], down_weight, pieces // 2)
+    )
+    order.also(arrived)
+
+    feed_arrived = [exchange(array, "batch", 1) for array in order(away)]
+    later = moved(order(heads[1]))
+    first = order.done(attention(spots, gathered(heads[0], order(arrived)), cosine, sine))
+    order.also(feed_arrived)
+    feed_rows = order.done(add_pieces(order(here), feed_arrived))
+    order.also(later)
+
+    groups = [list(range(number, pieces, 2)) for number in range(2)]
+    feed_rows = lax.psum_scatter(
+        order(feed_rows), "batch", scatter_dimension=0, axis_index_groups=groups, tiled=False
+    )
+    arrived = moved(order(first))
+    second = order.done(attention(spots, gathered(heads[1], order(later)), cosine, sine))
+    cot_sum = order.done(jnp.sum(order(cot).astype(F32), axis=0))
+    order.also(arrived)
+
+    parts = gathered(first, order(arrived))
+    first_kept, first_sent = order.done(weight_grads(info, turned, cot, parts, pieces // 2))
+
+    grad_arrived = exchange(order(first_sent), "batch", 1)
+    later = moved(order(second))
+    sums = order.done(sums_of(info, 0, chunks, order(parts), qkv_weight, out_weight, (out_sum, norm_sum)))
+    order.also(grad_arrived)
+    first_held = order.done(add_for_chips(place >> 1, [order(first_kept)], [grad_arrived]))
+    order.also(later, feed_rows)
+
+    feed_rows = lax.psum_scatter(order(feed_rows), "seq", scatter_dimension=0, tiled=False)
+    parts = gathered(second, order(later))
+    second_kept, second_sent = order.done(weight_grads(info, turned, cot, parts, pieces // 2))
+
+    first_arrived = [exchange(order(first_held[mask]), "batch", 2 * mask) for mask in (1, 2, 3)]
+    grad_arrived = exchange(order(second_sent), "batch", 1)
+    output, hidden_grad, gain_grad, bias_grad = order.done(
+        sums_of(
+            info, 1, chunks, order(parts), qkv_weight, out_weight, sums, (stream, cot, norm_gain[None], down_bias[None])
         )
-
-    qkv_sum = sum_over_devices(*core_halves(qkv_weight_grad))
-    out_sum = sum_over_devices(*core_halves(out_weight_grad))
-    qkv_weight_grad = qkv_sum.reshape(width // owners, -1).astype(F32)
-    out_weight_grad = out_sum.reshape(width // owners, -1).astype(F32)
-
-    output = stream + dot_nn(mixed, out_weight) + feed[0][3] + feed[1][3] + down_bias[None]
-    centre = stream - jnp.mean(stream, axis=-1, keepdims=True)
-    spread = jnp.mean(centre * centre, axis=-1, keepdims=True)
-    inverse = lax.rsqrt(spread + EPSILON)
-    hat = centre * inverse
-    gained = normed_grad * norm_gain[None]
-    stream_part = inverse * (
-        gained
-        - jnp.mean(gained, axis=-1, keepdims=True)
-        - hat * jnp.mean(gained * hat, axis=-1, keepdims=True)
-    )
-    hidden_grad = cot.astype(F32) + stream_part
+    )
+    order.also(first_arrived, grad_arrived)
+    second_held = order.done(add_for_chips(place >> 1, [order(second_kept)], [grad_arrived]))
+    bias_low = jnp.where(core == 0, in_bias_grad[owners:], in_bias_grad[:owners])
+    bias_high = jnp.where(core == 0, in_bias_grad[:owners], in_bias_grad[owners:])
     small = jnp.concatenate(
         [
-            in_bias_grad.reshape(owners, -1),
-            jnp.sum(cot.astype(F32), axis=0).reshape(owners, -1),
-            jnp.sum(normed_grad * hat, axis=0).reshape(owners, -1),
-            jnp.sum(normed_grad, axis=0).reshape(owners, -1),
+            jnp.concatenate([bias_low, bias_high], axis=1).reshape(owners, -1),
+            cot_sum.reshape(owners, -1),
+            gain_grad.reshape(owners, -1),
+            bias_grad.reshape(owners, -1),
         ],
         axis=1,
     )
-    small = lax.dynamic_index_in_dim(lax.psum(small, ("batch", "seq")), me, 0, keepdims=False)
-    few = width // owners
+    order.done((second_held, order(small)))
+
+    def send_owners(rows):
+        return [around(picked(rows, lax.rem(me + shift, owners)), shift) for shift in range(1, owners)]
+
+    second_arrived = [exchange(order(second_held[mask]), "batch", 2 * mask) for mask in (1, 2, 3)]
+    small_arrived = exchange(order(small), "batch", 1)
+    order.also(second_arrived, small_arrived, feed_rows)
+    feed_total = lax.all_gather(order(feed_rows), "batch", axis=0)
+    small = small + order(small_arrived)
+    grad_rows = order.done(
+        jnp.concatenate(
+            [
+                total_of(order(held[0]), *arrived)
+                for held, arrived in ((first_held, first_arrived), (second_held, second_arrived))
+            ],
+            axis=1,
+        )
+    )
+    order.also(small)
+
+    grad_rows = order(grad_rows)
+    grad_arrived = send_owners(grad_rows)
+    order.also(grad_arrived)
+    grad_rows = order.done(total_of(picked(grad_rows, me), *order(grad_arrived)))
+
+    grad_back = back(order(grad_rows))
+    order.also(grad_back)
+    grad_mine = order.done(jnp.stack([grad_rows] + order(grad_back)))
+
+    grad_other = exchange(order(grad_mine), "batch", 1)
+    small_arrived = back(order(small))
+    order.also(small_arrived, grad_other)
+    small = order.done(sum(order(small_arrived), small))
+
+    small_arrived = [around(order(small), shift) for shift in range(1, owners)]
+    heads_info = jnp.stack([core, place >> 1]).astype(jnp.int32)
+    qkv_weight_grad, out_weight_grad = order.done(
+        place_heads(heads_info, order(grad_mine), grad_other, own_rows, width)
+    )
+    in_weight_grad, down_weight_grad = order.done(
+        place_feed(order(feed_total), (own_rows, in_weight.shape[1]), (down_weight.shape[0] // owners, width))
+    )
+    small = picked(sum(order(small_arrived), small), me)
+    few = own_rows
     many = in_bias.shape[0] // owners
     return (
-        output.astype(BF16)[None],
+        output[None],
         hidden_grad[None],
         small[many + few : many + 2 * few],
         small[many + 2 * few :],
@@ -877,8 +1188,7 @@
     def body(*arrays):
         hidden = arrays[0]
         owners = mesh.shape["seq"]
-        wide = hidden.shape[2] // owners
-        if hidden.shape[0] == 1 and wide % PAIR == 0:
+        if hidden.shape[0] == 1 and hidden.shape[2] == 2 * PAIR * owners and owners == 4 and mesh.shape["batch"] == 8:
             return fast_body(*arrays)
         return plain_body(*arrays)
 

time: 538 us -> 372 us (0.69)
  waiting for transfers between devices: 152 us -> 93 us
  blocking collectives: 40.2 us -> 0 us
  other arithmetic: 41.2 us -> 9.08 us
  starting transfers between devices: 89.9 us -> 67.1 us
  local copies, waits for them, and re-layouts: 28.3 us -> 9.49 us
  matrix products: 16.1 us -> 0 us
  Pallas kernels: 162 us -> 178 us
  between operations: 3.7 us -> 15.4 us
    ppermute x56 -> x18, waiting for transfers between devices: 122 us -> 56 us  [exchange(): lax.ppermute(rows, axis, [(place, place ^ mask) for place in range(size)])]
    ppermute x56 -> x18, starting transfers between devices: 69.4 us -> 14.8 us  [exchange(): lax.ppermute(rows, axis, [(place, place ^ mask) for place in range(size)])]
    psum x1 -> x0, blocking collectives: 40.2 us -> none  [fast_body(): lax.psum(small, ('batch', 'seq'))]
    ppermute x12 -> x18, starting transfers between devices: 20.4 us -> 52 us  [around(): lax.ppermute(rows, 'seq', [(place, (place + shift) % owners) for place in...]
    convert_element_type x40 -> x3, other arithmetic: 29 us -> 2.77 us  [total_of(): return sum((term.astype(F32) for term in terms)).astype(BF16)]
    pallas_call x4 -> x12, Pallas kernels: 139 us -> 162 us  [the longest x2 61.4 us: attention(): pl.pallas_call(lambda *refs: attention_kernel(pieces, *refs), grid=(1,),...]
    dot_general x4 -> x0, matrix products: 16.1 us -> none  [the longest x2 7.62 us: dot_nn(): lax.dot_general(left, right, (((1,), (0,)), ((), ())), preferred_element_...]
    unnamed x69 -> x38, local copies, waits for them, and re-layouts: 13.4 us -> 5.03 us
  transfers between devices with their start and end apart: 68 -> 39, of which waited for: 30 -> 14; matrix products, arithmetic and copies ran while one was open for 12% -> 2% of each run, Pallas kernels for 29% -> 44%
where the time goes in v3:
time: 372 us
  Pallas kernels  178 us (48%)
  waiting for transfers between devices  93 us (25%)
  starting transfers between devices  67.1 us (18%)
  between operations  15.4 us (4%)
  local copies, waits for them, and re-layouts  9.49 us (3%)
  other arithmetic  9.08 us (2%)
    pallas_call x2, Pallas kernels, attention(): pl.pallas_call(lambda *refs: attention_kernel(pieces, *refs), grid=(1,),...  61.4 us
    ppermute x18, waiting for transfers between devices, exchange(): lax.ppermute(rows, axis, [(place, place ^ mask) for place in range(size)])  56 us
    ppermute x18, starting transfers between devices, around(): lax.ppermute(rows, 'seq', [(place, (place + shift) % owners) for place in...  52 us
    pallas_call x1, Pallas kernels, feed_forward(): pl.pallas_call(feed_kernel, grid_spec=pltpu.PrefetchScalarGridSpec(num_sc...  40.9 us
    ppermute x18, waiting for transfers between devices, around(): lax.ppermute(rows, 'seq', [(place, (place + shift) % owners) for place in...  36.9 us
    pallas_call x2, Pallas kernels, sums_of(): pl.pallas_call(lambda *refs: sums_kernel(last, owners, *refs), grid=(1,),...  19.1 us
    ppermute x18, starting transfers between devices, exchange(): lax.ppermute(rows, axis, [(place, place ^ mask) for place in range(size)])  14.8 us
    pallas_call x2, Pallas kernels, weight_grads(): pl.pallas_call(lambda *refs: weight_kernel(pieces, *refs), grid=(1,), in_...  13.7 us
  transfers between devices with their start and end apart: 39, of which 14 were waited for; matrix products, arithmetic and copies ran while one was open for 2% of the time, Pallas kernels for 44%

profile of v3, /device:TPU:0, one launch (start us, length us, event | category | flops | bytes accessed | tf_op | source)
XLA Modules:
  0.0 371.6 jit_solution(2299603066717857140)
XLA Ops:
  12.5 4.6 %prep.1 = (f32[512,1024]{1,0:T(8,128)}, bf16[512,1024]{1,0:T(8,128)(2,1)}, bf16[1024,512]{1,0:T(8,128)(2,1)}) custom-call(bf16[512,1024]{1,0:T(8,128)(2,1)} %bitcast.48, s32[512,1]{1,0:T(8,128)} %select_select_fusion.mark_ref, bf16[32,1024]{1,0:T(8,128)(2,1)} %table_ref.1, f32[1,1024]{1,0:T(1,128)} %bitcast.56, f32[1,1024]{1,0:T(1,128)} %bitcast.58), custom_call_target="tpu_custom_call" | custom-call | flops 1000 | bytes 1000 | tf_op jit(solution)/shard_map/prep/pallas_call | solution.py:77
  17.1 11.1 %heads.1 = (bf16[512,512]{1,0:T(8,128)(2,1)}, bf16[512,512]{1,0:T(8,128)(2,1)}, bf16[512,512]{1,0:T(8,128)(2,1)}, bf16[512,512]{1,0:T(8,128)(2,1)}, bf16[512,512...) custom-call(s32[4]{0:T(128)} %compare_select_fusion.owners_ref, ...), custom_call_target="tpu_custom_call" | custom-call | flops 1000 | bytes 1000 | tf_op jit(solution)/shard_map/heads/pallas_call | solution.py:138
  35.8 40.9 %feed.1 = (bf16[4,4,256,512]{3,2,1,0:T(8,128)(2,1)}, bf16[4,4,256,512]{3,2,1,0:T(8,128)(2,1)}, bf16[4,4,256,512]{3,2,1,0:T(8,128)(2,1)}, bf16[4,4,256,512]{3,2,1...) custom-call(s32[8]{0:T(128)} %pad_add_fusion.2.cells_ref, ...), custom_call_target="tpu_custom_call" | custom-call | flops 1000 | bytes 1000 | tf_op jit(solution)/shard_map/feed/pallas_call | solution.py:390
  83.3 30.6 %attention.2 = (bf16[512,512]{1,0:T(8,128)(2,1)}, bf16[512,512]{1,0:T(8,128)(2,1)}, bf16[512,512]{1,0:T(8,128)(2,1)}, bf16[512,512]{1,0:T(8,128)(2,1)}) custom-call(s32[2]{0:T(128)} %get-tuple-element.267.refs_0_, bf16[512,512]{1,0:T(8,128)(2,1)} %get-tuple-element.138.refs_1_, bf16[512,512]{1,0:T(8,128)(2,1)} %copy-done.11, bf16[512,512]{1,0:T(8,128)(2,1)} %copy-done.13, ...), custom_call_target="tpu_custom_call" | custom-call | flops 1000 | bytes 1000 | tf_op jit(solution)/shard_map/attention/pallas_call | solution.py:294
  113.9 9.5 %add_pieces.1 = bf16[4,4,512,512]{3,2,1,0:T(8,128)(2,1)} custom-call(bf16[4,4,256,512]{3,2,1,0:T(8,128)(2,1)} %get-tuple-element.166.refs_0_, bf16[4,4,256,512]{3,2,1,0:T(8,128)(2,1)} %collective-permute-done.6.refs_1_, bf16[4,4,256,512]{3,2,1,0:T(8,128)(2,1)} %get-tuple-element.167.refs_2_, bf16[4,4,256,512]{3,2,1,0:T(8,128)(2,1)} %collective-permute-done.7.refs_3_), custom_call_target="tpu_custom_call" | custom-call | flops 1000 | bytes 1000 | tf_op jit(solution)/shard_map/add_pieces/pallas_call | solution.py:644
  124.4 3.9 %collective-permute-start.8 = (bf16[512,512]{1,0:T(8,128)(2,1)}, bf16[512,512]{1,0:T(8,128)(2,1)S(1)}, u32[]{:S(2)}, u32[]{:S(2)}) collective-permute-start(bf16[512,512]{1,0:T(8,128)(2,1)} %get-tuple-element.175), channel_id=1, source_target_pairs={{0,1},{1,2},{2,3},{3,0},{4,5},{5,6},{6,7},{7,4},{8,9},{9,10},{10,1... | collective-permute-start | bytes 1572872 | tf_op jit(solution)/shard_map/ppermute | solution.py:617
  130.7 30.7 %attention.3 = (bf16[512,512]{1,0:T(8,128)(2,1)}, bf16[512,512]{1,0:T(8,128)(2,1)}, bf16[512,512]{1,0:T(8,128)(2,1)}, bf16[512,512]{1,0:T(8,128)(2,1)}) custom-call(s32[2]{0:T(128)} %get-tuple-element.267.refs_0_, bf16[512,512]{1,0:T(8,128)(2,1)} %get-tuple-element.134.refs_1_, bf16[512,512]{1,0:T(8,128)(2,1)} %copy-done.12, bf16[512,512]{1,0:T(8,128)(2,1)} %copy-done.14, ...), custom_call_target="tpu_custom_call" | custom-call | flops 1000 | bytes 1000 | tf_op jit(solution)/shard_map/attention/pallas_call | solution.py:294
  164.8 6.9 %weight_grads.2 = (bf16[4,4,128,512]{3,2,1,0:T(8,128)(2,1)}, bf16[4,4,128,512]{3,2,1,0:T(8,128)(2,1)}) custom-call(s32[2]{0:T(128)} %get-tuple-element.266.refs_0_, bf16[1024,512]{1,0:T(8,128)(2,1)} %get-tuple-element.143.turned_ref.refs_1_, bf16[512,1024]{1,0:T(8,128)(2,1)} %bitcast.42, bf16[512,512]{1,0:T(8,128)(2,1)} %get-tuple-element.187.refs_3_.refs_1_, ...), custom_call_target="tpu_custom_call" | custom-call | flops 1000 | bytes 1000 | tf_op jit(solution)/shard_map/weight_grads/pallas_call | solution.py:456
  171.7 11.7 %collective-permute-start.11 = (bf16[512,512]{1,0:T(8,128)(2,1)}, bf16[512,512]{1,0:T(8,128)(2,1)S(1)}, u32[]{:S(2)}, u32[]{:S(2)}) collective-permute-start(bf16[512,512]{1,0:T(8,128)(2,1)} %get-tuple-element.184), channel_id=1, source_target_pairs={{0,1},{1,2},{2,3},{3,0},{4,5},{5,6},{6,7},{7,4},{8,9},{9,10},{10,1... | collective-permute-start | bytes 1572872 | tf_op jit(solution)/shard_map/ppermute | solution.py:617
  185.7 8.9 %sums.2 = (f32[512,1024]{1,0:T(8,128)}, f32[512,1024]{1,0:T(8,128)}) custom-call(s32[2]{0:T(128)} %get-tuple-element.266.refs_0_, bf16[512,512]{1,0:T(8,128)(2,1)} %get-tuple-element.187.refs_3_.refs_1_, bf16[512,512]{1,0:T(8,128)(2,1)} %copy-done.6, bf16[512,512]{1,0:T(8,128)(2,1)} %copy-done.7, bf16[512,512]{1,0:T(8,128)(2,1)} %copy-done.8, ...), custom_call_target="tpu_custom_call" | custom-call | flops 1000 | bytes 1000 | tf_op jit(solution)/shard_map/sums/pallas_call | solution.py:521
  196.0 3.7 add_for_chips.2
  199.7 20.3 %collective-permute-done.12.refs_5_.refs_3_ = bf16[512,512]{1,0:T(8,128)(2,1)S(1)} collective-permute-done((bf16[512,512]{1,0:T(8,128)(2,1)}, bf16[512,512]{1,0:T(8,128)(2,1)S(1)}, u32[]{:S(2)}, u32[]{:S(2)}) %collective-permute-start.12) | collective-permute-done | bytes 524320 | tf_op jit(solution)/shard_map/ppermute | solution.py:617
  220.8 6.8 %weight_grads.3 = (bf16[4,4,128,512]{3,2,1,0:T(8,128)(2,1)}, bf16[4,4,128,512]{3,2,1,0:T(8,128)(2,1)}) custom-call(s32[2]{0:T(128)} %get-tuple-element.266.refs_0_, bf16[1024,512]{1,0:T(8,128)(2,1)} %get-tuple-element.143.turned_ref.refs_1_, bf16[512,1024]{1,0:T(8,128)(2,1)} %bitcast.43, bf16[512,512]{1,0:T(8,128)(2,1)} %get-tuple-element.205.refs_3_.refs_1_, ...), custom_call_target="tpu_custom_call" | custom-call | flops 1000 | bytes 1000 | tf_op jit(solution)/shard_map/weight_grads/pallas_call | solution.py:456
  231.2 10.2 %sums.3 = (bf16[512,1024]{1,0:T(8,128)(2,1)}, f32[512,1024]{1,0:T(8,128)}, f32[1,1024]{1,0:T(1,128)}, f32[1,1024]{1,0:T(1,128)}) custom-call(s32[2]{0:T(128)} %get-tuple-element.266.refs_0_, bf16[512,512]{1,0:T(8,128)(2,1)} %get-tuple-element.205.refs_3_.refs_1_, bf16[512,512]{1,0:T(8,128)(2,1)} %copy-done.4, bf16[512,512]{1,0:T(8,128)(2,1)} %copy-done.5, ...), custom_call_target="tpu_custom_call" | custom-call | flops 1000 | bytes 1000 | tf_op jit(solution)/shard_map/sums/pallas_call | solution.py:521
  244.7 10.0 %collective-permute-done.16 = bf16[4,128,512]{2,1,0:T(8,128)(2,1)S(1)} collective-permute-done((bf16[4,128,512]{2,1,0:T(8,128)(2,1)}, bf16[4,128,512]{2,1,0:T(8,128)(2,1)S(1)}, u32[]{:S(2)}, u32[]{:S(2)}) %collective-permute-start.16) | collective-permute-done | bytes 524320 | tf_op jit(solution)/shard_map/ppermute | solution.py:612
  264.3 10.4 %collective-permute-done.20 = bf16[4,128,512]{2,1,0:T(8,128)(2,1)S(1)} collective-permute-done((bf16[4,128,512]{2,1,0:T(8,128)(2,1)}, bf16[4,128,512]{2,1,0:T(8,128)(2,1)S(1)}, u32[]{:S(2)}, u32[]{:S(2)}) %collective-permute-start.20) | collective-permute-done | bytes 524320 | tf_op jit(solution)/shard_map/ppermute | solution.py:612
  274.7 11.0 %collective-permute-done.21 = bf16[4,128,512]{2,1,0:T(8,128)(2,1)S(1)} collective-permute-done((bf16[4,128,512]{2,1,0:T(8,128)(2,1)}, bf16[4,128,512]{2,1,0:T(8,128)(2,1)S(1)}, u32[]{:S(2)}, u32[]{:S(2)}) %collective-permute-start.21) | collective-permute-done | bytes 524320 | tf_op jit(solution)/shard_map/ppermute | solution.py:612
  288.6 11.4 %collective-permute-start.23 = (bf16[256,512]{1,0:T(8,128)(2,1)S(1)}, bf16[256,512]{1,0:T(8,128)(2,1)S(1)}, u32[]{:S(2)}, u32[]{:S(2)}) collective-permute-start(bf16[256,512]{1,0:T(8,128)(2,1)S(1)} %get-tuple-element.258), channel_id=1, source_target_pairs={{0,1},{1,2},{2,3},{3,0},{4,5},{5,6},{6,7},{7,4},{8,9},{9,10},{10,1... | collective-permute-start | bytes 786440 | tf_op jit(solution)/shard_map/ppermute | solution.py:617
  302.4 5.6 %collective-permute-done.23 = bf16[256,512]{1,0:T(8,128)(2,1)S(1)} collective-permute-done((bf16[256,512]{1,0:T(8,128)(2,1)S(1)}, bf16[256,512]{1,0:T(8,128)(2,1)S(1)}, u32[]{:S(2)}, u32[]{:S(2)}) %collective-permute-start.23) | collective-permute-done | bytes 262176 | tf_op jit(solution)/shard_map/ppermute | solution.py:617
  308.1 8.8 %collective-permute-done.24 = bf16[256,512]{1,0:T(8,128)(2,1)S(1)} collective-permute-done((bf16[256,512]{1,0:T(8,128)(2,1)S(1)}, bf16[256,512]{1,0:T(8,128)(2,1)S(1)}, u32[]{:S(2)}, u32[]{:S(2)}) %collective-permute-start.24) | collective-permute-done | bytes 262176 | tf_op jit(solution)/shard_map/ppermute | solution.py:617
  320.5 11.3 %collective-permute-done.26 = bf16[256,512]{1,0:T(8,128)(2,1)S(1)} collective-permute-done((bf16[256,512]{1,0:T(8,128)(2,1)S(1)}, bf16[256,512]{1,0:T(8,128)(2,1)S(1)}, u32[]{:S(2)}, u32[]{:S(2)}) %collective-permute-start.26) | collective-permute-done | bytes 262176 | tf_op jit(solution)/shard_map/ppermute | solution.py:612
  333.0 8.8 %collective-permute-done.28 = bf16[256,512]{1,0:T(8,128)(2,1)S(1)} collective-permute-done((bf16[256,512]{1,0:T(8,128)(2,1)S(1)}, bf16[256,512]{1,0:T(8,128)(2,1)S(1)}, u32[]{:S(2)}, u32[]{:S(2)}) %collective-permute-start.28) | collective-permute-done | bytes 262176 | tf_op jit(solution)/shard_map/ppermute | solution.py:612
  353.9 3.9 %place_heads.1 = (f32[256,3072]{1,0:T(8,128)}, f32[256,1024]{1,0:T(8,128)}) custom-call(s32[2]{0:T(128)} %pad_add_fusion.3.info_ref, bf16[4,256,512]{2,1,0:T(8,128)(2,1)} %copy-done.3, bf16[4,256,512]{2,1,0:T(8,128)(2,1)} %copy-done.9), custom_call_target="tpu_custom_call" | custom-call | flops 1000 | bytes 1000 | tf_op jit(solution)/shard_map/place_heads/pallas_call | solution.py:598
  357.8 6.1 %place_feed.1 = (f32[256,4096]{1,0:T(8,128)}, f32[1024,1024]{1,0:T(8,128)}) custom-call(bf16[8,512,512]{2,1,0:T(8,128)(2,1)} %bitcast.46), custom_call_target="tpu_custom_call" | custom-call | flops 1000 | bytes 1000 | tf_op jit(solution)/shard_map/place_feed/pallas_call | solution.py:560
  (138 shorter events, 69.3 us)
Async XLA Ops:
  7.2 212.8 %reduce-scatter.7.cloned.1.call-start = ((), (), s32[]{:S(2)}) async-start(), calls=%async_computation.4 | async-start | bytes 10485760
  28.2 48.5 %collective-permute-start = (bf16[512,512]{1,0:T(8,128)(2,1)}, bf16[512,512]{1,0:T(8,128)(2,1)S(1)}, u32[]{:S(2)}, u32[]{:S(2)}) collective-permute-start(bf16[512,512]{1,0:T(8,128)(2,1)} %get-tuple-element.151), channel_id=1, source_target_pairs={{0,1},{1,2},{2,3},{3,0},{4,5},{5,6},{6,7},{7,4},{8,9},{9,10},{10,1... | collective-permute-start | bytes 1572872 | tf_op jit(solution)/shard_map/ppermute | solution.py:617
  31.2 45.5 %collective-permute-start.1 = (bf16[512,512]{1,0:T(8,128)(2,1)}, bf16[512,512]{1,0:T(8,128)(2,1)S(1)}, u32[]{:S(2)}, u32[]{:S(2)}) collective-permute-start(bf16[512,512]{1,0:T(8,128)(2,1)} %get-tuple-element.152), channel_id=1, source_target_pairs={{0,2},{1,3},{2,0},{3,1},{4,6},{5,7},{6,4},{7,5},{8,10},{9,11},{10,... | collective-permute-start | bytes 1572872 | tf_op jit(solution)/shard_map/ppermute | solution.py:617
  33.8 42.9 %collective-permute-start.2 = (bf16[512,512]{1,0:T(8,128)(2,1)}, bf16[512,512]{1,0:T(8,128)(2,1)S(1)}, u32[]{:S(2)}, u32[]{:S(2)}) collective-permute-start(bf16[512,512]{1,0:T(8,128)(2,1)} %get-tuple-element.153), channel_id=1, source_target_pairs={{0,3},{1,0},{2,1},{3,2},{4,7},{5,4},{6,5},{7,6},{8,11},{9,8},{10,9... | collective-permute-start | bytes 1572872 | tf_op jit(solution)/shard_map/ppermute | solution.py:617
  76.8 37.1 %collective-permute-start.6 = (bf16[4,4,256,512]{3,2,1,0:T(8,128)(2,1)}, bf16[4,4,256,512]{3,2,1,0:T(8,128)(2,1)}, u32[]{:S(2)}, u32[]{:S(2)}) collective-permute-start(bf16[4,4,256,512]{3,2,1,0:T(8,128)(2,1)} %get-tuple-element.164), channel_id=1, source_target_pairs={{0,4},{4,0},{8,12},{12,8},{16,20},{20,16},{24,28},{28,24},{1,5},{5... | collective-permute-start | bytes 12582920 | tf_op jit(solution)/shard_map/ppermute | solution.py:612
  76.9 37.1 %collective-permute-start.7 = (bf16[4,4,256,512]{3,2,1,0:T(8,128)(2,1)}, bf16[4,4,256,512]{3,2,1,0:T(8,128)(2,1)}, u32[]{:S(2)}, u32[]{:S(2)}) collective-permute-start(bf16[4,4,256,512]{3,2,1,0:T(8,128)(2,1)} %get-tuple-element.165), channel_id=1, source_target_pairs={{0,4},{4,0},{8,12},{12,8},{16,20},{20,16},{24,28},{28,24},{1,5},{5... | collective-permute-start | bytes 12582920 | tf_op jit(solution)/shard_map/ppermute | solution.py:612
  77.4 46.1 %collective-permute-start.3 = (bf16[512,512]{1,0:T(8,128)(2,1)}, bf16[512,512]{1,0:T(8,128)(2,1)S(1)}, u32[]{:S(2)}, u32[]{:S(2)}) collective-permute-start(bf16[512,512]{1,0:T(8,128)(2,1)} %get-tuple-element.154), channel_id=1, source_target_pairs={{0,1},{1,2},{2,3},{3,0},{4,5},{5,6},{6,7},{7,4},{8,9},{9,10},{10,1... | collective-permute-start | bytes 1572872 | tf_op jit(solution)/shard_map/ppermute | solution.py:617
  80.2 43.2 %collective-permute-start.4 = (bf16[512,512]{1,0:T(8,128)(2,1)}, bf16[512,512]{1,0:T(8,128)(2,1)S(1)}, u32[]{:S(2)}, u32[]{:S(2)}) collective-permute-start(bf16[512,512]{1,0:T(8,128)(2,1)} %get-tuple-element.155), channel_id=1, source_target_pairs={{0,2},{1,3},{2,0},{3,1},{4,6},{5,7},{6,4},{7,5},{8,10},{9,11},{10,... | collective-permute-start | bytes 1572872 | tf_op jit(solution)/shard_map/ppermute | solution.py:617
  81.9 41.6 %collective-permute-start.5 = (bf16[512,512]{1,0:T(8,128)(2,1)}, bf16[512,512]{1,0:T(8,128)(2,1)}, u32[]{:S(2)}, u32[]{:S(2)}) collective-permute-start(bf16[512,512]{1,0:T(8,128)(2,1)} %get-tuple-element.156), channel_id=1, source_target_pairs={{0,3},{1,0},{2,1},{3,2},{4,7},{5,4},{6,5},{7,6},{8,11},{9,8},{10,9... | collective-permute-start | bytes 1572872 | tf_op jit(solution)/shard_map/ppermute | solution.py:617
  124.4 161.3 %reduce-scatter.5.cloned.1.call-start = ((), (), s32[]{:S(2)}) async-start(), calls=%async_computation.2 | async-start | bytes 2621440 | tf_op jit(solution)/shard_map/reduce_scatter | solution.py:788
  124.4 37.2 %collective-permute-start.8 = (bf16[512,512]{1,0:T(8,128)(2,1)}, bf16[512,512]{1,0:T(8,128)(2,1)S(1)}, u32[]{:S(2)}, u32[]{:S(2)}) collective-permute-start(bf16[512,512]{1,0:T(8,128)(2,1)} %get-tuple-element.175), channel_id=1, source_target_pairs={{0,1},{1,2},{2,3},{3,0},{4,5},{5,6},{6,7},{7,4},{8,9},{9,10},{10,1... | collective-permute-start | bytes 1572872 | tf_op jit(solution)/shard_map/ppermute | solution.py:617
  128.3 35.5 %collective-permute-start.9 = (bf16[512,512]{1,0:T(8,128)(2,1)}, bf16[512,512]{1,0:T(8,128)(2,1)S(1)}, u32[]{:S(2)}, u32[]{:S(2)}) collective-permute-start(bf16[512,512]{1,0:T(8,128)(2,1)} %get-tuple-element.176), channel_id=1, source_target_pairs={{0,2},{1,3},{2,0},{3,1},{4,6},{5,7},{6,4},{7,5},{8,10},{9,11},{10,... | collective-permute-start | bytes 1572872 | tf_op jit(solution)/shard_map/ppermute | solution.py:617
  130.0 33.8 %collective-permute-start.10 = (bf16[512,512]{1,0:T(8,128)(2,1)}, bf16[512,512]{1,0:T(8,128)(2,1)S(1)}, u32[]{:S(2)}, u32[]{:S(2)}) collective-permute-start(bf16[512,512]{1,0:T(8,128)(2,1)} %get-tuple-element.177), channel_id=1, source_target_pairs={{0,3},{1,0},{2,1},{3,2},{4,7},{5,4},{6,5},{7,6},{8,11},{9,8},{10,9... | collective-permute-start | bytes 1572872 | tf_op jit(solution)/shard_map/ppermute | solution.py:617
  171.7 23.0 %collective-permute-start.14 = (bf16[4,4,128,512]{3,2,1,0:T(8,128)(2,1)}, bf16[4,4,128,512]{3,2,1,0:T(8,128)(2,1)S(1)}, u32[]{:S(2)}, u32[]{:S(2)}) collective-permute-start(bf16[4,4,128,512]{3,2,1,0:T(8,128)(2,1)} %get-tuple-element.193), channel_id=1, source_target_pairs={{0,4},{4,0},{8,12},{12,8},{16,20},{20,16},{24,28},{28,24},{1,5},{5... | collective-permute-start | bytes 6291464 | tf_op jit(solution)/shard_map/ppermute | solution.py:612
  171.7 28.0 %collective-permute-start.11 = (bf16[512,512]{1,0:T(8,128)(2,1)}, bf16[512,512]{1,0:T(8,128)(2,1)S(1)}, u32[]{:S(2)}, u32[]{:S(2)}) collective-permute-start(bf16[512,512]{1,0:T(8,128)(2,1)} %get-tuple-element.184), channel_id=1, source_target_pairs={{0,1},{1,2},{2,3},{3,0},{4,5},{5,6},{6,7},{7,4},{8,9},{9,10},{10,1... | collective-permute-start | bytes 1572872 | tf_op jit(solution)/shard_map/ppermute | solution.py:617
  183.4 36.6 %collective-permute-start.12 = (bf16[512,512]{1,0:T(8,128)(2,1)}, bf16[512,512]{1,0:T(8,128)(2,1)S(1)}, u32[]{:S(2)}, u32[]{:S(2)}) collective-permute-start(bf16[512,512]{1,0:T(8,128)(2,1)} %get-tuple-element.185), channel_id=1, source_target_pairs={{0,2},{1,3},{2,0},{3,1},{4,6},{5,7},{6,4},{7,5},{8,10},{9,11},{10,... | collective-permute-start | bytes 1572872 | tf_op jit(solution)/shard_map/ppermute | solution.py:617
  185.1 34.8 %collective-permute-start.13 = (bf16[512,512]{1,0:T(8,128)(2,1)}, bf16[512,512]{1,0:T(8,128)(2,1)}, u32[]{:S(2)}, u32[]{:S(2)}) collective-permute-start(bf16[512,512]{1,0:T(8,128)(2,1)} %get-tuple-element.186), channel_id=1, source_target_pairs={{0,3},{1,0},{2,1},{3,2},{4,7},{5,4},{6,5},{7,6},{8,11},{9,8},{10,9... | collective-permute-start | bytes 1572872 | tf_op jit(solution)/shard_map/ppermute | solution.py:617
  220.0 137.8 %all-gather.3.cloned.1.call-start = ((), (), s32[]{:S(2)}) async-start(), calls=%async_computation.3 | async-start | bytes 4718592 | tf_op jit(solution)/shard_map/all_gather | solution.py:820
  227.6 27.1 %collective-permute-start.18 = (bf16[4,4,128,512]{3,2,1,0:T(8,128)(2,1)}, bf16[4,4,128,512]{3,2,1,0:T(8,128)(2,1)S(1)}, u32[]{:S(2)}, u32[]{:S(2)}) collective-permute-start(bf16[4,4,128,512]{3,2,1,0:T(8,128)(2,1)} %get-tuple-element.217), channel_id=1, source_target_pairs={{0,4},{4,0},{8,12},{12,8},{16,20},{20,16},{24,28},{28,24},{1,5},{5... | collective-permute-start | bytes 6291464 | tf_op jit(solution)/shard_map/ppermute | solution.py:612
  229.2 25.5 %collective-permute-start.16 = (bf16[4,128,512]{2,1,0:T(8,128)(2,1)}, bf16[4,128,512]{2,1,0:T(8,128)(2,1)S(1)}, u32[]{:S(2)}, u32[]{:S(2)}) collective-permute-start(bf16[4,128,512]{2,1,0:T(8,128)(2,1)} %get-tuple-element.215), channel_id=1, source_target_pairs={{0,16},{4,20},{8,24},{12,28},{16,0},{20,4},{24,8},{28,12},{1,17},{... | collective-permute-start | bytes 1572872 | tf_op jit(solution)/shard_map/ppermute | solution.py:612
  230.7 24.0 %collective-permute-start.17 = (bf16[4,128,512]{2,1,0:T(8,128)(2,1)}, bf16[4,128,512]{2,1,0:T(8,128)(2,1)}, u32[]{:S(2)}, u32[]{:S(2)}) collective-permute-start(bf16[4,128,512]{2,1,0:T(8,128)(2,1)} %get-tuple-element.216), channel_id=1, source_target_pairs={{0,24},{4,28},{8,16},{12,20},{16,8},{20,12},{24,0},{28,4},{1,25},{... | collective-permute-start | bytes 1572872 | tf_op jit(solution)/shard_map/ppermute | solution.py:612
  261.0 24.7 %collective-permute-start.21 = (bf16[4,128,512]{2,1,0:T(8,128)(2,1)}, bf16[4,128,512]{2,1,0:T(8,128)(2,1)S(1)}, u32[]{:S(2)}, u32[]{:S(2)}) collective-permute-start(bf16[4,128,512]{2,1,0:T(8,128)(2,1)} %get-tuple-element.226), channel_id=1, source_target_pairs={{0,16},{4,20},{8,24},{12,28},{16,0},{20,4},{24,8},{28,12},{1,17},{... | collective-permute-start | bytes 1572872 | tf_op jit(solution)/shard_map/ppermute | solution.py:612
  261.7 24.0 %collective-permute-start.22 = (bf16[4,128,512]{2,1,0:T(8,128)(2,1)}, bf16[4,128,512]{2,1,0:T(8,128)(2,1)S(1)}, u32[]{:S(2)}, u32[]{:S(2)}) collective-permute-start(bf16[4,128,512]{2,1,0:T(8,128)(2,1)} %get-tuple-element.227), channel_id=1, source_target_pairs={{0,24},{4,28},{8,16},{12,20},{16,8},{20,12},{24,0},{28,4},{1,25},{... | collective-permute-start | bytes 1572872 | tf_op jit(solution)/shard_map/ppermute | solution.py:612
  319.4 22.4 %collective-permute-start.28 = (bf16[256,512]{1,0:T(8,128)(2,1)S(1)}, bf16[256,512]{1,0:T(8,128)(2,1)S(1)}, u32[]{:S(2)}, u32[]{:S(2)}) collective-permute-start(bf16[256,512]{1,0:T(8,128)(2,1)S(1)} %fusion.2), channel_id=1, source_target_pairs={{0,24},{4,28},{8,16},{12,20},{16,8},{20,12},{24,0},{28,4},{1,25},{... | collective-permute-start | bytes 786440 | tf_op jit(solution)/shard_map/ppermute | solution.py:612
  (32 other events, 316.1 us)
Sparse Core Ops, SparseCore 0:
  123.6 89.2 reduce-scatter.6
  220.1 53.6 reduce-scatter.4
  285.8 55.3 all-gather.2

commit v4 on v3

--- a/solution.py
+++ b/solution.py
@@ -130,7 +130,7 @@
     wide = width // owners
     chunks = wide // PAIR
     fixed = pl.BlockSpec((rows, width), lambda i, o: (0, 0))
-    table = pl.BlockSpec((rows, PAIR), lambda i, o: (0, 0))
+    table = pl.BlockSpec((rows, PAIR), lambda i, o: (o[0], 0))
 
     def columns(part):
         return pl.BlockSpec((width, wide), lambda i, o: (0, part * owners + o[i]))
@@ -498,8 +498,11 @@
         - jnp.mean(gained, axis=-1, keepdims=True)
         - hat * jnp.mean(gained * hat, axis=-1, keepdims=True)
     )
-    gain_grad[...] = jnp.sum(norm * hat, axis=0, keepdims=True)
-    bias_grad[...] = jnp.sum(norm, axis=0, keepdims=True)
+    for out_ref, rows in ((gain_grad, norm * hat), (bias_grad, norm)):
+        row = jnp.sum(rows, axis=0, keepdims=True)
+        wide = out_ref.shape[1]
+        for owner in range(owners):
+            out_ref[owner : owner + 1, :] = row[:, owner * wide : (owner + 1) * wide]
 
 
 def sums_of(info, chunk, chunks, parts, qkv_weight, out_weight, sums, final=()):
@@ -516,7 +519,7 @@
         return pl.BlockSpec((PAIR, width), lambda i: (owner * chunks + chunk, 0))
 
     full = jax.ShapeDtypeStruct((rows, width), F32)
-    row = jax.ShapeDtypeStruct((1, width), F32)
+    row = jax.ShapeDtypeStruct((owners, width // owners), F32)
     shapes = [jax.ShapeDtypeStruct((rows, width), BF16), full, row, row] if last else [full, full]
     return pl.pallas_call(
         lambda *refs: sums_kernel(last, owners, *refs),
@@ -535,38 +538,38 @@
     )(info, *parts, *([qkv_weight] * (3 * owners)), *([out_weight] * owners), *sums, *final)
 
 
-def feed_place_kernel(sums_ref, in_ref, down_ref):
-    devices, total, tile = sums_ref.shape
-    kept = 2 * in_ref.shape[0] // devices
+def feed_place_kernel(info_ref, mine_ref, other_ref, in_ref, down_ref):
+    masks, total, tile = mine_ref.shape
+    kept = in_ref.shape[0] // masks
     tiles = in_ref.shape[1] // (2 * tile)
-    rows = down_ref.shape[0] // 2
-    down_kept = 2 * rows // devices
-    for device in range(devices):
-        core, chip = device & 1, device >> 1
-        rows_of = slice(chip * kept, (chip + 1) * kept)
-        for number in range(tiles):
-            column = (2 * number + core) * tile
-            in_ref[rows_of, column : column + tile] = sums_ref[device, number * kept : (number + 1) * kept].astype(F32)
-        start = core * rows + chip * down_kept
-        for group in range(down_ref.shape[1] // tile):
-            at = tiles * kept + group * down_kept
-            down_ref[start : start + down_kept, group * tile : (group + 1) * tile] = sums_ref[
-                device, at : at + down_kept
-            ].astype(F32)
-
-
-def place_feed(sums, in_shape, down_shape):
+    half = down_ref.shape[0] // 2
+    down_kept = half // masks
+    for source, ref in enumerate((mine_ref, other_ref)):
+        core = info_ref[0] ^ source
+        for mask in range(masks):
+            chip = info_ref[1] ^ mask
+            rows = pl.ds(pl.multiple_of(chip * kept, kept), kept)
+            for number in range(tiles):
+                columns = pl.ds(pl.multiple_of((2 * number + core) * tile, tile), tile)
+                in_ref[rows, columns] = ref[mask, number * kept : (number + 1) * kept].astype(F32)
+            rows = pl.ds(pl.multiple_of(core * half + chip * down_kept, down_kept), down_kept)
+            for group in range(down_ref.shape[1] // tile):
+                at = tiles * kept + group * down_kept
+                down_ref[rows, group * tile : (group + 1) * tile] = ref[mask, at : at + down_kept].astype(F32)
+
+
+def place_feed(info, mine, other, in_shape, down_shape):
     shapes = [jax.ShapeDtypeStruct(in_shape, F32), jax.ShapeDtypeStruct(down_shape, F32)]
     return pl.pallas_call(
         feed_place_kernel,
         grid=(1,),
-        in_specs=[whole(sums)],
+        in_specs=[SCALARS, whole(mine), whole(other)],
         out_specs=[whole(shape) for shape in shapes],
         out_shape=shapes,
         compiler_params=pltpu.CompilerParams(vmem_limit_bytes=60 * MIB),
         cost_estimate=SHORT,
         name="place_feed",
-    )(sums)
+    )(info, mine, other)
 
 
 def heads_place_kernel(info_ref, mine_ref, other_ref, qkv_ref, out_ref):
@@ -732,8 +735,6 @@
         hidden.reshape(rows, width), marked, token_table, norm_gain[None], norm_bias[None]
     )
     cosine, sine = (jnp.asarray(table) for table in trig_tables(length))
-    own_cosine = lax.dynamic_slice_in_dim(cosine, me * rows, rows)
-    own_sine = lax.dynamic_slice_in_dim(sine, me * rows, rows)
     place = lax.axis_index("batch")
     info = jnp.stack([me, core]).astype(jnp.int32)
     spots = jnp.stack([me, end]).astype(jnp.int32)
@@ -749,7 +750,7 @@
         return [exchange(rows, "batch", mask) for mask in (2, 4, 6)]
 
     shifts = lax.rem(me + jnp.arange(owners, dtype=jnp.int32), owners)
-    heads = order.done(heads_of(shifts, normed, cot, qkv_weight, out_weight, own_cosine, own_sine))
+    heads = order.done(heads_of(shifts, normed, cot, qkv_weight, out_weight, cosine, sine))
 
     arrived = moved(order(heads[0]))
     cells = 2 * jnp.arange(owners, dtype=jnp.int32)
@@ -775,19 +776,18 @@
     cot_sum = order.done(jnp.sum(order(cot).astype(F32), axis=0))
     order.also(arrived)
 
+    later = moved(order(second))
     parts = gathered(first, order(arrived))
-    first_kept, first_sent = order.done(weight_grads(info, turned, cot, parts, pieces // 2))
-
+    sums = order.done(sums_of(info, 0, chunks, order(parts), qkv_weight, out_weight, (out_sum, norm_sum)))
+    first_kept, first_sent = order.done(weight_grads(info, turned, cot, order(parts), pieces // 2))
+    order.also(later, feed_rows)
+
+    feed_rows = lax.psum_scatter(order(feed_rows), "seq", scatter_dimension=0, tiled=False)
     grad_arrived = exchange(order(first_sent), "batch", 1)
-    later = moved(order(second))
-    sums = order.done(sums_of(info, 0, chunks, order(parts), qkv_weight, out_weight, (out_sum, norm_sum)))
+    parts = gathered(second, order(later))
+    second_kept, second_sent = order.done(weight_grads(info, turned, cot, parts, pieces // 2))
     order.also(grad_arrived)
     first_held = order.done(add_for_chips(place >> 1, [order(first_kept)], [grad_arrived]))
-    order.also(later, feed_rows)
-
-    feed_rows = lax.psum_scatter(order(feed_rows), "seq", scatter_dimension=0, tiled=False)
-    parts = gathered(second, order(later))
-    second_kept, second_sent = order.done(weight_grads(info, turned, cot, parts, pieces // 2))
 
     first_arrived = [exchange(order(first_held[mask]), "batch", 2 * mask) for mask in (1, 2, 3)]
     grad_arrived = exchange(order(second_sent), "batch", 1)
@@ -798,27 +798,28 @@
     )
     order.also(first_arrived, grad_arrived)
     second_held = order.done(add_for_chips(place >> 1, [order(second_kept)], [grad_arrived]))
+
+    def halve_seq(rows, number):
+        bit = (me >> number) & 1
+        split = rows.reshape((rows.shape[0] // 2, 2) + rows.shape[1:])
+        return picked(split, bit, 1), exchange(picked(split, 1 - bit, 1), "seq", 1 << number)
+
+    second_arrived = [exchange(order(second_held[mask]), "batch", 2 * mask) for mask in (1, 2, 3)]
+    in_bias_grad = order(in_bias_grad)
     bias_low = jnp.where(core == 0, in_bias_grad[owners:], in_bias_grad[:owners])
     bias_high = jnp.where(core == 0, in_bias_grad[:owners], in_bias_grad[owners:])
-    small = jnp.concatenate(
-        [
-            jnp.concatenate([bias_low, bias_high], axis=1).reshape(owners, -1),
-            cot_sum.reshape(owners, -1),
-            gain_grad.reshape(owners, -1),
-            bias_grad.reshape(owners, -1),
-        ],
-        axis=1,
-    )
-    order.done((second_held, order(small)))
-
-    def send_owners(rows):
-        return [around(picked(rows, lax.rem(me + shift, owners)), shift) for shift in range(1, owners)]
-
-    second_arrived = [exchange(order(second_held[mask]), "batch", 2 * mask) for mask in (1, 2, 3)]
-    small_arrived = exchange(order(small), "batch", 1)
-    order.also(second_arrived, small_arrived, feed_rows)
-    feed_total = lax.all_gather(order(feed_rows), "batch", axis=0)
-    small = small + order(small_arrived)
+    small = order.done(
+        jnp.concatenate(
+            [
+                jnp.concatenate([bias_low, bias_high], axis=1).reshape(owners, -1),
+                cot_sum.reshape(owners, -1),
+                gain_grad,
+                bias_grad,
+            ],
+            axis=1,
+        )
+    )
+    order.also(second_arrived, feed_rows)
     grad_rows = order.done(
         jnp.concatenate(
             [
@@ -828,30 +829,43 @@
             axis=1,
         )
     )
-    order.also(small)
-
-    grad_rows = order(grad_rows)
-    grad_arrived = send_owners(grad_rows)
-    order.also(grad_arrived)
-    grad_rows = order.done(total_of(picked(grad_rows, me), *order(grad_arrived)))
+
+    feed_rows = order(feed_rows)
+    feed_back = [exchange(feed_rows, "batch", mask) for mask in (2, 4)]
+    small_arrived = exchange(order(small), "batch", 1)
+    grad_rows, grad_arrived = halve_seq(order(grad_rows), 0)
+    order.also(feed_back, grad_arrived, small_arrived)
+    small = small + order(small_arrived)
+    grad_rows = total_of(order(grad_rows), grad_arrived)
+    order.done((grad_rows, small))
+
+    feed_back.append(exchange(order(feed_rows), "batch", 6))
+    small_arrived = back(order(small))
+    grad_rows, grad_arrived = halve_seq(order(grad_rows), 1)
+    order.also(feed_back, grad_arrived, small_arrived)
+    grad_rows = total_of(order(grad_rows), grad_arrived)[0]
+    small = sum(order(small_arrived), small)
+    feed_mine = jnp.stack([feed_rows] + order(feed_back))
+    order.done((grad_rows, feed_mine, small))
 
     grad_back = back(order(grad_rows))
+    feed_other = exchange(order(feed_mine), "batch", 1)
+    place_info = jnp.stack([core, place >> 1]).astype(jnp.int32)
+    in_weight_grad, down_weight_grad = order.done(
+        place_feed(
+            place_info,
+            order(feed_mine),
+            feed_other,
+            (own_rows, in_weight.shape[1]),
+            (down_weight.shape[0] // owners, width),
+        )
+    )
     order.also(grad_back)
     grad_mine = order.done(jnp.stack([grad_rows] + order(grad_back)))
 
     grad_other = exchange(order(grad_mine), "batch", 1)
-    small_arrived = back(order(small))
-    order.also(small_arrived, grad_other)
-    small = order.done(sum(order(small_arrived), small))
-
     small_arrived = [around(order(small), shift) for shift in range(1, owners)]
-    heads_info = jnp.stack([core, place >> 1]).astype(jnp.int32)
-    qkv_weight_grad, out_weight_grad = order.done(
-        place_heads(heads_info, order(grad_mine), grad_other, own_rows, width)
-    )
-    in_weight_grad, down_weight_grad = order.done(
-        place_feed(order(feed_total), (own_rows, in_weight.shape[1]), (down_weight.shape[0] // owners, width))
-    )
+    qkv_weight_grad, out_weight_grad = place_heads(place_info, order(grad_mine), grad_other, own_rows, width)
     small = picked(sum(order(small_arrived), small), me)
     few = own_rows
     many = in_bias.shape[0] // owners

time: 372 us -> 361 us (0.970)
  waiting for transfers between devices: 93 us -> 81.5 us
  starting transfers between devices: 67.1 us -> 71 us
    ppermute x18 -> x24, starting transfers between devices: 14.8 us -> 32.4 us  [exchange(): lax.ppermute(rows, axis, [(place, place ^ mask) for place in range(size)])]
    ppermute x18 -> x15, waiting for transfers between devices: 36.9 us -> 21.7 us  [around(): lax.ppermute(rows, 'seq', [(place, (place + shift) % owners) for place in...]
    ppermute x18 -> x15, starting transfers between devices: 52 us -> 38.6 us  [around(): lax.ppermute(rows, 'seq', [(place, (place + shift) % owners) for place in...]
    reduce_scatter x1, waiting for transfers between devices: 0.01 us -> 5.94 us  [fast_body(): lax.psum_scatter(order(feed_rows), 'seq', scatter_dimension=0, tiled=False)]
    ppermute x18 -> x24, waiting for transfers between devices: 56 us -> 52.6 us  [exchange(): lax.ppermute(rows, axis, [(place, place ^ mask) for place in range(size)])]
  transfers between devices with their start and end apart: 39 -> 41, of which waited for: 14 -> 19; matrix products, arithmetic and copies ran while one was open for 2% -> 1% of each run, Pallas kernels for 44% -> 44%
where the time goes in v4:
time: 361 us
  Pallas kernels  178 us (49%)
  waiting for transfers between devices  81.5 us (23%)
  starting transfers between devices  71 us (20%)
  between operations  15.7 us (4%)
  other arithmetic  8.02 us (2%)
  local copies, waits for them, and re-layouts  6.91 us (2%)
    pallas_call x2, Pallas kernels, attention(): pl.pallas_call(lambda *refs: attention_kernel(pieces, *refs), grid=(1,),...  61.8 us
    ppermute x24, waiting for transfers between devices, exchange(): lax.ppermute(rows, axis, [(place, place ^ mask) for place in range(size)])  52.6 us
    pallas_call x1, Pallas kernels, feed_forward(): pl.pallas_call(feed_kernel, grid_spec=pltpu.PrefetchScalarGridSpec(num_sc...  40.9 us
    ppermute x15, starting transfers between devices, around(): lax.ppermute(rows, 'seq', [(place, (place + shift) % owners) for place in...  38.6 us
    ppermute x24, starting transfers between devices, exchange(): lax.ppermute(rows, axis, [(place, place ^ mask) for place in range(size)])  32.4 us
    ppermute x15, waiting for transfers between devices, around(): lax.ppermute(rows, 'seq', [(place, (place + shift) % owners) for place in...  21.7 us
    pallas_call x2, Pallas kernels, sums_of(): pl.pallas_call(lambda *refs: sums_kernel(last, owners, *refs), grid=(1,),...  18.3 us
    pallas_call x2, Pallas kernels, weight_grads(): pl.pallas_call(lambda *refs: weight_kernel(pieces, *refs), grid=(1,), in_...  14 us
  transfers between devices with their start and end apart: 41, of which 19 were waited for; matrix products, arithmetic and copies ran while one was open for 1% of the time, Pallas kernels for 44%

profile of v4, /device:TPU:0, one launch (start us, length us, event | category | flops | bytes accessed | tf_op | source)
XLA Modules:
  0.0 360.7 jit_solution(17552350217539852487)
XLA Ops:
  10.7 4.6 %prep.1 = (f32[512,1024]{1,0:T(8,128)}, bf16[512,1024]{1,0:T(8,128)(2,1)}, bf16[1024,512]{1,0:T(8,128)(2,1)}) custom-call(bf16[512,1024]{1,0:T(8,128)(2,1)} %bitcast.51, s32[512,1]{1,0:T(8,128)} %select_select_fusion.mark_ref, bf16[32,1024]{1,0:T(8,128)(2,1)} %table_ref.1, f32[1,1024]{1,0:T(1,128)} %bitcast.65, f32[1,1024]{1,0:T(1,128)} %bitcast.67), custom_call_target="tpu_custom_call" | custom-call | flops 1000 | bytes 1000 | tf_op jit(solution)/shard_map/prep/pallas_call | solution.py:77
  15.2 11.2 %heads.1 = (bf16[512,512]{1,0:T(8,128)(2,1)}, bf16[512,512]{1,0:T(8,128)(2,1)}, bf16[512,512]{1,0:T(8,128)(2,1)}, bf16[512,512]{1,0:T(8,128)(2,1)}, bf16[512,512...) custom-call(s32[4]{0:T(128)} %compare_select_fusion.owners_ref, ...), custom_call_target="tpu_custom_call" | custom-call | flops 1000 | bytes 1000 | tf_op jit(solution)/shard_map/heads/pallas_call | solution.py:138
  34.0 40.9 %feed.1 = (bf16[4,4,256,512]{3,2,1,0:T(8,128)(2,1)}, bf16[4,4,256,512]{3,2,1,0:T(8,128)(2,1)}, bf16[4,4,256,512]{3,2,1,0:T(8,128)(2,1)}, bf16[4,4,256,512]{3,2,1...) custom-call(s32[8]{0:T(128)} %pad_add_fusion.2.cells_ref, ...), custom_call_target="tpu_custom_call" | custom-call | flops 1000 | bytes 1000 | tf_op jit(solution)/shard_map/feed/pallas_call | solution.py:390
  81.4 30.6 %attention.2 = (bf16[512,512]{1,0:T(8,128)(2,1)}, bf16[512,512]{1,0:T(8,128)(2,1)}, bf16[512,512]{1,0:T(8,128)(2,1)}, bf16[512,512]{1,0:T(8,128)(2,1)}) custom-call(s32[2]{0:T(128)} %get-tuple-element.282.refs_0_, bf16[512,512]{1,0:T(8,128)(2,1)} %get-tuple-element.145.refs_1_, bf16[512,512]{1,0:T(8,128)(2,1)} %copy-done.12, bf16[512,512]{1,0:T(8,128)(2,1)} %copy-done.14, ...), custom_call_target="tpu_custom_call" | custom-call | flops 1000 | bytes 1000 | tf_op jit(solution)/shard_map/attention/pallas_call | solution.py:294
  112.1 9.5 %add_pieces.1 = bf16[4,4,512,512]{3,2,1,0:T(8,128)(2,1)} custom-call(bf16[4,4,256,512]{3,2,1,0:T(8,128)(2,1)} %get-tuple-element.173.refs_0_, bf16[4,4,256,512]{3,2,1,0:T(8,128)(2,1)} %collective-permute-done.6.refs_1_, bf16[4,4,256,512]{3,2,1,0:T(8,128)(2,1)} %get-tuple-element.174.refs_2_, bf16[4,4,256,512]{3,2,1,0:T(8,128)(2,1)} %collective-permute-done.7.refs_3_), custom_call_target="tpu_custom_call" | custom-call | flops 1000 | bytes 1000 | tf_op jit(solution)/shard_map/add_pieces/pallas_call | solution.py:647
  122.7 4.3 %collective-permute-start.8 = (bf16[512,512]{1,0:T(8,128)(2,1)}, bf16[512,512]{1,0:T(8,128)(2,1)S(1)}, u32[]{:S(2)}, u32[]{:S(2)}) collective-permute-start(bf16[512,512]{1,0:T(8,128)(2,1)} %get-tuple-element.183), channel_id=1, source_target_pairs={{0,1},{1,2},{2,3},{3,0},{4,5},{5,6},{6,7},{7,4},{8,9},{9,10},{10,1... | collective-permute-start | bytes 1572872 | tf_op jit(solution)/shard_map/ppermute | solution.py:620
  129.4 31.2 %attention.3 = (bf16[512,512]{1,0:T(8,128)(2,1)}, bf16[512,512]{1,0:T(8,128)(2,1)}, bf16[512,512]{1,0:T(8,128)(2,1)}, bf16[512,512]{1,0:T(8,128)(2,1)}) custom-call(s32[2]{0:T(128)} %get-tuple-element.282.refs_0_, bf16[512,512]{1,0:T(8,128)(2,1)} %get-tuple-element.141.refs_1_, bf16[512,512]{1,0:T(8,128)(2,1)} %copy-done.13, bf16[512,512]{1,0:T(8,128)(2,1)} %copy-done.15, ...), custom_call_target="tpu_custom_call" | custom-call | flops 1000 | bytes 1000 | tf_op jit(solution)/shard_map/attention/pallas_call | solution.py:294
  162.2 11.7 %collective-permute-start.11 = (bf16[512,512]{1,0:T(8,128)(2,1)}, bf16[512,512]{1,0:T(8,128)(2,1)S(1)}, u32[]{:S(2)}, u32[]{:S(2)}) collective-permute-start(bf16[512,512]{1,0:T(8,128)(2,1)} %get-tuple-element.186), channel_id=1, source_target_pairs={{0,1},{1,2},{2,3},{3,0},{4,5},{5,6},{6,7},{7,4},{8,9},{9,10},{10,1... | collective-permute-start | bytes 1572872 | tf_op jit(solution)/shard_map/ppermute | solution.py:620
  176.3 8.4 %sums.2 = (f32[512,1024]{1,0:T(8,128)}, f32[512,1024]{1,0:T(8,128)}) custom-call(s32[2]{0:T(128)} %get-tuple-element.281.refs_0_, bf16[512,512]{1,0:T(8,128)(2,1)} %get-tuple-element.198.refs_1_.refs_3_, bf16[512,512]{1,0:T(8,128)(2,1)} %copy-done.7, bf16[512,512]{1,0:T(8,128)(2,1)} %copy-done.8, bf16[512,512]{1,0:T(8,128)(2,1)} %copy-done.9, ...), custom_call_target="tpu_custom_call" | custom-call | flops 1000 | bytes 1000 | tf_op jit(solution)/shard_map/sums/pallas_call | solution.py:524
  184.7 7.2 %weight_grads.2 = (bf16[4,4,128,512]{3,2,1,0:T(8,128)(2,1)}, bf16[4,4,128,512]{3,2,1,0:T(8,128)(2,1)}) custom-call(s32[2]{0:T(128)} %get-tuple-element.281.refs_0_, bf16[1024,512]{1,0:T(8,128)(2,1)} %get-tuple-element.150.turned_ref.refs_1_, bf16[512,1024]{1,0:T(8,128)(2,1)} %bitcast.45, bf16[512,512]{1,0:T(8,128)(2,1)} %get-tuple-element.198.refs_1_.refs_3_, ...), custom_call_target="tpu_custom_call" | custom-call | flops 1000 | bytes 1000 | tf_op jit(solution)/shard_map/weight_grads/pallas_call | solution.py:456
  191.9 17.9 %collective-permute-done.12.refs_5_.refs_3_ = bf16[512,512]{1,0:T(8,128)(2,1)S(1)} collective-permute-done((bf16[512,512]{1,0:T(8,128)(2,1)}, bf16[512,512]{1,0:T(8,128)(2,1)S(1)}, u32[]{:S(2)}, u32[]{:S(2)}) %collective-permute-start.12) | collective-permute-done | bytes 524320 | tf_op jit(solution)/shard_map/ppermute | solution.py:620
  211.1 6.8 %weight_grads.3 = (bf16[4,4,128,512]{3,2,1,0:T(8,128)(2,1)}, bf16[4,4,128,512]{3,2,1,0:T(8,128)(2,1)}) custom-call(s32[2]{0:T(128)} %get-tuple-element.281.refs_0_, bf16[1024,512]{1,0:T(8,128)(2,1)} %get-tuple-element.150.turned_ref.refs_1_, bf16[512,1024]{1,0:T(8,128)(2,1)} %bitcast.46, bf16[512,512]{1,0:T(8,128)(2,1)} %get-tuple-element.216.refs_3_.refs_1_, ...), custom_call_target="tpu_custom_call" | custom-call | flops 1000 | bytes 1000 | tf_op jit(solution)/shard_map/weight_grads/pallas_call | solution.py:456
  226.9 9.8 %sums.3 = (bf16[512,1024]{1,0:T(8,128)(2,1)}, f32[512,1024]{1,0:T(8,128)}, f32[4,256]{1,0:T(4,128)}, f32[4,256]{1,0:T(4,128)}) custom-call(s32[2]{0:T(128)} %get-tuple-element.281.refs_0_, bf16[512,512]{1,0:T(8,128)(2,1)} %get-tuple-element.216.refs_3_.refs_1_, bf16[512,512]{1,0:T(8,128)(2,1)} %copy-done.5, bf16[512,512]{1,0:T(8,128)(2,1)} %copy-done.6, ...), custom_call_target="tpu_custom_call" | custom-call | flops 1000 | bytes 1000 | tf_op jit(solution)/shard_map/sums/pallas_call | solution.py:524
  238.4 11.4 %collective-permute-done.16 = bf16[4,128,512]{2,1,0:T(8,128)(2,1)S(1)} collective-permute-done((bf16[4,128,512]{2,1,0:T(8,128)(2,1)}, bf16[4,128,512]{2,1,0:T(8,128)(2,1)S(1)}, u32[]{:S(2)}, u32[]{:S(2)}) %collective-permute-start.16) | collective-permute-done | bytes 524320 | tf_op jit(solution)/shard_map/ppermute | solution.py:615
  251.1 3.6 %add_for_chips.3 = (bf16[4,128,512]{2,1,0:T(8,128)(2,1)}, bf16[4,128,512]{2,1,0:T(8,128)(2,1)}, bf16[4,128,512]{2,1,0:T(8,128)(2,1)}, bf16[4,128,512]{2,1,0:T(8,128)(2,1)}) custom-call(s32[1]{0:T(128)} %bitcast.12.refs_0_, bf16[4,4,128,512]{3,2,1,0:T(8,128)(2,1)} %get-tuple-element.229.refs_1_.refs_3_.refs_5_.refs_7_, bf16[4,4,128,512]{3,2,1,0:T(8,128)(2,1)} %copy-done.1, ...), custom_call_target="tpu_custom_call" | custom-call | flops 1000 | bytes 1000 | tf_op jit(solution)/shard_map/add_for_chips/pallas_call | solution.py:671
  258.4 5.9 %reduce-scatter.5.cloned.1.call-done = bf16[1,512,512]{2,1,0:T(8,128)(2,1)} async-done(((bf16[4,512,512]{2,1,0:T(8,128)(2,1)}), bf16[1,512,512]{2,1,0:T(8,128)(2,1)}) %reduce-scatter.5.cloned.1.call-update) | async-done | bytes 524304 | tf_op jit(solution)/shard_map/reduce_scatter | solution.py:785
  264.3 6.4 %collective-permute-done.21 = bf16[4,128,512]{2,1,0:T(8,128)(2,1)S(1)} collective-permute-done((bf16[4,128,512]{2,1,0:T(8,128)(2,1)}, bf16[4,128,512]{2,1,0:T(8,128)(2,1)S(1)}, u32[]{:S(2)}, u32[]{:S(2)}) %collective-permute-start.21) | collective-permute-done | bytes 524320 | tf_op jit(solution)/shard_map/ppermute | solution.py:615
  270.7 9.2 %collective-permute-done.20 = bf16[4,128,512]{2,1,0:T(8,128)(2,1)S(1)} collective-permute-done((bf16[4,128,512]{2,1,0:T(8,128)(2,1)}, bf16[4,128,512]{2,1,0:T(8,128)(2,1)S(1)}, u32[]{:S(2)}, u32[]{:S(2)}) %collective-permute-start.20) | collective-permute-done | bytes 524320 | tf_op jit(solution)/shard_map/ppermute | solution.py:615
  285.4 10.7 %collective-permute-start.25 = (bf16[2,256,512]{2,1,0:T(8,128)(2,1)S(1)}, bf16[2,256,512]{2,1,0:T(8,128)(2,1)S(1)}, u32[]{:S(2)}, u32[]{:S(2)}) collective-permute-start(bf16[2,256,512]{2,1,0:T(8,128)(2,1)S(1)} %get-tuple-element.271), channel_id=1, source_target_pairs={{0,1},{1,0},{2,3},{3,2},{4,5},{5,4},{6,7},{7,6},{8,9},{9,8},{10,11... | collective-permute-start | bytes 1572872 | tf_op jit(solution)/shard_map/ppermute | solution.py:615
  297.3 10.3 %collective-permute-done.25 = bf16[2,256,512]{2,1,0:T(8,128)(2,1)S(1)} collective-permute-done((bf16[2,256,512]{2,1,0:T(8,128)(2,1)S(1)}, bf16[2,256,512]{2,1,0:T(8,128)(2,1)S(1)}, u32[]{:S(2)}, u32[]{:S(2)}) %collective-permute-start.25) | collective-permute-done | bytes 524320 | tf_op jit(solution)/shard_map/ppermute | solution.py:615
  315.4 5.3 %collective-permute-done.26 = f32[4,1792]{1,0:T(4,128)S(1)} collective-permute-done((f32[4,1792]{1,0:T(4,128)S(1)}, f32[4,1792]{1,0:T(4,128)S(1)}, u32[]{:S(2)}, u32[]{:S(2)}) %collective-permute-start.26) | collective-permute-done | bytes 28704 | tf_op jit(solution)/shard_map/ppermute | solution.py:615
  328.5 6.1 %place_feed.1 = (f32[256,4096]{1,0:T(8,128)}, f32[1024,1024]{1,0:T(8,128)}) custom-call(s32[2]{0:T(128)} %pad_add_fusion.3.info_ref, bf16[4,512,512]{2,1,0:T(8,128)(2,1)} %copy-done.3, bf16[4,512,512]{2,1,0:T(8,128)(2,1)} %collective-permute-done.34.other_ref), custom_call_target="tpu_custom_call" | custom-call | flops 1000 | bytes 1000 | tf_op jit(solution)/shard_map/place_feed/pallas_call | solution.py:563
  334.6 5.0 %collective-permute-done.32 = bf16[256,512]{1,0:T(8,128)(2,1)S(1)} collective-permute-done((bf16[256,512]{1,0:T(8,128)(2,1)S(1)}, bf16[256,512]{1,0:T(8,128)(2,1)S(1)}, u32[]{:S(2)}, u32[]{:S(2)}) %collective-permute-start.32) | collective-permute-done | bytes 262176 | tf_op jit(solution)/shard_map/ppermute | solution.py:615
  350.0 3.9 %place_heads.1 = (f32[256,3072]{1,0:T(8,128)}, f32[256,1024]{1,0:T(8,128)}) custom-call(s32[2]{0:T(128)} %pad_add_fusion.3.info_ref, bf16[4,256,512]{2,1,0:T(8,128)(2,1)} %copy-done.4, bf16[4,256,512]{2,1,0:T(8,128)(2,1)} %copy-done.10), custom_call_target="tpu_custom_call" | custom-call | flops 1000 | bytes 1000 | tf_op jit(solution)/shard_map/place_heads/pallas_call | solution.py:601
  (148 shorter events, 72.9 us)
Async XLA Ops:
  7.2 203.9 %reduce-scatter.7.cloned.1.call-start = ((), (), s32[]{:S(2)}) async-start(), calls=%async_computation.3 | async-start | bytes 10485760
  26.4 48.5 %collective-permute-start = (bf16[512,512]{1,0:T(8,128)(2,1)}, bf16[512,512]{1,0:T(8,128)(2,1)S(1)}, u32[]{:S(2)}, u32[]{:S(2)}) collective-permute-start(bf16[512,512]{1,0:T(8,128)(2,1)} %get-tuple-element.158), channel_id=1, source_target_pairs={{0,1},{1,2},{2,3},{3,0},{4,5},{5,6},{6,7},{7,4},{8,9},{9,10},{10,1... | collective-permute-start | bytes 1572872 | tf_op jit(solution)/shard_map/ppermute | solution.py:620
  29.5 45.5 %collective-permute-start.1 = (bf16[512,512]{1,0:T(8,128)(2,1)}, bf16[512,512]{1,0:T(8,128)(2,1)S(1)}, u32[]{:S(2)}, u32[]{:S(2)}) collective-permute-start(bf16[512,512]{1,0:T(8,128)(2,1)} %get-tuple-element.159), channel_id=1, source_target_pairs={{0,2},{1,3},{2,0},{3,1},{4,6},{5,7},{6,4},{7,5},{8,10},{9,11},{10,... | collective-permute-start | bytes 1572872 | tf_op jit(solution)/shard_map/ppermute | solution.py:620
  32.0 42.9 %collective-permute-start.2 = (bf16[512,512]{1,0:T(8,128)(2,1)}, bf16[512,512]{1,0:T(8,128)(2,1)S(1)}, u32[]{:S(2)}, u32[]{:S(2)}) collective-permute-start(bf16[512,512]{1,0:T(8,128)(2,1)} %get-tuple-element.160), channel_id=1, source_target_pairs={{0,3},{1,0},{2,1},{3,2},{4,7},{5,4},{6,5},{7,6},{8,11},{9,8},{10,9... | collective-permute-start | bytes 1572872 | tf_op jit(solution)/shard_map/ppermute | solution.py:620
  75.0 37.1 %collective-permute-start.6 = (bf16[4,4,256,512]{3,2,1,0:T(8,128)(2,1)}, bf16[4,4,256,512]{3,2,1,0:T(8,128)(2,1)}, u32[]{:S(2)}, u32[]{:S(2)}) collective-permute-start(bf16[4,4,256,512]{3,2,1,0:T(8,128)(2,1)} %get-tuple-element.171), channel_id=1, source_target_pairs={{0,4},{4,0},{8,12},{12,8},{16,20},{20,16},{24,28},{28,24},{1,5},{5... | collective-permute-start | bytes 12582920 | tf_op jit(solution)/shard_map/ppermute | solution.py:615
  75.1 37.0 %collective-permute-start.7 = (bf16[4,4,256,512]{3,2,1,0:T(8,128)(2,1)}, bf16[4,4,256,512]{3,2,1,0:T(8,128)(2,1)}, u32[]{:S(2)}, u32[]{:S(2)}) collective-permute-start(bf16[4,4,256,512]{3,2,1,0:T(8,128)(2,1)} %get-tuple-element.172), channel_id=1, source_target_pairs={{0,4},{4,0},{8,12},{12,8},{16,20},{20,16},{24,28},{28,24},{1,5},{5... | collective-permute-start | bytes 12582920 | tf_op jit(solution)/shard_map/ppermute | solution.py:615
  75.5 46.0 %collective-permute-start.3 = (bf16[512,512]{1,0:T(8,128)(2,1)}, bf16[512,512]{1,0:T(8,128)(2,1)S(1)}, u32[]{:S(2)}, u32[]{:S(2)}) collective-permute-start(bf16[512,512]{1,0:T(8,128)(2,1)} %get-tuple-element.161), channel_id=1, source_target_pairs={{0,1},{1,2},{2,3},{3,0},{4,5},{5,6},{6,7},{7,4},{8,9},{9,10},{10,1... | collective-permute-start | bytes 1572872 | tf_op jit(solution)/shard_map/ppermute | solution.py:620
  78.4 43.1 %collective-permute-start.4 = (bf16[512,512]{1,0:T(8,128)(2,1)}, bf16[512,512]{1,0:T(8,128)(2,1)S(1)}, u32[]{:S(2)}, u32[]{:S(2)}) collective-permute-start(bf16[512,512]{1,0:T(8,128)(2,1)} %get-tuple-element.162), channel_id=1, source_target_pairs={{0,2},{1,3},{2,0},{3,1},{4,6},{5,7},{6,4},{7,5},{8,10},{9,11},{10,... | collective-permute-start | bytes 1572872 | tf_op jit(solution)/shard_map/ppermute | solution.py:620
  80.1 41.5 %collective-permute-start.5 = (bf16[512,512]{1,0:T(8,128)(2,1)}, bf16[512,512]{1,0:T(8,128)(2,1)S(1)}, u32[]{:S(2)}, u32[]{:S(2)}) collective-permute-start(bf16[512,512]{1,0:T(8,128)(2,1)} %get-tuple-element.163), channel_id=1, source_target_pairs={{0,3},{1,0},{2,1},{3,2},{4,7},{5,4},{6,5},{7,6},{8,11},{9,8},{10,9... | collective-permute-start | bytes 1572872 | tf_op jit(solution)/shard_map/ppermute | solution.py:620
  122.7 141.6 %reduce-scatter.5.cloned.1.call-start = ((), (), s32[]{:S(2)}) async-start(), calls=%async_computation.2 | async-start | bytes 2621440 | tf_op jit(solution)/shard_map/reduce_scatter | solution.py:785
  122.7 38.1 %collective-permute-start.8 = (bf16[512,512]{1,0:T(8,128)(2,1)}, bf16[512,512]{1,0:T(8,128)(2,1)S(1)}, u32[]{:S(2)}, u32[]{:S(2)}) collective-permute-start(bf16[512,512]{1,0:T(8,128)(2,1)} %get-tuple-element.183), channel_id=1, source_target_pairs={{0,1},{1,2},{2,3},{3,0},{4,5},{5,6},{6,7},{7,4},{8,9},{9,10},{10,1... | collective-permute-start | bytes 1572872 | tf_op jit(solution)/shard_map/ppermute | solution.py:620
  127.0 35.2 %collective-permute-start.9 = (bf16[512,512]{1,0:T(8,128)(2,1)}, bf16[512,512]{1,0:T(8,128)(2,1)S(1)}, u32[]{:S(2)}, u32[]{:S(2)}) collective-permute-start(bf16[512,512]{1,0:T(8,128)(2,1)} %get-tuple-element.184), channel_id=1, source_target_pairs={{0,2},{1,3},{2,0},{3,1},{4,6},{5,7},{6,4},{7,5},{8,10},{9,11},{10,... | collective-permute-start | bytes 1572872 | tf_op jit(solution)/shard_map/ppermute | solution.py:620
  128.4 33.8 %collective-permute-start.10 = (bf16[512,512]{1,0:T(8,128)(2,1)}, bf16[512,512]{1,0:T(8,128)(2,1)S(1)}, u32[]{:S(2)}, u32[]{:S(2)}) collective-permute-start(bf16[512,512]{1,0:T(8,128)(2,1)} %get-tuple-element.185), channel_id=1, source_target_pairs={{0,3},{1,0},{2,1},{3,2},{4,7},{5,4},{6,5},{7,6},{8,11},{9,8},{10,9... | collective-permute-start | bytes 1572872 | tf_op jit(solution)/shard_map/ppermute | solution.py:620
  162.2 29.7 %collective-permute-start.11 = (bf16[512,512]{1,0:T(8,128)(2,1)}, bf16[512,512]{1,0:T(8,128)(2,1)S(1)}, u32[]{:S(2)}, u32[]{:S(2)}) collective-permute-start(bf16[512,512]{1,0:T(8,128)(2,1)} %get-tuple-element.186), channel_id=1, source_target_pairs={{0,1},{1,2},{2,3},{3,0},{4,5},{5,6},{6,7},{7,4},{8,9},{9,10},{10,1... | collective-permute-start | bytes 1572872 | tf_op jit(solution)/shard_map/ppermute | solution.py:620
  173.9 36.0 %collective-permute-start.12 = (bf16[512,512]{1,0:T(8,128)(2,1)}, bf16[512,512]{1,0:T(8,128)(2,1)S(1)}, u32[]{:S(2)}, u32[]{:S(2)}) collective-permute-start(bf16[512,512]{1,0:T(8,128)(2,1)} %get-tuple-element.187), channel_id=1, source_target_pairs={{0,2},{1,3},{2,0},{3,1},{4,6},{5,7},{6,4},{7,5},{8,10},{9,11},{10,... | collective-permute-start | bytes 1572872 | tf_op jit(solution)/shard_map/ppermute | solution.py:620
  176.0 33.8 %collective-permute-start.13 = (bf16[512,512]{1,0:T(8,128)(2,1)}, bf16[512,512]{1,0:T(8,128)(2,1)}, u32[]{:S(2)}, u32[]{:S(2)}) collective-permute-start(bf16[512,512]{1,0:T(8,128)(2,1)} %get-tuple-element.188), channel_id=1, source_target_pairs={{0,3},{1,0},{2,1},{3,2},{4,7},{5,4},{6,5},{7,6},{8,11},{9,8},{10,9... | collective-permute-start | bytes 1572872 | tf_op jit(solution)/shard_map/ppermute | solution.py:620
  222.9 26.9 %collective-permute-start.18 = (bf16[4,4,128,512]{3,2,1,0:T(8,128)(2,1)}, bf16[4,4,128,512]{3,2,1,0:T(8,128)(2,1)S(1)}, u32[]{:S(2)}, u32[]{:S(2)}) collective-permute-start(bf16[4,4,128,512]{3,2,1,0:T(8,128)(2,1)} %get-tuple-element.228), channel_id=1, source_target_pairs={{0,4},{4,0},{8,12},{12,8},{16,20},{20,16},{24,28},{28,24},{1,5},{5... | collective-permute-start | bytes 6291464 | tf_op jit(solution)/shard_map/ppermute | solution.py:615
  223.4 15.0 %collective-permute-start.15 = (bf16[4,128,512]{2,1,0:T(8,128)(2,1)}, bf16[4,128,512]{2,1,0:T(8,128)(2,1)S(1)}, u32[]{:S(2)}, u32[]{:S(2)}) collective-permute-start(bf16[4,128,512]{2,1,0:T(8,128)(2,1)} %get-tuple-element.225), channel_id=1, source_target_pairs={{0,8},{4,12},{8,0},{12,4},{16,24},{20,28},{24,16},{28,20},{1,9},{5... | collective-permute-start | bytes 1572872 | tf_op jit(solution)/shard_map/ppermute | solution.py:615
  224.8 25.0 %collective-permute-start.16 = (bf16[4,128,512]{2,1,0:T(8,128)(2,1)}, bf16[4,128,512]{2,1,0:T(8,128)(2,1)S(1)}, u32[]{:S(2)}, u32[]{:S(2)}) collective-permute-start(bf16[4,128,512]{2,1,0:T(8,128)(2,1)} %get-tuple-element.226), channel_id=1, source_target_pairs={{0,16},{4,20},{8,24},{12,28},{16,0},{20,4},{24,8},{28,12},{1,17},{... | collective-permute-start | bytes 1572872 | tf_op jit(solution)/shard_map/ppermute | solution.py:615
  225.4 24.3 %collective-permute-start.17 = (bf16[4,128,512]{2,1,0:T(8,128)(2,1)}, bf16[4,128,512]{2,1,0:T(8,128)(2,1)}, u32[]{:S(2)}, u32[]{:S(2)}) collective-permute-start(bf16[4,128,512]{2,1,0:T(8,128)(2,1)} %get-tuple-element.227), channel_id=1, source_target_pairs={{0,24},{4,28},{8,16},{12,20},{16,8},{20,12},{24,0},{28,4},{1,25},{... | collective-permute-start | bytes 1572872 | tf_op jit(solution)/shard_map/ppermute | solution.py:615
  254.7 16.0 %collective-permute-start.21 = (bf16[4,128,512]{2,1,0:T(8,128)(2,1)}, bf16[4,128,512]{2,1,0:T(8,128)(2,1)S(1)}, u32[]{:S(2)}, u32[]{:S(2)}) collective-permute-start(bf16[4,128,512]{2,1,0:T(8,128)(2,1)} %get-tuple-element.237), channel_id=1, source_target_pairs={{0,24},{4,28},{8,16},{12,20},{16,8},{20,12},{24,0},{28,4},{1,25},{... | collective-permute-start | bytes 1572872 | tf_op jit(solution)/shard_map/ppermute | solution.py:615
  256.2 23.7 %collective-permute-start.20 = (bf16[4,128,512]{2,1,0:T(8,128)(2,1)}, bf16[4,128,512]{2,1,0:T(8,128)(2,1)S(1)}, u32[]{:S(2)}, u32[]{:S(2)}) collective-permute-start(bf16[4,128,512]{2,1,0:T(8,128)(2,1)} %get-tuple-element.236), channel_id=1, source_target_pairs={{0,16},{4,20},{8,24},{12,28},{16,0},{20,4},{24,8},{28,12},{1,17},{... | collective-permute-start | bytes 1572872 | tf_op jit(solution)/shard_map/ppermute | solution.py:615
  257.2 22.8 %collective-permute-start.19 = (bf16[4,128,512]{2,1,0:T(8,128)(2,1)}, bf16[4,128,512]{2,1,0:T(8,128)(2,1)S(1)}, u32[]{:S(2)}, u32[]{:S(2)}) collective-permute-start(bf16[4,128,512]{2,1,0:T(8,128)(2,1)} %get-tuple-element.235), channel_id=1, source_target_pairs={{0,8},{4,12},{8,0},{12,4},{16,24},{20,28},{24,16},{28,20},{1,9},{5... | collective-permute-start | bytes 1572872 | tf_op jit(solution)/shard_map/ppermute | solution.py:615
  285.4 22.2 %collective-permute-start.25 = (bf16[2,256,512]{2,1,0:T(8,128)(2,1)S(1)}, bf16[2,256,512]{2,1,0:T(8,128)(2,1)S(1)}, u32[]{:S(2)}, u32[]{:S(2)}) collective-permute-start(bf16[2,256,512]{2,1,0:T(8,128)(2,1)S(1)} %get-tuple-element.271), channel_id=1, source_target_pairs={{0,1},{1,0},{2,3},{3,2},{4,5},{5,4},{6,7},{7,6},{8,9},{9,8},{10,11... | collective-permute-start | bytes 1572872 | tf_op jit(solution)/shard_map/ppermute | solution.py:615
  (39 other events, 348.0 us)
Sparse Core Ops, SparseCore 0:
  121.8 89.2 reduce-scatter.6
  213.4 50.8 reduce-scatter.4

commit v5 on v4

--- a/solution.py
+++ b/solution.py
@@ -849,6 +849,8 @@
     order.done((grad_rows, feed_mine, small))
 
     grad_back = back(order(grad_rows))
+    small = order(small)
+    small_arrived = exchange(small, "seq", 1)
     feed_other = exchange(order(feed_mine), "batch", 1)
     place_info = jnp.stack([core, place >> 1]).astype(jnp.int32)
     in_weight_grad, down_weight_grad = order.done(
@@ -860,13 +862,16 @@
             (down_weight.shape[0] // owners, width),
         )
     )
-    order.also(grad_back)
-    grad_mine = order.done(jnp.stack([grad_rows] + order(grad_back)))
+    order.also(grad_back, small_arrived)
+    small = small + order(small_arrived)
+    grad_mine = jnp.stack([grad_rows] + order(grad_back))
+    order.done((grad_mine, small))
 
     grad_other = exchange(order(grad_mine), "batch", 1)
-    small_arrived = [around(order(small), shift) for shift in range(1, owners)]
+    small = order(small)
+    small_arrived = exchange(small, "seq", 2)
     qkv_weight_grad, out_weight_grad = place_heads(place_info, order(grad_mine), grad_other, own_rows, width)
-    small = picked(sum(order(small_arrived), small), me)
+    small = picked(small + small_arrived, me)
     few = own_rows
     many = in_bias.shape[0] // owners
     return (

time: 361 us -> 358 us (level)
    ppermute x15 -> x12, starting transfers between devices: 38.6 us -> 33 us  [around(): lax.ppermute(rows, 'seq', [(place, (place + shift) % owners) for place in...]
    ppermute x24 -> x26, starting transfers between devices: 32.4 us -> 36.5 us  [exchange(): lax.ppermute(rows, axis, [(place, place ^ mask) for place in range(size)])]
    ppermute x15 -> x12, waiting for transfers between devices: 21.7 us -> 19.3 us  [around(): lax.ppermute(rows, 'seq', [(place, (place + shift) % owners) for place in...]
    ppermute x24 -> x26, waiting for transfers between devices: 52.6 us -> 53.4 us  [exchange(): lax.ppermute(rows, axis, [(place, place ^ mask) for place in range(size)])]
  transfers between devices with their start and end apart: 41 -> 40, of which waited for: 19 -> 16; matrix products, arithmetic and copies ran while one was open for 1% -> 1% of each run, Pallas kernels for 44% -> 44%
where the time goes in v5:
time: 358 us
  Pallas kernels  178 us (50%)
  waiting for transfers between devices  79.8 us (22%)
  starting transfers between devices  69.5 us (19%)
  between operations  15.7 us (4%)
  other arithmetic  8.04 us (2%)
  local copies, waits for them, and re-layouts  6.92 us (2%)
    pallas_call x2, Pallas kernels, attention(): pl.pallas_call(lambda *refs: attention_kernel(pieces, *refs), grid=(1,),...  61.8 us
    ppermute x26, waiting for transfers between devices, exchange(): lax.ppermute(rows, axis, [(place, place ^ mask) for place in range(size)])  53.4 us
    pallas_call x1, Pallas kernels, feed_forward(): pl.pallas_call(feed_kernel, grid_spec=pltpu.PrefetchScalarGridSpec(num_sc...  40.9 us
    ppermute x26, starting transfers between devices, exchange(): lax.ppermute(rows, axis, [(place, place ^ mask) for place in range(size)])  36.5 us
    ppermute x12, starting transfers between devices, around(): lax.ppermute(rows, 'seq', [(place, (place + shift) % owners) for place in...  33 us
    ppermute x12, waiting for transfers between devices, around(): lax.ppermute(rows, 'seq', [(place, (place + shift) % owners) for place in...  19.3 us
    pallas_call x2, Pallas kernels, sums_of(): pl.pallas_call(lambda *refs: sums_kernel(last, owners, *refs), grid=(1,),...  18.3 us
    pallas_call x2, Pallas kernels, weight_grads(): pl.pallas_call(lambda *refs: weight_kernel(pieces, *refs), grid=(1,), in_...  14 us
  transfers between devices with their start and end apart: 40, of which 16 were waited for; matrix products, arithmetic and copies ran while one was open for 1% of the time, Pallas kernels for 44%

profile of v5, /device:TPU:0, one launch (start us, length us, event | category | flops | bytes accessed | tf_op | source)
XLA Modules:
  0.0 357.6 jit_solution(17156962667162750377)
XLA Ops:
  10.7 4.6 %prep.1 = (f32[512,1024]{1,0:T(8,128)}, bf16[512,1024]{1,0:T(8,128)(2,1)}, bf16[1024,512]{1,0:T(8,128)(2,1)}) custom-call(bf16[512,1024]{1,0:T(8,128)(2,1)} %bitcast.51, s32[512,1]{1,0:T(8,128)} %select_select_fusion.mark_ref, bf16[32,1024]{1,0:T(8,128)(2,1)} %table_ref.1, f32[1,1024]{1,0:T(1,128)} %bitcast.65, f32[1,1024]{1,0:T(1,128)} %bitcast.67), custom_call_target="tpu_custom_call" | custom-call | flops 1000 | bytes 1000 | tf_op jit(solution)/shard_map/prep/pallas_call | solution.py:77
  15.2 11.2 %heads.1 = (bf16[512,512]{1,0:T(8,128)(2,1)}, bf16[512,512]{1,0:T(8,128)(2,1)}, bf16[512,512]{1,0:T(8,128)(2,1)}, bf16[512,512]{1,0:T(8,128)(2,1)}, bf16[512,512...) custom-call(s32[4]{0:T(128)} %compare_select_fusion.owners_ref, ...), custom_call_target="tpu_custom_call" | custom-call | flops 1000 | bytes 1000 | tf_op jit(solution)/shard_map/heads/pallas_call | solution.py:138
  34.0 40.9 %feed.1 = (bf16[4,4,256,512]{3,2,1,0:T(8,128)(2,1)}, bf16[4,4,256,512]{3,2,1,0:T(8,128)(2,1)}, bf16[4,4,256,512]{3,2,1,0:T(8,128)(2,1)}, bf16[4,4,256,512]{3,2,1...) custom-call(s32[8]{0:T(128)} %pad_add_fusion.2.cells_ref, ...), custom_call_target="tpu_custom_call" | custom-call | flops 1000 | bytes 1000 | tf_op jit(solution)/shard_map/feed/pallas_call | solution.py:390
  81.4 30.6 %attention.2 = (bf16[512,512]{1,0:T(8,128)(2,1)}, bf16[512,512]{1,0:T(8,128)(2,1)}, bf16[512,512]{1,0:T(8,128)(2,1)}, bf16[512,512]{1,0:T(8,128)(2,1)}) custom-call(s32[2]{0:T(128)} %get-tuple-element.280.refs_0_, bf16[512,512]{1,0:T(8,128)(2,1)} %get-tuple-element.144.refs_1_, bf16[512,512]{1,0:T(8,128)(2,1)} %copy-done.12, bf16[512,512]{1,0:T(8,128)(2,1)} %copy-done.14, ...), custom_call_target="tpu_custom_call" | custom-call | flops 1000 | bytes 1000 | tf_op jit(solution)/shard_map/attention/pallas_call | solution.py:294
  112.1 9.5 %add_pieces.1 = bf16[4,4,512,512]{3,2,1,0:T(8,128)(2,1)} custom-call(bf16[4,4,256,512]{3,2,1,0:T(8,128)(2,1)} %get-tuple-element.172.refs_0_, bf16[4,4,256,512]{3,2,1,0:T(8,128)(2,1)} %collective-permute-done.6.refs_1_, bf16[4,4,256,512]{3,2,1,0:T(8,128)(2,1)} %get-tuple-element.173.refs_2_, bf16[4,4,256,512]{3,2,1,0:T(8,128)(2,1)} %collective-permute-done.7.refs_3_), custom_call_target="tpu_custom_call" | custom-call | flops 1000 | bytes 1000 | tf_op jit(solution)/shard_map/add_pieces/pallas_call | solution.py:647
  122.7 4.3 %collective-permute-start.8 = (bf16[512,512]{1,0:T(8,128)(2,1)}, bf16[512,512]{1,0:T(8,128)(2,1)S(1)}, u32[]{:S(2)}, u32[]{:S(2)}) collective-permute-start(bf16[512,512]{1,0:T(8,128)(2,1)} %get-tuple-element.182), channel_id=1, source_target_pairs={{0,1},{1,2},{2,3},{3,0},{4,5},{5,6},{6,7},{7,4},{8,9},{9,10},{10,1... | collective-permute-start | bytes 1572872 | tf_op jit(solution)/shard_map/ppermute | solution.py:620
  129.5 31.2 %attention.3 = (bf16[512,512]{1,0:T(8,128)(2,1)}, bf16[512,512]{1,0:T(8,128)(2,1)}, bf16[512,512]{1,0:T(8,128)(2,1)}, bf16[512,512]{1,0:T(8,128)(2,1)}) custom-call(s32[2]{0:T(128)} %get-tuple-element.280.refs_0_, bf16[512,512]{1,0:T(8,128)(2,1)} %get-tuple-element.140.refs_1_, bf16[512,512]{1,0:T(8,128)(2,1)} %copy-done.13, bf16[512,512]{1,0:T(8,128)(2,1)} %copy-done.15, ...), custom_call_target="tpu_custom_call" | custom-call | flops 1000 | bytes 1000 | tf_op jit(solution)/shard_map/attention/pallas_call | solution.py:294
  162.2 11.7 %collective-permute-start.11 = (bf16[512,512]{1,0:T(8,128)(2,1)}, bf16[512,512]{1,0:T(8,128)(2,1)S(1)}, u32[]{:S(2)}, u32[]{:S(2)}) collective-permute-start(bf16[512,512]{1,0:T(8,128)(2,1)} %get-tuple-element.185), channel_id=1, source_target_pairs={{0,1},{1,2},{2,3},{3,0},{4,5},{5,6},{6,7},{7,4},{8,9},{9,10},{10,1... | collective-permute-start | bytes 1572872 | tf_op jit(solution)/shard_map/ppermute | solution.py:620
  176.3 8.4 %sums.2 = (f32[512,1024]{1,0:T(8,128)}, f32[512,1024]{1,0:T(8,128)}) custom-call(s32[2]{0:T(128)} %get-tuple-element.279.refs_0_, bf16[512,512]{1,0:T(8,128)(2,1)} %get-tuple-element.197.refs_1_.refs_3_, bf16[512,512]{1,0:T(8,128)(2,1)} %copy-done.7, bf16[512,512]{1,0:T(8,128)(2,1)} %copy-done.8, bf16[512,512]{1,0:T(8,128)(2,1)} %copy-done.9, ...), custom_call_target="tpu_custom_call" | custom-call | flops 1000 | bytes 1000 | tf_op jit(solution)/shard_map/sums/pallas_call | solution.py:524
  184.7 7.2 %weight_grads.2 = (bf16[4,4,128,512]{3,2,1,0:T(8,128)(2,1)}, bf16[4,4,128,512]{3,2,1,0:T(8,128)(2,1)}) custom-call(s32[2]{0:T(128)} %get-tuple-element.279.refs_0_, bf16[1024,512]{1,0:T(8,128)(2,1)} %get-tuple-element.149.turned_ref.refs_1_, bf16[512,1024]{1,0:T(8,128)(2,1)} %bitcast.45, bf16[512,512]{1,0:T(8,128)(2,1)} %get-tuple-element.197.refs_1_.refs_3_, ...), custom_call_target="tpu_custom_call" | custom-call | flops 1000 | bytes 1000 | tf_op jit(solution)/shard_map/weight_grads/pallas_call | solution.py:456
  192.0 17.9 %collective-permute-done.12.refs_5_.refs_3_ = bf16[512,512]{1,0:T(8,128)(2,1)S(1)} collective-permute-done((bf16[512,512]{1,0:T(8,128)(2,1)}, bf16[512,512]{1,0:T(8,128)(2,1)S(1)}, u32[]{:S(2)}, u32[]{:S(2)}) %collective-permute-start.12) | collective-permute-done | bytes 524320 | tf_op jit(solution)/shard_map/ppermute | solution.py:620
  211.1 6.8 %weight_grads.3 = (bf16[4,4,128,512]{3,2,1,0:T(8,128)(2,1)}, bf16[4,4,128,512]{3,2,1,0:T(8,128)(2,1)}) custom-call(s32[2]{0:T(128)} %get-tuple-element.279.refs_0_, bf16[1024,512]{1,0:T(8,128)(2,1)} %get-tuple-element.149.turned_ref.refs_1_, bf16[512,1024]{1,0:T(8,128)(2,1)} %bitcast.46, bf16[512,512]{1,0:T(8,128)(2,1)} %get-tuple-element.215.refs_3_.refs_1_, ...), custom_call_target="tpu_custom_call" | custom-call | flops 1000 | bytes 1000 | tf_op jit(solution)/shard_map/weight_grads/pallas_call | solution.py:456
  226.9 9.8 %sums.3 = (bf16[512,1024]{1,0:T(8,128)(2,1)}, f32[512,1024]{1,0:T(8,128)}, f32[4,256]{1,0:T(4,128)}, f32[4,256]{1,0:T(4,128)}) custom-call(s32[2]{0:T(128)} %get-tuple-element.279.refs_0_, bf16[512,512]{1,0:T(8,128)(2,1)} %get-tuple-element.215.refs_3_.refs_1_, bf16[512,512]{1,0:T(8,128)(2,1)} %copy-done.5, bf16[512,512]{1,0:T(8,128)(2,1)} %copy-done.6, ...), custom_call_target="tpu_custom_call" | custom-call | flops 1000 | bytes 1000 | tf_op jit(solution)/shard_map/sums/pallas_call | solution.py:524
  238.4 11.4 %collective-permute-done.16 = bf16[4,128,512]{2,1,0:T(8,128)(2,1)S(1)} collective-permute-done((bf16[4,128,512]{2,1,0:T(8,128)(2,1)}, bf16[4,128,512]{2,1,0:T(8,128)(2,1)S(1)}, u32[]{:S(2)}, u32[]{:S(2)}) %collective-permute-start.16) | collective-permute-done | bytes 524320 | tf_op jit(solution)/shard_map/ppermute | solution.py:615
  251.2 3.6 %add_for_chips.3 = (bf16[4,128,512]{2,1,0:T(8,128)(2,1)}, bf16[4,128,512]{2,1,0:T(8,128)(2,1)}, bf16[4,128,512]{2,1,0:T(8,128)(2,1)}, bf16[4,128,512]{2,1,0:T(8,128)(2,1)}) custom-call(s32[1]{0:T(128)} %bitcast.12.refs_0_, bf16[4,4,128,512]{3,2,1,0:T(8,128)(2,1)} %get-tuple-element.228.refs_1_.refs_3_.refs_5_.refs_7_, bf16[4,4,128,512]{3,2,1,0:T(8,128)(2,1)} %copy-done.1, ...), custom_call_target="tpu_custom_call" | custom-call | flops 1000 | bytes 1000 | tf_op jit(solution)/shard_map/add_for_chips/pallas_call | solution.py:671
  258.4 5.9 %reduce-scatter.5.cloned.1.call-done = bf16[1,512,512]{2,1,0:T(8,128)(2,1)} async-done(((bf16[4,512,512]{2,1,0:T(8,128)(2,1)}), bf16[1,512,512]{2,1,0:T(8,128)(2,1)}) %reduce-scatter.5.cloned.1.call-update) | async-done | bytes 524304 | tf_op jit(solution)/shard_map/reduce_scatter | solution.py:785
  264.3 6.5 %collective-permute-done.21 = bf16[4,128,512]{2,1,0:T(8,128)(2,1)S(1)} collective-permute-done((bf16[4,128,512]{2,1,0:T(8,128)(2,1)}, bf16[4,128,512]{2,1,0:T(8,128)(2,1)S(1)}, u32[]{:S(2)}, u32[]{:S(2)}) %collective-permute-start.21) | collective-permute-done | bytes 524320 | tf_op jit(solution)/shard_map/ppermute | solution.py:615
  270.8 9.2 %collective-permute-done.20 = bf16[4,128,512]{2,1,0:T(8,128)(2,1)S(1)} collective-permute-done((bf16[4,128,512]{2,1,0:T(8,128)(2,1)}, bf16[4,128,512]{2,1,0:T(8,128)(2,1)S(1)}, u32[]{:S(2)}, u32[]{:S(2)}) %collective-permute-start.20) | collective-permute-done | bytes 524320 | tf_op jit(solution)/shard_map/ppermute | solution.py:615
  285.5 10.6 %collective-permute-start.25 = (bf16[2,256,512]{2,1,0:T(8,128)(2,1)S(1)}, bf16[2,256,512]{2,1,0:T(8,128)(2,1)S(1)}, u32[]{:S(2)}, u32[]{:S(2)}) collective-permute-start(bf16[2,256,512]{2,1,0:T(8,128)(2,1)S(1)} %get-tuple-element.269), channel_id=1, source_target_pairs={{0,1},{1,0},{2,3},{3,2},{4,5},{5,4},{6,7},{7,6},{8,9},{9,8},{10,11... | collective-permute-start | bytes 1572872 | tf_op jit(solution)/shard_map/ppermute | solution.py:615
  297.3 10.3 %collective-permute-done.25 = bf16[2,256,512]{2,1,0:T(8,128)(2,1)S(1)} collective-permute-done((bf16[2,256,512]{2,1,0:T(8,128)(2,1)S(1)}, bf16[2,256,512]{2,1,0:T(8,128)(2,1)S(1)}, u32[]{:S(2)}, u32[]{:S(2)}) %collective-permute-start.25) | collective-permute-done | bytes 524320 | tf_op jit(solution)/shard_map/ppermute | solution.py:615
  315.5 5.3 %collective-permute-done.26 = f32[4,1792]{1,0:T(4,128)S(1)} collective-permute-done((f32[4,1792]{1,0:T(4,128)S(1)}, f32[4,1792]{1,0:T(4,128)S(1)}, u32[]{:S(2)}, u32[]{:S(2)}) %collective-permute-start.26) | collective-permute-done | bytes 28704 | tf_op jit(solution)/shard_map/ppermute | solution.py:615
  329.8 6.1 %place_feed.1 = (f32[256,4096]{1,0:T(8,128)}, f32[1024,1024]{1,0:T(8,128)}) custom-call(s32[2]{0:T(128)} %pad_add_fusion.3.info_ref, bf16[4,512,512]{2,1,0:T(8,128)(2,1)} %copy-done.3, bf16[4,512,512]{2,1,0:T(8,128)(2,1)} %collective-permute-done.32.other_ref), custom_call_target="tpu_custom_call" | custom-call | flops 1000 | bytes 1000 | tf_op jit(solution)/shard_map/place_feed/pallas_call | solution.py:563
  335.9 3.7 %collective-permute-done.34 = bf16[256,512]{1,0:T(8,128)(2,1)S(1)} collective-permute-done((bf16[256,512]{1,0:T(8,128)(2,1)S(1)}, bf16[256,512]{1,0:T(8,128)(2,1)S(1)}, u32[]{:S(2)}, u32[]{:S(2)}) %collective-permute-start.34) | collective-permute-done | bytes 262176 | tf_op jit(solution)/shard_map/ppermute | solution.py:615
  346.9 3.9 %place_heads.1 = (f32[256,3072]{1,0:T(8,128)}, f32[256,1024]{1,0:T(8,128)}) custom-call(s32[2]{0:T(128)} %pad_add_fusion.3.info_ref, bf16[4,256,512]{2,1,0:T(8,128)(2,1)} %copy-done.4, bf16[4,256,512]{2,1,0:T(8,128)(2,1)} %copy-done.10), custom_call_target="tpu_custom_call" | custom-call | flops 1000 | bytes 1000 | tf_op jit(solution)/shard_map/place_heads/pallas_call | solution.py:601
  (147 shorter events, 71.0 us)
Async XLA Ops:
  7.2 203.9 %reduce-scatter.7.cloned.1.call-start = ((), (), s32[]{:S(2)}) async-start(), calls=%async_computation.3 | async-start | bytes 10485760
  26.5 48.5 %collective-permute-start = (bf16[512,512]{1,0:T(8,128)(2,1)}, bf16[512,512]{1,0:T(8,128)(2,1)S(1)}, u32[]{:S(2)}, u32[]{:S(2)}) collective-permute-start(bf16[512,512]{1,0:T(8,128)(2,1)} %get-tuple-element.157), channel_id=1, source_target_pairs={{0,1},{1,2},{2,3},{3,0},{4,5},{5,6},{6,7},{7,4},{8,9},{9,10},{10,1... | collective-permute-start | bytes 1572872 | tf_op jit(solution)/shard_map/ppermute | solution.py:620
  29.5 45.5 %collective-permute-start.1 = (bf16[512,512]{1,0:T(8,128)(2,1)}, bf16[512,512]{1,0:T(8,128)(2,1)S(1)}, u32[]{:S(2)}, u32[]{:S(2)}) collective-permute-start(bf16[512,512]{1,0:T(8,128)(2,1)} %get-tuple-element.158), channel_id=1, source_target_pairs={{0,2},{1,3},{2,0},{3,1},{4,6},{5,7},{6,4},{7,5},{8,10},{9,11},{10,... | collective-permute-start | bytes 1572872 | tf_op jit(solution)/shard_map/ppermute | solution.py:620
  32.1 42.9 %collective-permute-start.2 = (bf16[512,512]{1,0:T(8,128)(2,1)}, bf16[512,512]{1,0:T(8,128)(2,1)S(1)}, u32[]{:S(2)}, u32[]{:S(2)}) collective-permute-start(bf16[512,512]{1,0:T(8,128)(2,1)} %get-tuple-element.159), channel_id=1, source_target_pairs={{0,3},{1,0},{2,1},{3,2},{4,7},{5,4},{6,5},{7,6},{8,11},{9,8},{10,9... | collective-permute-start | bytes 1572872 | tf_op jit(solution)/shard_map/ppermute | solution.py:620
  75.0 37.1 %collective-permute-start.6 = (bf16[4,4,256,512]{3,2,1,0:T(8,128)(2,1)}, bf16[4,4,256,512]{3,2,1,0:T(8,128)(2,1)}, u32[]{:S(2)}, u32[]{:S(2)}) collective-permute-start(bf16[4,4,256,512]{3,2,1,0:T(8,128)(2,1)} %get-tuple-element.170), channel_id=1, source_target_pairs={{0,4},{4,0},{8,12},{12,8},{16,20},{20,16},{24,28},{28,24},{1,5},{5... | collective-permute-start | bytes 12582920 | tf_op jit(solution)/shard_map/ppermute | solution.py:615
  75.1 37.0 %collective-permute-start.7 = (bf16[4,4,256,512]{3,2,1,0:T(8,128)(2,1)}, bf16[4,4,256,512]{3,2,1,0:T(8,128)(2,1)}, u32[]{:S(2)}, u32[]{:S(2)}) collective-permute-start(bf16[4,4,256,512]{3,2,1,0:T(8,128)(2,1)} %get-tuple-element.171), channel_id=1, source_target_pairs={{0,4},{4,0},{8,12},{12,8},{16,20},{20,16},{24,28},{28,24},{1,5},{5... | collective-permute-start | bytes 12582920 | tf_op jit(solution)/shard_map/ppermute | solution.py:615
  75.6 46.0 %collective-permute-start.3 = (bf16[512,512]{1,0:T(8,128)(2,1)}, bf16[512,512]{1,0:T(8,128)(2,1)S(1)}, u32[]{:S(2)}, u32[]{:S(2)}) collective-permute-start(bf16[512,512]{1,0:T(8,128)(2,1)} %get-tuple-element.160), channel_id=1, source_target_pairs={{0,1},{1,2},{2,3},{3,0},{4,5},{5,6},{6,7},{7,4},{8,9},{9,10},{10,1... | collective-permute-start | bytes 1572872 | tf_op jit(solution)/shard_map/ppermute | solution.py:620
  78.5 43.1 %collective-permute-start.4 = (bf16[512,512]{1,0:T(8,128)(2,1)}, bf16[512,512]{1,0:T(8,128)(2,1)S(1)}, u32[]{:S(2)}, u32[]{:S(2)}) collective-permute-start(bf16[512,512]{1,0:T(8,128)(2,1)} %get-tuple-element.161), channel_id=1, source_target_pairs={{0,2},{1,3},{2,0},{3,1},{4,6},{5,7},{6,4},{7,5},{8,10},{9,11},{10,... | collective-permute-start | bytes 1572872 | tf_op jit(solution)/shard_map/ppermute | solution.py:620
  80.1 41.5 %collective-permute-start.5 = (bf16[512,512]{1,0:T(8,128)(2,1)}, bf16[512,512]{1,0:T(8,128)(2,1)S(1)}, u32[]{:S(2)}, u32[]{:S(2)}) collective-permute-start(bf16[512,512]{1,0:T(8,128)(2,1)} %get-tuple-element.162), channel_id=1, source_target_pairs={{0,3},{1,0},{2,1},{3,2},{4,7},{5,4},{6,5},{7,6},{8,11},{9,8},{10,9... | collective-permute-start | bytes 1572872 | tf_op jit(solution)/shard_map/ppermute | solution.py:620
  122.7 141.6 %reduce-scatter.5.cloned.1.call-start = ((), (), s32[]{:S(2)}) async-start(), calls=%async_computation.2 | async-start | bytes 2621440 | tf_op jit(solution)/shard_map/reduce_scatter | solution.py:785
  122.7 38.1 %collective-permute-start.8 = (bf16[512,512]{1,0:T(8,128)(2,1)}, bf16[512,512]{1,0:T(8,128)(2,1)S(1)}, u32[]{:S(2)}, u32[]{:S(2)}) collective-permute-start(bf16[512,512]{1,0:T(8,128)(2,1)} %get-tuple-element.182), channel_id=1, source_target_pairs={{0,1},{1,2},{2,3},{3,0},{4,5},{5,6},{6,7},{7,4},{8,9},{9,10},{10,1... | collective-permute-start | bytes 1572872 | tf_op jit(solution)/shard_map/ppermute | solution.py:620
  127.0 35.2 %collective-permute-start.9 = (bf16[512,512]{1,0:T(8,128)(2,1)}, bf16[512,512]{1,0:T(8,128)(2,1)S(1)}, u32[]{:S(2)}, u32[]{:S(2)}) collective-permute-start(bf16[512,512]{1,0:T(8,128)(2,1)} %get-tuple-element.183), channel_id=1, source_target_pairs={{0,2},{1,3},{2,0},{3,1},{4,6},{5,7},{6,4},{7,5},{8,10},{9,11},{10,... | collective-permute-start | bytes 1572872 | tf_op jit(solution)/shard_map/ppermute | solution.py:620
  128.4 33.8 %collective-permute-start.10 = (bf16[512,512]{1,0:T(8,128)(2,1)}, bf16[512,512]{1,0:T(8,128)(2,1)S(1)}, u32[]{:S(2)}, u32[]{:S(2)}) collective-permute-start(bf16[512,512]{1,0:T(8,128)(2,1)} %get-tuple-element.184), channel_id=1, source_target_pairs={{0,3},{1,0},{2,1},{3,2},{4,7},{5,4},{6,5},{7,6},{8,11},{9,8},{10,9... | collective-permute-start | bytes 1572872 | tf_op jit(solution)/shard_map/ppermute | solution.py:620
  162.2 29.7 %collective-permute-start.11 = (bf16[512,512]{1,0:T(8,128)(2,1)}, bf16[512,512]{1,0:T(8,128)(2,1)S(1)}, u32[]{:S(2)}, u32[]{:S(2)}) collective-permute-start(bf16[512,512]{1,0:T(8,128)(2,1)} %get-tuple-element.185), channel_id=1, source_target_pairs={{0,1},{1,2},{2,3},{3,0},{4,5},{5,6},{6,7},{7,4},{8,9},{9,10},{10,1... | collective-permute-start | bytes 1572872 | tf_op jit(solution)/shard_map/ppermute | solution.py:620
  173.9 36.0 %collective-permute-start.12 = (bf16[512,512]{1,0:T(8,128)(2,1)}, bf16[512,512]{1,0:T(8,128)(2,1)S(1)}, u32[]{:S(2)}, u32[]{:S(2)}) collective-permute-start(bf16[512,512]{1,0:T(8,128)(2,1)} %get-tuple-element.186), channel_id=1, source_target_pairs={{0,2},{1,3},{2,0},{3,1},{4,6},{5,7},{6,4},{7,5},{8,10},{9,11},{10,... | collective-permute-start | bytes 1572872 | tf_op jit(solution)/shard_map/ppermute | solution.py:620
  176.0 33.8 %collective-permute-start.13 = (bf16[512,512]{1,0:T(8,128)(2,1)}, bf16[512,512]{1,0:T(8,128)(2,1)}, u32[]{:S(2)}, u32[]{:S(2)}) collective-permute-start(bf16[512,512]{1,0:T(8,128)(2,1)} %get-tuple-element.187), channel_id=1, source_target_pairs={{0,3},{1,0},{2,1},{3,2},{4,7},{5,4},{6,5},{7,6},{8,11},{9,8},{10,9... | collective-permute-start | bytes 1572872 | tf_op jit(solution)/shard_map/ppermute | solution.py:620
  222.9 26.9 %collective-permute-start.18 = (bf16[4,4,128,512]{3,2,1,0:T(8,128)(2,1)}, bf16[4,4,128,512]{3,2,1,0:T(8,128)(2,1)S(1)}, u32[]{:S(2)}, u32[]{:S(2)}) collective-permute-start(bf16[4,4,128,512]{3,2,1,0:T(8,128)(2,1)} %get-tuple-element.227), channel_id=1, source_target_pairs={{0,4},{4,0},{8,12},{12,8},{16,20},{20,16},{24,28},{28,24},{1,5},{5... | collective-permute-start | bytes 6291464 | tf_op jit(solution)/shard_map/ppermute | solution.py:615
  223.4 15.0 %collective-permute-start.15 = (bf16[4,128,512]{2,1,0:T(8,128)(2,1)}, bf16[4,128,512]{2,1,0:T(8,128)(2,1)S(1)}, u32[]{:S(2)}, u32[]{:S(2)}) collective-permute-start(bf16[4,128,512]{2,1,0:T(8,128)(2,1)} %get-tuple-element.224), channel_id=1, source_target_pairs={{0,8},{4,12},{8,0},{12,4},{16,24},{20,28},{24,16},{28,20},{1,9},{5... | collective-permute-start | bytes 1572872 | tf_op jit(solution)/shard_map/ppermute | solution.py:615
  224.8 25.0 %collective-permute-start.16 = (bf16[4,128,512]{2,1,0:T(8,128)(2,1)}, bf16[4,128,512]{2,1,0:T(8,128)(2,1)S(1)}, u32[]{:S(2)}, u32[]{:S(2)}) collective-permute-start(bf16[4,128,512]{2,1,0:T(8,128)(2,1)} %get-tuple-element.225), channel_id=1, source_target_pairs={{0,16},{4,20},{8,24},{12,28},{16,0},{20,4},{24,8},{28,12},{1,17},{... | collective-permute-start | bytes 1572872 | tf_op jit(solution)/shard_map/ppermute | solution.py:615
  225.5 24.3 %collective-permute-start.17 = (bf16[4,128,512]{2,1,0:T(8,128)(2,1)}, bf16[4,128,512]{2,1,0:T(8,128)(2,1)}, u32[]{:S(2)}, u32[]{:S(2)}) collective-permute-start(bf16[4,128,512]{2,1,0:T(8,128)(2,1)} %get-tuple-element.226), channel_id=1, source_target_pairs={{0,24},{4,28},{8,16},{12,20},{16,8},{20,12},{24,0},{28,4},{1,25},{... | collective-permute-start | bytes 1572872 | tf_op jit(solution)/shard_map/ppermute | solution.py:615
  254.8 16.0 %collective-permute-start.21 = (bf16[4,128,512]{2,1,0:T(8,128)(2,1)}, bf16[4,128,512]{2,1,0:T(8,128)(2,1)S(1)}, u32[]{:S(2)}, u32[]{:S(2)}) collective-permute-start(bf16[4,128,512]{2,1,0:T(8,128)(2,1)} %get-tuple-element.236), channel_id=1, source_target_pairs={{0,24},{4,28},{8,16},{12,20},{16,8},{20,12},{24,0},{28,4},{1,25},{... | collective-permute-start | bytes 1572872 | tf_op jit(solution)/shard_map/ppermute | solution.py:615
  256.2 23.7 %collective-permute-start.20 = (bf16[4,128,512]{2,1,0:T(8,128)(2,1)}, bf16[4,128,512]{2,1,0:T(8,128)(2,1)S(1)}, u32[]{:S(2)}, u32[]{:S(2)}) collective-permute-start(bf16[4,128,512]{2,1,0:T(8,128)(2,1)} %get-tuple-element.235), channel_id=1, source_target_pairs={{0,16},{4,20},{8,24},{12,28},{16,0},{20,4},{24,8},{28,12},{1,17},{... | collective-permute-start | bytes 1572872 | tf_op jit(solution)/shard_map/ppermute | solution.py:615
  257.2 22.7 %collective-permute-start.19 = (bf16[4,128,512]{2,1,0:T(8,128)(2,1)}, bf16[4,128,512]{2,1,0:T(8,128)(2,1)S(1)}, u32[]{:S(2)}, u32[]{:S(2)}) collective-permute-start(bf16[4,128,512]{2,1,0:T(8,128)(2,1)} %get-tuple-element.234), channel_id=1, source_target_pairs={{0,8},{4,12},{8,0},{12,4},{16,24},{20,28},{24,16},{28,20},{1,9},{5... | collective-permute-start | bytes 1572872 | tf_op jit(solution)/shard_map/ppermute | solution.py:615
  285.5 22.2 %collective-permute-start.25 = (bf16[2,256,512]{2,1,0:T(8,128)(2,1)S(1)}, bf16[2,256,512]{2,1,0:T(8,128)(2,1)S(1)}, u32[]{:S(2)}, u32[]{:S(2)}) collective-permute-start(bf16[2,256,512]{2,1,0:T(8,128)(2,1)S(1)} %get-tuple-element.269), channel_id=1, source_target_pairs={{0,1},{1,0},{2,3},{3,2},{4,5},{5,4},{6,7},{7,6},{8,9},{9,8},{10,11... | collective-permute-start | bytes 1572872 | tf_op jit(solution)/shard_map/ppermute | solution.py:615
  (38 other events, 343.4 us)
Sparse Core Ops, SparseCore 0:
  121.8 89.2 reduce-scatter.6
  213.5 50.7 reduce-scatter.4

commit v6 on v5

--- a/solution.py
+++ b/solution.py
@@ -819,20 +819,21 @@
             axis=1,
         )
     )
-    order.also(second_arrived, feed_rows)
-    grad_rows = order.done(
-        jnp.concatenate(
-            [
-                total_of(order(held[0]), *arrived)
-                for held, arrived in ((first_held, first_arrived), (second_held, second_arrived))
-            ],
-            axis=1,
-        )
-    )
+    small_arrived = exchange(order(small), "batch", 1)
+    order.also(second_arrived, feed_rows, small_arrived)
+    small = small + order(small_arrived)
+    grad_rows = jnp.concatenate(
+        [
+            total_of(order(held[0]), *arrived)
+            for held, arrived in ((first_held, first_arrived), (second_held, second_arrived))
+        ],
+        axis=1,
+    )
+    order.done((grad_rows, small))
 
     feed_rows = order(feed_rows)
     feed_back = [exchange(feed_rows, "batch", mask) for mask in (2, 4)]
-    small_arrived = exchange(order(small), "batch", 1)
+    small_arrived = exchange(order(small), "batch", 2)
     grad_rows, grad_arrived = halve_seq(order(grad_rows), 0)
     order.also(feed_back, grad_arrived, small_arrived)
     small = small + order(small_arrived)
@@ -840,11 +841,11 @@
     order.done((grad_rows, small))
 
     feed_back.append(exchange(order(feed_rows), "batch", 6))
-    small_arrived = back(order(small))
+    small_arrived = exchange(order(small), "batch", 4)
     grad_rows, grad_arrived = halve_seq(order(grad_rows), 1)
     order.also(feed_back, grad_arrived, small_arrived)
     grad_rows = total_of(order(grad_rows), grad_arrived)[0]
-    small = sum(order(small_arrived), small)
+    small = small + order(small_arrived)
     feed_mine = jnp.stack([feed_rows] + order(feed_back))
     order.done((grad_rows, feed_mine, small))
 

time: 358 us -> 354 us (0.989)
    ppermute x26 -> x25, starting transfers between devices: 36.5 us -> 33.2 us  [exchange(): lax.ppermute(rows, axis, [(place, place ^ mask) for place in range(size)])]
    ppermute x26 -> x25, waiting for transfers between devices: 53.4 us -> 52.9 us  [exchange(): lax.ppermute(rows, axis, [(place, place ^ mask) for place in range(size)])]
  transfers between devices with their start and end apart: 40 -> 39, of which waited for: 16 -> 14; matrix products, arithmetic and copies ran while one was open for 1% -> 1% of each run, Pallas kernels for 44% -> 45%
where the time goes in v6:
time: 354 us
  Pallas kernels  177 us (50%)
  waiting for transfers between devices  79.3 us (22%)
  starting transfers between devices  66.2 us (19%)
  between operations  15.8 us (4%)
  other arithmetic  8.07 us (2%)
  local copies, waits for them, and re-layouts  6.92 us (2%)
    pallas_call x2, Pallas kernels, attention(): pl.pallas_call(lambda *refs: attention_kernel(pieces, *refs), grid=(1,),...  61.8 us
    ppermute x25, waiting for transfers between devices, exchange(): lax.ppermute(rows, axis, [(place, place ^ mask) for place in range(size)])  52.9 us
    pallas_call x1, Pallas kernels, feed_forward(): pl.pallas_call(feed_kernel, grid_spec=pltpu.PrefetchScalarGridSpec(num_sc...  40.9 us
    ppermute x25, starting transfers between devices, exchange(): lax.ppermute(rows, axis, [(place, place ^ mask) for place in range(size)])  33.2 us
    ppermute x12, starting transfers between devices, around(): lax.ppermute(rows, 'seq', [(place, (place + shift) % owners) for place in...  33 us
    ppermute x12, waiting for transfers between devices, around(): lax.ppermute(rows, 'seq', [(place, (place + shift) % owners) for place in...  19.3 us
    pallas_call x2, Pallas kernels, sums_of(): pl.pallas_call(lambda *refs: sums_kernel(last, owners, *refs), grid=(1,),...  18.3 us
    pallas_call x2, Pallas kernels, weight_grads(): pl.pallas_call(lambda *refs: weight_kernel(pieces, *refs), grid=(1,), in_...  14 us
  transfers between devices with their start and end apart: 39, of which 14 were waited for; matrix products, arithmetic and copies ran while one was open for 1% of the time, Pallas kernels for 45%

profile of v6, /device:TPU:0, one launch (start us, length us, event | category | flops | bytes accessed | tf_op | source)
XLA Modules:
  0.0 353.8 jit_solution(2306623797249169538)
XLA Ops:
  10.7 4.6 %prep.1 = (f32[512,1024]{1,0:T(8,128)}, bf16[512,1024]{1,0:T(8,128)(2,1)}, bf16[1024,512]{1,0:T(8,128)(2,1)}) custom-call(bf16[512,1024]{1,0:T(8,128)(2,1)} %bitcast.51, s32[512,1]{1,0:T(8,128)} %select_select_fusion.mark_ref, bf16[32,1024]{1,0:T(8,128)(2,1)} %table_ref.1, f32[1,1024]{1,0:T(1,128)} %bitcast.65, f32[1,1024]{1,0:T(1,128)} %bitcast.67), custom_call_target="tpu_custom_call" | custom-call | flops 1000 | bytes 1000 | tf_op jit(solution)/shard_map/prep/pallas_call | solution.py:77
  15.2 11.2 %heads.1 = (bf16[512,512]{1,0:T(8,128)(2,1)}, bf16[512,512]{1,0:T(8,128)(2,1)}, bf16[512,512]{1,0:T(8,128)(2,1)}, bf16[512,512]{1,0:T(8,128)(2,1)}, bf16[512,512...) custom-call(s32[4]{0:T(128)} %compare_select_fusion.owners_ref, ...), custom_call_target="tpu_custom_call" | custom-call | flops 1000 | bytes 1000 | tf_op jit(solution)/shard_map/heads/pallas_call | solution.py:138
  34.0 40.9 %feed.1 = (bf16[4,4,256,512]{3,2,1,0:T(8,128)(2,1)}, bf16[4,4,256,512]{3,2,1,0:T(8,128)(2,1)}, bf16[4,4,256,512]{3,2,1,0:T(8,128)(2,1)}, bf16[4,4,256,512]{3,2,1...) custom-call(s32[8]{0:T(128)} %pad_add_fusion.2.cells_ref, ...), custom_call_target="tpu_custom_call" | custom-call | flops 1000 | bytes 1000 | tf_op jit(solution)/shard_map/feed/pallas_call | solution.py:390
  81.4 30.6 %attention.2 = (bf16[512,512]{1,0:T(8,128)(2,1)}, bf16[512,512]{1,0:T(8,128)(2,1)}, bf16[512,512]{1,0:T(8,128)(2,1)}, bf16[512,512]{1,0:T(8,128)(2,1)}) custom-call(s32[2]{0:T(128)} %get-tuple-element.280.refs_0_, bf16[512,512]{1,0:T(8,128)(2,1)} %get-tuple-element.144.refs_1_, bf16[512,512]{1,0:T(8,128)(2,1)} %copy-done.12, bf16[512,512]{1,0:T(8,128)(2,1)} %copy-done.14, ...), custom_call_target="tpu_custom_call" | custom-call | flops 1000 | bytes 1000 | tf_op jit(solution)/shard_map/attention/pallas_call | solution.py:294
  112.1 9.5 %add_pieces.1 = bf16[4,4,512,512]{3,2,1,0:T(8,128)(2,1)} custom-call(bf16[4,4,256,512]{3,2,1,0:T(8,128)(2,1)} %get-tuple-element.172.refs_0_, bf16[4,4,256,512]{3,2,1,0:T(8,128)(2,1)} %collective-permute-done.6.refs_1_, bf16[4,4,256,512]{3,2,1,0:T(8,128)(2,1)} %get-tuple-element.173.refs_2_, bf16[4,4,256,512]{3,2,1,0:T(8,128)(2,1)} %collective-permute-done.7.refs_3_), custom_call_target="tpu_custom_call" | custom-call | flops 1000 | bytes 1000 | tf_op jit(solution)/shard_map/add_pieces/pallas_call | solution.py:647
  122.7 4.3 %collective-permute-start.8 = (bf16[512,512]{1,0:T(8,128)(2,1)}, bf16[512,512]{1,0:T(8,128)(2,1)S(1)}, u32[]{:S(2)}, u32[]{:S(2)}) collective-permute-start(bf16[512,512]{1,0:T(8,128)(2,1)} %get-tuple-element.182), channel_id=1, source_target_pairs={{0,1},{1,2},{2,3},{3,0},{4,5},{5,6},{6,7},{7,4},{8,9},{9,10},{10,1... | collective-permute-start | bytes 1572872 | tf_op jit(solution)/shard_map/ppermute | solution.py:620
  129.5 31.2 %attention.3 = (bf16[512,512]{1,0:T(8,128)(2,1)}, bf16[512,512]{1,0:T(8,128)(2,1)}, bf16[512,512]{1,0:T(8,128)(2,1)}, bf16[512,512]{1,0:T(8,128)(2,1)}) custom-call(s32[2]{0:T(128)} %get-tuple-element.280.refs_0_, bf16[512,512]{1,0:T(8,128)(2,1)} %get-tuple-element.140.refs_1_, bf16[512,512]{1,0:T(8,128)(2,1)} %copy-done.13, bf16[512,512]{1,0:T(8,128)(2,1)} %copy-done.15, ...), custom_call_target="tpu_custom_call" | custom-call | flops 1000 | bytes 1000 | tf_op jit(solution)/shard_map/attention/pallas_call | solution.py:294
  162.2 11.7 %collective-permute-start.11 = (bf16[512,512]{1,0:T(8,128)(2,1)}, bf16[512,512]{1,0:T(8,128)(2,1)S(1)}, u32[]{:S(2)}, u32[]{:S(2)}) collective-permute-start(bf16[512,512]{1,0:T(8,128)(2,1)} %get-tuple-element.185), channel_id=1, source_target_pairs={{0,1},{1,2},{2,3},{3,0},{4,5},{5,6},{6,7},{7,4},{8,9},{9,10},{10,1... | collective-permute-start | bytes 1572872 | tf_op jit(solution)/shard_map/ppermute | solution.py:620
  176.3 8.5 %sums.2 = (f32[512,1024]{1,0:T(8,128)}, f32[512,1024]{1,0:T(8,128)}) custom-call(s32[2]{0:T(128)} %get-tuple-element.279.refs_0_, bf16[512,512]{1,0:T(8,128)(2,1)} %get-tuple-element.197.refs_1_.refs_3_, bf16[512,512]{1,0:T(8,128)(2,1)} %copy-done.7, bf16[512,512]{1,0:T(8,128)(2,1)} %copy-done.8, bf16[512,512]{1,0:T(8,128)(2,1)} %copy-done.9, ...), custom_call_target="tpu_custom_call" | custom-call | flops 1000 | bytes 1000 | tf_op jit(solution)/shard_map/sums/pallas_call | solution.py:524
  184.7 7.2 %weight_grads.2 = (bf16[4,4,128,512]{3,2,1,0:T(8,128)(2,1)}, bf16[4,4,128,512]{3,2,1,0:T(8,128)(2,1)}) custom-call(s32[2]{0:T(128)} %get-tuple-element.279.refs_0_, bf16[1024,512]{1,0:T(8,128)(2,1)} %get-tuple-element.149.turned_ref.refs_1_, bf16[512,1024]{1,0:T(8,128)(2,1)} %bitcast.45, bf16[512,512]{1,0:T(8,128)(2,1)} %get-tuple-element.197.refs_1_.refs_3_, ...), custom_call_target="tpu_custom_call" | custom-call | flops 1000 | bytes 1000 | tf_op jit(solution)/shard_map/weight_grads/pallas_call | solution.py:456
  191.9 17.9 %collective-permute-done.12.refs_5_.refs_3_ = bf16[512,512]{1,0:T(8,128)(2,1)S(1)} collective-permute-done((bf16[512,512]{1,0:T(8,128)(2,1)}, bf16[512,512]{1,0:T(8,128)(2,1)S(1)}, u32[]{:S(2)}, u32[]{:S(2)}) %collective-permute-start.12) | collective-permute-done | bytes 524320 | tf_op jit(solution)/shard_map/ppermute | solution.py:620
  211.1 6.8 %weight_grads.3 = (bf16[4,4,128,512]{3,2,1,0:T(8,128)(2,1)}, bf16[4,4,128,512]{3,2,1,0:T(8,128)(2,1)}) custom-call(s32[2]{0:T(128)} %get-tuple-element.279.refs_0_, bf16[1024,512]{1,0:T(8,128)(2,1)} %get-tuple-element.149.turned_ref.refs_1_, bf16[512,1024]{1,0:T(8,128)(2,1)} %bitcast.46, bf16[512,512]{1,0:T(8,128)(2,1)} %get-tuple-element.215.refs_3_.refs_1_, ...), custom_call_target="tpu_custom_call" | custom-call | flops 1000 | bytes 1000 | tf_op jit(solution)/shard_map/weight_grads/pallas_call | solution.py:456
  226.9 9.8 %sums.3 = (bf16[512,1024]{1,0:T(8,128)(2,1)}, f32[512,1024]{1,0:T(8,128)}, f32[4,256]{1,0:T(4,128)}, f32[4,256]{1,0:T(4,128)}) custom-call(s32[2]{0:T(128)} %get-tuple-element.279.refs_0_, bf16[512,512]{1,0:T(8,128)(2,1)} %get-tuple-element.215.refs_3_.refs_1_, bf16[512,512]{1,0:T(8,128)(2,1)} %copy-done.5, bf16[512,512]{1,0:T(8,128)(2,1)} %copy-done.6, ...), custom_call_target="tpu_custom_call" | custom-call | flops 1000 | bytes 1000 | tf_op jit(solution)/shard_map/sums/pallas_call | solution.py:524
  238.4 11.3 %collective-permute-done.16 = bf16[4,128,512]{2,1,0:T(8,128)(2,1)S(1)} collective-permute-done((bf16[4,128,512]{2,1,0:T(8,128)(2,1)}, bf16[4,128,512]{2,1,0:T(8,128)(2,1)S(1)}, u32[]{:S(2)}, u32[]{:S(2)}) %collective-permute-start.16) | collective-permute-done | bytes 524320 | tf_op jit(solution)/shard_map/ppermute | solution.py:615
  258.4 5.9 %reduce-scatter.5.cloned.1.call-done = bf16[1,512,512]{2,1,0:T(8,128)(2,1)} async-done(((bf16[4,512,512]{2,1,0:T(8,128)(2,1)}), bf16[1,512,512]{2,1,0:T(8,128)(2,1)}) %reduce-scatter.5.cloned.1.call-update) | async-done | bytes 524304 | tf_op jit(solution)/shard_map/reduce_scatter | solution.py:785
  264.3 5.5 %collective-permute-done.20 = bf16[4,128,512]{2,1,0:T(8,128)(2,1)S(1)} collective-permute-done((bf16[4,128,512]{2,1,0:T(8,128)(2,1)}, bf16[4,128,512]{2,1,0:T(8,128)(2,1)S(1)}, u32[]{:S(2)}, u32[]{:S(2)}) %collective-permute-start.20) | collective-permute-done | bytes 524320 | tf_op jit(solution)/shard_map/ppermute | solution.py:615
  269.8 10.6 %collective-permute-done.21 = bf16[4,128,512]{2,1,0:T(8,128)(2,1)S(1)} collective-permute-done((bf16[4,128,512]{2,1,0:T(8,128)(2,1)}, bf16[4,128,512]{2,1,0:T(8,128)(2,1)S(1)}, u32[]{:S(2)}, u32[]{:S(2)}) %collective-permute-start.21) | collective-permute-done | bytes 524320 | tf_op jit(solution)/shard_map/ppermute | solution.py:615
  285.4 10.6 %collective-permute-start.26 = (bf16[2,256,512]{2,1,0:T(8,128)(2,1)S(1)}, bf16[2,256,512]{2,1,0:T(8,128)(2,1)S(1)}, u32[]{:S(2)}, u32[]{:S(2)}) collective-permute-start(bf16[2,256,512]{2,1,0:T(8,128)(2,1)S(1)} %get-tuple-element.269), channel_id=1, source_target_pairs={{0,1},{1,0},{2,3},{3,2},{4,5},{5,4},{6,7},{7,6},{8,9},{9,8},{10,11... | collective-permute-start | bytes 1572872 | tf_op jit(solution)/shard_map/ppermute | solution.py:615
  299.9 5.9 %collective-permute-done.26 = bf16[2,256,512]{2,1,0:T(8,128)(2,1)S(1)} collective-permute-done((bf16[2,256,512]{2,1,0:T(8,128)(2,1)S(1)}, bf16[2,256,512]{2,1,0:T(8,128)(2,1)S(1)}, u32[]{:S(2)}, u32[]{:S(2)}) %collective-permute-start.26) | collective-permute-done | bytes 524320 | tf_op jit(solution)/shard_map/ppermute | solution.py:615
  306.3 4.2 %collective-permute-start.29 = (bf16[1,256,512]{2,1,0:T(8,128)(2,1)S(1)}, bf16[1,256,512]{2,1,0:T(8,128)(2,1)S(1)}, u32[]{:S(2)}, u32[]{:S(2)}) collective-permute-start(bf16[1,256,512]{2,1,0:T(8,128)(2,1)S(1)} %get-tuple-element.271), channel_id=1, source_target_pairs={{0,2},{1,3},{2,0},{3,1},{4,6},{5,7},{6,4},{7,5},{8,10},{9,11},{10,... | collective-permute-start | bytes 786440 | tf_op jit(solution)/shard_map/ppermute | solution.py:615
  311.3 7.1 %collective-permute-done.27 = f32[4,1792]{1,0:T(4,128)S(1)} collective-permute-done((f32[4,1792]{1,0:T(4,128)S(1)}, f32[4,1792]{1,0:T(4,128)S(1)}, u32[]{:S(2)}, u32[]{:S(2)}) %collective-permute-start.27) | collective-permute-done | bytes 28704 | tf_op jit(solution)/shard_map/ppermute | solution.py:615
  325.9 6.1 %place_feed.1 = (f32[256,4096]{1,0:T(8,128)}, f32[1024,1024]{1,0:T(8,128)}) custom-call(s32[2]{0:T(128)} %pad_add_fusion.3.info_ref, bf16[4,512,512]{2,1,0:T(8,128)(2,1)} %copy-done.3, bf16[4,512,512]{2,1,0:T(8,128)(2,1)} %collective-permute-done.31.other_ref), custom_call_target="tpu_custom_call" | custom-call | flops 1000 | bytes 1000 | tf_op jit(solution)/shard_map/place_feed/pallas_call | solution.py:563
  332.0 3.8 %collective-permute-done.33 = bf16[256,512]{1,0:T(8,128)(2,1)S(1)} collective-permute-done((bf16[256,512]{1,0:T(8,128)(2,1)S(1)}, bf16[256,512]{1,0:T(8,128)(2,1)S(1)}, u32[]{:S(2)}, u32[]{:S(2)}) %collective-permute-start.33) | collective-permute-done | bytes 262176 | tf_op jit(solution)/shard_map/ppermute | solution.py:615
  343.1 3.9 %place_heads.1 = (f32[256,3072]{1,0:T(8,128)}, f32[256,1024]{1,0:T(8,128)}) custom-call(s32[2]{0:T(128)} %pad_add_fusion.3.info_ref, bf16[4,256,512]{2,1,0:T(8,128)(2,1)} %copy-done.4, bf16[4,256,512]{2,1,0:T(8,128)(2,1)} %copy-done.10), custom_call_target="tpu_custom_call" | custom-call | flops 1000 | bytes 1000 | tf_op jit(solution)/shard_map/place_heads/pallas_call | solution.py:601
  (146 shorter events, 68.9 us)
Async XLA Ops:
  7.2 203.9 %reduce-scatter.7.cloned.1.call-start = ((), (), s32[]{:S(2)}) async-start(), calls=%async_computation.3 | async-start | bytes 10485760
  26.4 48.5 %collective-permute-start = (bf16[512,512]{1,0:T(8,128)(2,1)}, bf16[512,512]{1,0:T(8,128)(2,1)S(1)}, u32[]{:S(2)}, u32[]{:S(2)}) collective-permute-start(bf16[512,512]{1,0:T(8,128)(2,1)} %get-tuple-element.157), channel_id=1, source_target_pairs={{0,1},{1,2},{2,3},{3,0},{4,5},{5,6},{6,7},{7,4},{8,9},{9,10},{10,1... | collective-permute-start | bytes 1572872 | tf_op jit(solution)/shard_map/ppermute | solution.py:620
  29.5 45.5 %collective-permute-start.1 = (bf16[512,512]{1,0:T(8,128)(2,1)}, bf16[512,512]{1,0:T(8,128)(2,1)S(1)}, u32[]{:S(2)}, u32[]{:S(2)}) collective-permute-start(bf16[512,512]{1,0:T(8,128)(2,1)} %get-tuple-element.158), channel_id=1, source_target_pairs={{0,2},{1,3},{2,0},{3,1},{4,6},{5,7},{6,4},{7,5},{8,10},{9,11},{10,... | collective-permute-start | bytes 1572872 | tf_op jit(solution)/shard_map/ppermute | solution.py:620
  32.1 42.9 %collective-permute-start.2 = (bf16[512,512]{1,0:T(8,128)(2,1)}, bf16[512,512]{1,0:T(8,128)(2,1)S(1)}, u32[]{:S(2)}, u32[]{:S(2)}) collective-permute-start(bf16[512,512]{1,0:T(8,128)(2,1)} %get-tuple-element.159), channel_id=1, source_target_pairs={{0,3},{1,0},{2,1},{3,2},{4,7},{5,4},{6,5},{7,6},{8,11},{9,8},{10,9... | collective-permute-start | bytes 1572872 | tf_op jit(solution)/shard_map/ppermute | solution.py:620
  75.0 37.1 %collective-permute-start.6 = (bf16[4,4,256,512]{3,2,1,0:T(8,128)(2,1)}, bf16[4,4,256,512]{3,2,1,0:T(8,128)(2,1)}, u32[]{:S(2)}, u32[]{:S(2)}) collective-permute-start(bf16[4,4,256,512]{3,2,1,0:T(8,128)(2,1)} %get-tuple-element.170), channel_id=1, source_target_pairs={{0,4},{4,0},{8,12},{12,8},{16,20},{20,16},{24,28},{28,24},{1,5},{5... | collective-permute-start | bytes 12582920 | tf_op jit(solution)/shard_map/ppermute | solution.py:615
  75.1 37.0 %collective-permute-start.7 = (bf16[4,4,256,512]{3,2,1,0:T(8,128)(2,1)}, bf16[4,4,256,512]{3,2,1,0:T(8,128)(2,1)}, u32[]{:S(2)}, u32[]{:S(2)}) collective-permute-start(bf16[4,4,256,512]{3,2,1,0:T(8,128)(2,1)} %get-tuple-element.171), channel_id=1, source_target_pairs={{0,4},{4,0},{8,12},{12,8},{16,20},{20,16},{24,28},{28,24},{1,5},{5... | collective-permute-start | bytes 12582920 | tf_op jit(solution)/shard_map/ppermute | solution.py:615
  75.6 46.0 %collective-permute-start.3 = (bf16[512,512]{1,0:T(8,128)(2,1)}, bf16[512,512]{1,0:T(8,128)(2,1)S(1)}, u32[]{:S(2)}, u32[]{:S(2)}) collective-permute-start(bf16[512,512]{1,0:T(8,128)(2,1)} %get-tuple-element.160), channel_id=1, source_target_pairs={{0,1},{1,2},{2,3},{3,0},{4,5},{5,6},{6,7},{7,4},{8,9},{9,10},{10,1... | collective-permute-start | bytes 1572872 | tf_op jit(solution)/shard_map/ppermute | solution.py:620
  78.5 43.1 %collective-permute-start.4 = (bf16[512,512]{1,0:T(8,128)(2,1)}, bf16[512,512]{1,0:T(8,128)(2,1)S(1)}, u32[]{:S(2)}, u32[]{:S(2)}) collective-permute-start(bf16[512,512]{1,0:T(8,128)(2,1)} %get-tuple-element.161), channel_id=1, source_target_pairs={{0,2},{1,3},{2,0},{3,1},{4,6},{5,7},{6,4},{7,5},{8,10},{9,11},{10,... | collective-permute-start | bytes 1572872 | tf_op jit(solution)/shard_map/ppermute | solution.py:620
  80.1 41.5 %collective-permute-start.5 = (bf16[512,512]{1,0:T(8,128)(2,1)}, bf16[512,512]{1,0:T(8,128)(2,1)S(1)}, u32[]{:S(2)}, u32[]{:S(2)}) collective-permute-start(bf16[512,512]{1,0:T(8,128)(2,1)} %get-tuple-element.162), channel_id=1, source_target_pairs={{0,3},{1,0},{2,1},{3,2},{4,7},{5,4},{6,5},{7,6},{8,11},{9,8},{10,9... | collective-permute-start | bytes 1572872 | tf_op jit(solution)/shard_map/ppermute | solution.py:620
  122.7 141.6 %reduce-scatter.5.cloned.1.call-start = ((), (), s32[]{:S(2)}) async-start(), calls=%async_computation.2 | async-start | bytes 2621440 | tf_op jit(solution)/shard_map/reduce_scatter | solution.py:785
  122.7 38.1 %collective-permute-start.8 = (bf16[512,512]{1,0:T(8,128)(2,1)}, bf16[512,512]{1,0:T(8,128)(2,1)S(1)}, u32[]{:S(2)}, u32[]{:S(2)}) collective-permute-start(bf16[512,512]{1,0:T(8,128)(2,1)} %get-tuple-element.182), channel_id=1, source_target_pairs={{0,1},{1,2},{2,3},{3,0},{4,5},{5,6},{6,7},{7,4},{8,9},{9,10},{10,1... | collective-permute-start | bytes 1572872 | tf_op jit(solution)/shard_map/ppermute | solution.py:620
  127.0 35.2 %collective-permute-start.9 = (bf16[512,512]{1,0:T(8,128)(2,1)}, bf16[512,512]{1,0:T(8,128)(2,1)S(1)}, u32[]{:S(2)}, u32[]{:S(2)}) collective-permute-start(bf16[512,512]{1,0:T(8,128)(2,1)} %get-tuple-element.183), channel_id=1, source_target_pairs={{0,2},{1,3},{2,0},{3,1},{4,6},{5,7},{6,4},{7,5},{8,10},{9,11},{10,... | collective-permute-start | bytes 1572872 | tf_op jit(solution)/shard_map/ppermute | solution.py:620
  128.4 33.8 %collective-permute-start.10 = (bf16[512,512]{1,0:T(8,128)(2,1)}, bf16[512,512]{1,0:T(8,128)(2,1)S(1)}, u32[]{:S(2)}, u32[]{:S(2)}) collective-permute-start(bf16[512,512]{1,0:T(8,128)(2,1)} %get-tuple-element.184), channel_id=1, source_target_pairs={{0,3},{1,0},{2,1},{3,2},{4,7},{5,4},{6,5},{7,6},{8,11},{9,8},{10,9... | collective-permute-start | bytes 1572872 | tf_op jit(solution)/shard_map/ppermute | solution.py:620
  162.2 29.7 %collective-permute-start.11 = (bf16[512,512]{1,0:T(8,128)(2,1)}, bf16[512,512]{1,0:T(8,128)(2,1)S(1)}, u32[]{:S(2)}, u32[]{:S(2)}) collective-permute-start(bf16[512,512]{1,0:T(8,128)(2,1)} %get-tuple-element.185), channel_id=1, source_target_pairs={{0,1},{1,2},{2,3},{3,0},{4,5},{5,6},{6,7},{7,4},{8,9},{9,10},{10,1... | collective-permute-start | bytes 1572872 | tf_op jit(solution)/shard_map/ppermute | solution.py:620
  173.9 36.0 %collective-permute-start.12 = (bf16[512,512]{1,0:T(8,128)(2,1)}, bf16[512,512]{1,0:T(8,128)(2,1)S(1)}, u32[]{:S(2)}, u32[]{:S(2)}) collective-permute-start(bf16[512,512]{1,0:T(8,128)(2,1)} %get-tuple-element.186), channel_id=1, source_target_pairs={{0,2},{1,3},{2,0},{3,1},{4,6},{5,7},{6,4},{7,5},{8,10},{9,11},{10,... | collective-permute-start | bytes 1572872 | tf_op jit(solution)/shard_map/ppermute | solution.py:620
  176.0 33.8 %collective-permute-start.13 = (bf16[512,512]{1,0:T(8,128)(2,1)}, bf16[512,512]{1,0:T(8,128)(2,1)}, u32[]{:S(2)}, u32[]{:S(2)}) collective-permute-start(bf16[512,512]{1,0:T(8,128)(2,1)} %get-tuple-element.187), channel_id=1, source_target_pairs={{0,3},{1,0},{2,1},{3,2},{4,7},{5,4},{6,5},{7,6},{8,11},{9,8},{10,9... | collective-permute-start | bytes 1572872 | tf_op jit(solution)/shard_map/ppermute | solution.py:620
  222.9 26.9 %collective-permute-start.18 = (bf16[4,4,128,512]{3,2,1,0:T(8,128)(2,1)}, bf16[4,4,128,512]{3,2,1,0:T(8,128)(2,1)S(1)}, u32[]{:S(2)}, u32[]{:S(2)}) collective-permute-start(bf16[4,4,128,512]{3,2,1,0:T(8,128)(2,1)} %get-tuple-element.227), channel_id=1, source_target_pairs={{0,4},{4,0},{8,12},{12,8},{16,20},{20,16},{24,28},{28,24},{1,5},{5... | collective-permute-start | bytes 6291464 | tf_op jit(solution)/shard_map/ppermute | solution.py:615
  224.7 25.0 %collective-permute-start.16 = (bf16[4,128,512]{2,1,0:T(8,128)(2,1)}, bf16[4,128,512]{2,1,0:T(8,128)(2,1)S(1)}, u32[]{:S(2)}, u32[]{:S(2)}) collective-permute-start(bf16[4,128,512]{2,1,0:T(8,128)(2,1)} %get-tuple-element.225), channel_id=1, source_target_pairs={{0,16},{4,20},{8,24},{12,28},{16,0},{20,4},{24,8},{28,12},{1,17},{... | collective-permute-start | bytes 1572872 | tf_op jit(solution)/shard_map/ppermute | solution.py:615
  225.4 24.3 %collective-permute-start.17 = (bf16[4,128,512]{2,1,0:T(8,128)(2,1)}, bf16[4,128,512]{2,1,0:T(8,128)(2,1)}, u32[]{:S(2)}, u32[]{:S(2)}) collective-permute-start(bf16[4,128,512]{2,1,0:T(8,128)(2,1)} %get-tuple-element.226), channel_id=1, source_target_pairs={{0,24},{4,28},{8,16},{12,20},{16,8},{20,12},{24,0},{28,4},{1,25},{... | collective-permute-start | bytes 1572872 | tf_op jit(solution)/shard_map/ppermute | solution.py:615
  255.7 24.7 %collective-permute-start.21 = (bf16[4,128,512]{2,1,0:T(8,128)(2,1)}, bf16[4,128,512]{2,1,0:T(8,128)(2,1)S(1)}, u32[]{:S(2)}, u32[]{:S(2)}) collective-permute-start(bf16[4,128,512]{2,1,0:T(8,128)(2,1)} %get-tuple-element.236), channel_id=1, source_target_pairs={{0,16},{4,20},{8,24},{12,28},{16,0},{20,4},{24,8},{28,12},{1,17},{... | collective-permute-start | bytes 1572872 | tf_op jit(solution)/shard_map/ppermute | solution.py:615
  256.8 23.7 %collective-permute-start.22 = (bf16[4,128,512]{2,1,0:T(8,128)(2,1)}, bf16[4,128,512]{2,1,0:T(8,128)(2,1)S(1)}, u32[]{:S(2)}, u32[]{:S(2)}) collective-permute-start(bf16[4,128,512]{2,1,0:T(8,128)(2,1)} %get-tuple-element.237), channel_id=1, source_target_pairs={{0,24},{4,28},{8,16},{12,20},{16,8},{20,12},{24,0},{28,4},{1,25},{... | collective-permute-start | bytes 1572872 | tf_op jit(solution)/shard_map/ppermute | solution.py:615
  283.5 16.4 %collective-permute-start.24 = (bf16[512,512]{1,0:T(8,128)(2,1)S(1)}, bf16[512,512]{1,0:T(8,128)(2,1)S(1)}, u32[]{:S(2)}, u32[]{:S(2)}) collective-permute-start(bf16[512,512]{1,0:T(8,128)(2,1)S(1)} %bitcast.55), channel_id=1, source_target_pairs={{0,8},{4,12},{8,0},{12,4},{16,24},{20,28},{24,16},{28,20},{1,9},{5... | collective-permute-start | bytes 1572872 | tf_op jit(solution)/shard_map/ppermute | solution.py:615
  283.9 16.0 %collective-permute-start.25 = (bf16[512,512]{1,0:T(8,128)(2,1)S(1)}, bf16[512,512]{1,0:T(8,128)(2,1)S(1)}, u32[]{:S(2)}, u32[]{:S(2)}) collective-permute-start(bf16[512,512]{1,0:T(8,128)(2,1)S(1)} %bitcast.56), channel_id=1, source_target_pairs={{0,16},{4,20},{8,24},{12,28},{16,0},{20,4},{24,8},{28,12},{1,17},{... | collective-permute-start | bytes 1572872 | tf_op jit(solution)/shard_map/ppermute | solution.py:615
  285.4 20.4 %collective-permute-start.26 = (bf16[2,256,512]{2,1,0:T(8,128)(2,1)S(1)}, bf16[2,256,512]{2,1,0:T(8,128)(2,1)S(1)}, u32[]{:S(2)}, u32[]{:S(2)}) collective-permute-start(bf16[2,256,512]{2,1,0:T(8,128)(2,1)S(1)} %get-tuple-element.269), channel_id=1, source_target_pairs={{0,1},{1,0},{2,3},{3,2},{4,5},{5,4},{6,7},{7,6},{8,9},{9,8},{10,11... | collective-permute-start | bytes 1572872 | tf_op jit(solution)/shard_map/ppermute | solution.py:615
  (37 other events, 331.6 us)
Sparse Core Ops, SparseCore 0:
  121.8 89.2 reduce-scatter.6
  213.5 50.7 reduce-scatter.4

commit v7 on v6

--- a/solution.py
+++ b/solution.py
@@ -601,10 +601,10 @@
     return pl.pallas_call(
         heads_place_kernel,
         grid=(1,),
-        in_specs=[SCALARS, whole(mine), whole(other)],
+        in_specs=[SCALARS] + [pl.BlockSpec(memory_space=pltpu.VMEM)] * 2,
         out_specs=[whole(shape) for shape in shapes],
         out_shape=shapes,
-        compiler_params=pltpu.CompilerParams(vmem_limit_bytes=60 * MIB),
+        compiler_params=pltpu.CompilerParams(vmem_limit_bytes=40 * MIB),
         cost_estimate=SHORT,
         name="place_heads",
     )(info, mine, other)
@@ -656,30 +656,34 @@
     )(*arrays)
 
 
+def chips_kernel(chip_ref, *refs):
+    chips = (len(refs) - 1) // 2
+    arrived_ref = refs[chips]
+    for mask in range(chips):
+        total = refs[mask][0].astype(F32) + arrived_ref[chip_ref[0] ^ mask].astype(F32)
+        refs[chips + 1 + mask][...] = total.astype(BF16)
+
+
 def add_for_chips(chip, kept, arrived):
-    specs, places, arrays = [], [], []
-    chips, owners = kept[0].shape[:2]
-    for mask in range(chips):
-        terms = []
-        for mine, other in zip(kept, arrived):
-            terms.append((len(arrays), len(arrays) + 1))
-            arrays += [mine, other]
-            specs += [pl.BlockSpec((1,) + mine.shape[1:], lambda i, c, mask=mask: (c[0] ^ mask, 0, 0, 0))] * 2
-        places.append(terms)
-    rows = sum(array.shape[2] for array in kept)
-    out = jax.ShapeDtypeStruct((owners, rows, kept[0].shape[3]), BF16)
+    chips = kept.shape[0]
+    block = (1,) + kept.shape[1:]
+    out = jax.ShapeDtypeStruct(kept.shape[1:], BF16)
     return pl.pallas_call(
-        lambda *refs: add_kernel(places, *refs),
+        chips_kernel,
         grid_spec=pltpu.PrefetchScalarGridSpec(
             num_scalar_prefetch=1,
             grid=(1,),
-            in_specs=specs,
+            in_specs=[
+                pl.BlockSpec(block, lambda i, c, mask=mask: (c[0] ^ mask, 0, 0, 0)) for mask in range(chips)
+            ]
+            + [pl.BlockSpec(memory_space=pltpu.VMEM)],
             out_specs=[pl.BlockSpec(out.shape, lambda i, c: (0, 0, 0))] * chips,
         ),
         out_shape=[out] * chips,
+        compiler_params=pltpu.CompilerParams(vmem_limit_bytes=40 * MIB),
         cost_estimate=SHORT,
         name="add_for_chips",
-    )(chip[None], *arrays)
+    )(chip[None], *([kept] * chips), arrived)
 
 
 class Order:
@@ -787,7 +791,7 @@
     parts = gathered(second, order(later))
     second_kept, second_sent = order.done(weight_grads(info, turned, cot, parts, pieces // 2))
     order.also(grad_arrived)
-    first_held = order.done(add_for_chips(place >> 1, [order(first_kept)], [grad_arrived]))
+    first_held = order.done(add_for_chips(place >> 1, order(first_kept), grad_arrived))
 
     first_arrived = [exchange(order(first_held[mask]), "batch", 2 * mask) for mask in (1, 2, 3)]
     grad_arrived = exchange(order(second_sent), "batch", 1)
@@ -797,7 +801,7 @@
         )
     )
     order.also(first_arrived, grad_arrived)
-    second_held = order.done(add_for_chips(place >> 1, [order(second_kept)], [grad_arrived]))
+    second_held = order.done(add_for_chips(place >> 1, order(second_kept), grad_arrived))
 
     def halve_seq(rows, number):
         bit = (me >> number) & 1

time: 354 us -> 350 us (0.989)
  local copies, waits for them, and re-layouts: 6.92 us -> 3.12 us
    reduce_scatter x1, waiting for transfers between devices: 5.87 us -> 9.79 us  [fast_body(): lax.psum_scatter(order(feed_rows), 'seq', scatter_dimension=0, tiled=False)]
    unnamed x48 -> x44, local copies, waits for them, and re-layouts: 4.82 us -> 1.02 us
where the time goes in v7:
time: 350 us
  Pallas kernels  175 us (50%)
  waiting for transfers between devices  80.7 us (23%)
  starting transfers between devices  66.3 us (19%)
  between operations  15.8 us (5%)
  other arithmetic  8.32 us (2%)
    pallas_call x2, Pallas kernels, attention(): pl.pallas_call(lambda *refs: attention_kernel(pieces, *refs), grid=(1,),...  61.4 us
    ppermute x25, waiting for transfers between devices, exchange(): lax.ppermute(rows, axis, [(place, place ^ mask) for place in range(size)])  49.6 us
    pallas_call x1, Pallas kernels, feed_forward(): pl.pallas_call(feed_kernel, grid_spec=pltpu.PrefetchScalarGridSpec(num_sc...  40.9 us
    ppermute x25, starting transfers between devices, exchange(): lax.ppermute(rows, axis, [(place, place ^ mask) for place in range(size)])  33.5 us
    ppermute x12, starting transfers between devices, around(): lax.ppermute(rows, 'seq', [(place, (place + shift) % owners) for place in...  32.7 us
    ppermute x12, waiting for transfers between devices, around(): lax.ppermute(rows, 'seq', [(place, (place + shift) % owners) for place in...  19.6 us
    pallas_call x2, Pallas kernels, sums_of(): pl.pallas_call(lambda *refs: sums_kernel(last, owners, *refs), grid=(1,),...  18.8 us
    pallas_call x2, Pallas kernels, weight_grads(): pl.pallas_call(lambda *refs: weight_kernel(pieces, *refs), grid=(1,), in_...  14.3 us
  transfers between devices with their start and end apart: 39, of which 14 were waited for; matrix products, arithmetic and copies ran while one was open for 1% of the time, Pallas kernels for 45%

profile of v7, /device:TPU:0, one launch (start us, length us, event | category | flops | bytes accessed | tf_op | source)
XLA Modules:
  0.0 349.5 jit_solution(4731772720093796643)
XLA Ops:
  10.7 4.6 %prep.1 = (f32[512,1024]{1,0:T(8,128)}, bf16[512,1024]{1,0:T(8,128)(2,1)}, bf16[1024,512]{1,0:T(8,128)(2,1)}) custom-call(bf16[512,1024]{1,0:T(8,128)(2,1)} %bitcast.51, s32[512,1]{1,0:T(8,128)} %select_select_fusion.mark_ref, bf16[32,1024]{1,0:T(8,128)(2,1)} %table_ref.1, f32[1,1024]{1,0:T(1,128)} %bitcast.65, f32[1,1024]{1,0:T(1,128)} %bitcast.67), custom_call_target="tpu_custom_call" | custom-call | flops 1000 | bytes 1000 | tf_op jit(solution)/shard_map/prep/pallas_call | solution.py:77
  15.2 11.2 %heads.1 = (bf16[512,512]{1,0:T(8,128)(2,1)}, bf16[512,512]{1,0:T(8,128)(2,1)}, bf16[512,512]{1,0:T(8,128)(2,1)}, bf16[512,512]{1,0:T(8,128)(2,1)}, bf16[512,512...) custom-call(s32[4]{0:T(128)} %compare_select_fusion.owners_ref, ...), custom_call_target="tpu_custom_call" | custom-call | flops 1000 | bytes 1000 | tf_op jit(solution)/shard_map/heads/pallas_call | solution.py:138
  26.4 3.0 collective-permute-start
  34.0 40.9 %feed.1 = (bf16[4,4,256,512]{3,2,1,0:T(8,128)(2,1)}, bf16[4,4,256,512]{3,2,1,0:T(8,128)(2,1)}, bf16[4,4,256,512]{3,2,1,0:T(8,128)(2,1)}, bf16[4,4,256,512]{3,2,1...) custom-call(s32[8]{0:T(128)} %pad_add_fusion.2.cells_ref, ...), custom_call_target="tpu_custom_call" | custom-call | flops 1000 | bytes 1000 | tf_op jit(solution)/shard_map/feed/pallas_call | solution.py:390
  81.4 30.6 %attention.2 = (bf16[512,512]{1,0:T(8,128)(2,1)}, bf16[512,512]{1,0:T(8,128)(2,1)}, bf16[512,512]{1,0:T(8,128)(2,1)}, bf16[512,512]{1,0:T(8,128)(2,1)}) custom-call(s32[2]{0:T(128)} %get-tuple-element.280.refs_0_, bf16[512,512]{1,0:T(8,128)(2,1)} %get-tuple-element.144.refs_1_, bf16[512,512]{1,0:T(8,128)(2,1)} %copy-done.11, bf16[512,512]{1,0:T(8,128)(2,1)} %copy-done.13, ...), custom_call_target="tpu_custom_call" | custom-call | flops 1000 | bytes 1000 | tf_op jit(solution)/shard_map/attention/pallas_call | solution.py:294
  112.1 9.5 %add_pieces.1 = bf16[4,4,512,512]{3,2,1,0:T(8,128)(2,1)} custom-call(bf16[4,4,256,512]{3,2,1,0:T(8,128)(2,1)} %get-tuple-element.172.refs_0_, bf16[4,4,256,512]{3,2,1,0:T(8,128)(2,1)} %collective-permute-done.6.refs_1_, bf16[4,4,256,512]{3,2,1,0:T(8,128)(2,1)} %get-tuple-element.173.refs_2_, bf16[4,4,256,512]{3,2,1,0:T(8,128)(2,1)} %collective-permute-done.7.refs_3_), custom_call_target="tpu_custom_call" | custom-call | flops 1000 | bytes 1000 | tf_op jit(solution)/shard_map/add_pieces/pallas_call | solution.py:647
  122.5 4.0 %collective-permute-start.8 = (bf16[512,512]{1,0:T(8,128)(2,1)}, bf16[512,512]{1,0:T(8,128)(2,1)S(1)}, u32[]{:S(2)}, u32[]{:S(2)}) collective-permute-start(bf16[512,512]{1,0:T(8,128)(2,1)} %get-tuple-element.182), channel_id=1, source_target_pairs={{0,1},{1,2},{2,3},{3,0},{4,5},{5,6},{6,7},{7,4},{8,9},{9,10},{10,1... | collective-permute-start | bytes 1572872 | tf_op jit(solution)/shard_map/ppermute | solution.py:620
  128.9 30.7 %attention.3 = (bf16[512,512]{1,0:T(8,128)(2,1)}, bf16[512,512]{1,0:T(8,128)(2,1)}, bf16[512,512]{1,0:T(8,128)(2,1)}, bf16[512,512]{1,0:T(8,128)(2,1)}) custom-call(s32[2]{0:T(128)} %get-tuple-element.280.refs_0_, bf16[512,512]{1,0:T(8,128)(2,1)} %get-tuple-element.140.refs_1_, bf16[512,512]{1,0:T(8,128)(2,1)} %copy-done.12, bf16[512,512]{1,0:T(8,128)(2,1)} %copy-done.14, ...), custom_call_target="tpu_custom_call" | custom-call | flops 1000 | bytes 1000 | tf_op jit(solution)/shard_map/attention/pallas_call | solution.py:294
  162.0 11.7 %collective-permute-start.11 = (bf16[512,512]{1,0:T(8,128)(2,1)}, bf16[512,512]{1,0:T(8,128)(2,1)S(1)}, u32[]{:S(2)}, u32[]{:S(2)}) collective-permute-start(bf16[512,512]{1,0:T(8,128)(2,1)} %get-tuple-element.185), channel_id=1, source_target_pairs={{0,1},{1,2},{2,3},{3,0},{4,5},{5,6},{6,7},{7,4},{8,9},{9,10},{10,1... | collective-permute-start | bytes 1572872 | tf_op jit(solution)/shard_map/ppermute | solution.py:620
  176.1 8.5 %sums.2 = (f32[512,1024]{1,0:T(8,128)}, f32[512,1024]{1,0:T(8,128)}) custom-call(s32[2]{0:T(128)} %get-tuple-element.279.refs_0_, bf16[512,512]{1,0:T(8,128)(2,1)} %get-tuple-element.197.refs_1_.refs_3_, bf16[512,512]{1,0:T(8,128)(2,1)} %copy-done.8, bf16[512,512]{1,0:T(8,128)(2,1)} %copy-done.9, bf16[512,512]{1,0:T(8,128)(2,1)} %copy-done.10, ...), custom_call_target="tpu_custom_call" | custom-call | flops 1000 | bytes 1000 | tf_op jit(solution)/shard_map/sums/pallas_call | solution.py:524
  184.6 7.3 %weight_grads.2 = (bf16[4,4,128,512]{3,2,1,0:T(8,128)(2,1)}, bf16[4,4,128,512]{3,2,1,0:T(8,128)(2,1)}) custom-call(s32[2]{0:T(128)} %get-tuple-element.279.refs_0_, bf16[1024,512]{1,0:T(8,128)(2,1)} %get-tuple-element.149.turned_ref.refs_1_, bf16[512,1024]{1,0:T(8,128)(2,1)} %bitcast.45, bf16[512,512]{1,0:T(8,128)(2,1)} %get-tuple-element.197.refs_1_.refs_3_, ...), custom_call_target="tpu_custom_call" | custom-call | flops 1000 | bytes 1000 | tf_op jit(solution)/shard_map/weight_grads/pallas_call | solution.py:456
  191.9 17.4 %collective-permute-done.12.refs_5_.refs_3_ = bf16[512,512]{1,0:T(8,128)(2,1)S(1)} collective-permute-done((bf16[512,512]{1,0:T(8,128)(2,1)}, bf16[512,512]{1,0:T(8,128)(2,1)S(1)}, u32[]{:S(2)}, u32[]{:S(2)}) %collective-permute-start.12) | collective-permute-done | bytes 524320 | tf_op jit(solution)/shard_map/ppermute | solution.py:620
  211.1 7.0 %weight_grads.3 = (bf16[4,4,128,512]{3,2,1,0:T(8,128)(2,1)}, bf16[4,4,128,512]{3,2,1,0:T(8,128)(2,1)}) custom-call(s32[2]{0:T(128)} %get-tuple-element.279.refs_0_, bf16[1024,512]{1,0:T(8,128)(2,1)} %get-tuple-element.149.turned_ref.refs_1_, bf16[512,1024]{1,0:T(8,128)(2,1)} %bitcast.46, bf16[512,512]{1,0:T(8,128)(2,1)} %get-tuple-element.215.refs_3_.refs_1_, ...), custom_call_target="tpu_custom_call" | custom-call | flops 1000 | bytes 1000 | tf_op jit(solution)/shard_map/weight_grads/pallas_call | solution.py:456
  224.9 10.3 %sums.3 = (bf16[512,1024]{1,0:T(8,128)(2,1)}, f32[512,1024]{1,0:T(8,128)}, f32[4,256]{1,0:T(4,128)}, f32[4,256]{1,0:T(4,128)}) custom-call(s32[2]{0:T(128)} %get-tuple-element.279.refs_0_, bf16[512,512]{1,0:T(8,128)(2,1)} %get-tuple-element.215.refs_3_.refs_1_, bf16[512,512]{1,0:T(8,128)(2,1)} %copy-done.5, bf16[512,512]{1,0:T(8,128)(2,1)} %copy-done.6, ...), custom_call_target="tpu_custom_call" | custom-call | flops 1000 | bytes 1000 | tf_op jit(solution)/shard_map/sums/pallas_call | solution.py:524
  237.4 10.3 %collective-permute-done.17 = bf16[4,128,512]{2,1,0:T(8,128)(2,1)} collective-permute-done((bf16[4,128,512]{2,1,0:T(8,128)(2,1)S(1)}, bf16[4,128,512]{2,1,0:T(8,128)(2,1)}, u32[]{:S(2)}, u32[]{:S(2)}) %collective-permute-start.17) | collective-permute-done | bytes 524320 | tf_op jit(solution)/shard_map/ppermute | solution.py:615
  254.4 9.8 %reduce-scatter.5.cloned.1.call-done = bf16[1,512,512]{2,1,0:T(8,128)(2,1)} async-done(((bf16[4,512,512]{2,1,0:T(8,128)(2,1)}), bf16[1,512,512]{2,1,0:T(8,128)(2,1)}) %reduce-scatter.5.cloned.1.call-update) | async-done | bytes 524304 | tf_op jit(solution)/shard_map/reduce_scatter | solution.py:789
  265.7 10.1 %collective-permute-done.21 = bf16[4,128,512]{2,1,0:T(8,128)(2,1)S(1)} collective-permute-done((bf16[4,128,512]{2,1,0:T(8,128)(2,1)}, bf16[4,128,512]{2,1,0:T(8,128)(2,1)S(1)}, u32[]{:S(2)}, u32[]{:S(2)}) %collective-permute-start.21) | collective-permute-done | bytes 524320 | tf_op jit(solution)/shard_map/ppermute | solution.py:615
  281.2 12.0 %collective-permute-start.26 = (bf16[2,256,512]{2,1,0:T(8,128)(2,1)S(1)}, bf16[2,256,512]{2,1,0:T(8,128)(2,1)S(1)}, u32[]{:S(2)}, u32[]{:S(2)}) collective-permute-start(bf16[2,256,512]{2,1,0:T(8,128)(2,1)S(1)} %get-tuple-element.269), channel_id=1, source_target_pairs={{0,1},{1,0},{2,3},{3,2},{4,5},{5,4},{6,7},{7,6},{8,9},{9,8},{10,11... | collective-permute-start | bytes 1572872 | tf_op jit(solution)/shard_map/ppermute | solution.py:615
  293.8 3.2 collective-permute-done.23
  297.0 6.4 %collective-permute-done.26 = bf16[2,256,512]{2,1,0:T(8,128)(2,1)S(1)} collective-permute-done((bf16[2,256,512]{2,1,0:T(8,128)(2,1)S(1)}, bf16[2,256,512]{2,1,0:T(8,128)(2,1)S(1)}, u32[]{:S(2)}, u32[]{:S(2)}) %collective-permute-start.26) | collective-permute-done | bytes 524320 | tf_op jit(solution)/shard_map/ppermute | solution.py:615
  307.8 8.7 %collective-permute-done.27 = f32[4,1792]{1,0:T(4,128)S(1)} collective-permute-done((f32[4,1792]{1,0:T(4,128)S(1)}, f32[4,1792]{1,0:T(4,128)S(1)}, u32[]{:S(2)}, u32[]{:S(2)}) %collective-permute-start.27) | collective-permute-done | bytes 28704 | tf_op jit(solution)/shard_map/ppermute | solution.py:615
  323.6 6.1 %place_feed.1 = (f32[256,4096]{1,0:T(8,128)}, f32[1024,1024]{1,0:T(8,128)}) custom-call(s32[2]{0:T(128)} %pad_add_fusion.3.info_ref, bf16[4,512,512]{2,1,0:T(8,128)(2,1)} %copy-done.4, bf16[4,512,512]{2,1,0:T(8,128)(2,1)} %collective-permute-done.31.other_ref), custom_call_target="tpu_custom_call" | custom-call | flops 1000 | bytes 1000 | tf_op jit(solution)/shard_map/place_feed/pallas_call | solution.py:563
  329.8 3.4 collective-permute-done.33
  334.9 3.8 %collective-permute-done.35 = f32[4,1792]{1,0:T(4,128)S(1)} collective-permute-done((f32[4,1792]{1,0:T(4,128)S(1)}, f32[4,1792]{1,0:T(4,128)S(1)}, u32[]{:S(2)}, u32[]{:S(2)}) %collective-permute-start.35) | collective-permute-done | bytes 28704 | tf_op jit(solution)/shard_map/ppermute | solution.py:615
  (142 shorter events, 63.4 us)
Async XLA Ops:
  7.2 203.9 %reduce-scatter.7.cloned.1.call-start = ((), (), s32[]{:S(2)}) async-start(), calls=%async_computation.3 | async-start | bytes 10485760
  26.4 48.5 %collective-permute-start = (bf16[512,512]{1,0:T(8,128)(2,1)}, bf16[512,512]{1,0:T(8,128)(2,1)S(1)}, u32[]{:S(2)}, u32[]{:S(2)}) collective-permute-start(bf16[512,512]{1,0:T(8,128)(2,1)} %get-tuple-element.157), channel_id=1, source_target_pairs={{0,1},{1,2},{2,3},{3,0},{4,5},{5,6},{6,7},{7,4},{8,9},{9,10},{10,1... | collective-permute-start | bytes 1572872 | tf_op jit(solution)/shard_map/ppermute | solution.py:620
  29.5 45.5 %collective-permute-start.1 = (bf16[512,512]{1,0:T(8,128)(2,1)}, bf16[512,512]{1,0:T(8,128)(2,1)S(1)}, u32[]{:S(2)}, u32[]{:S(2)}) collective-permute-start(bf16[512,512]{1,0:T(8,128)(2,1)} %get-tuple-element.158), channel_id=1, source_target_pairs={{0,2},{1,3},{2,0},{3,1},{4,6},{5,7},{6,4},{7,5},{8,10},{9,11},{10,... | collective-permute-start | bytes 1572872 | tf_op jit(solution)/shard_map/ppermute | solution.py:620
  32.0 42.9 %collective-permute-start.2 = (bf16[512,512]{1,0:T(8,128)(2,1)}, bf16[512,512]{1,0:T(8,128)(2,1)S(1)}, u32[]{:S(2)}, u32[]{:S(2)}) collective-permute-start(bf16[512,512]{1,0:T(8,128)(2,1)} %get-tuple-element.159), channel_id=1, source_target_pairs={{0,3},{1,0},{2,1},{3,2},{4,7},{5,4},{6,5},{7,6},{8,11},{9,8},{10,9... | collective-permute-start | bytes 1572872 | tf_op jit(solution)/shard_map/ppermute | solution.py:620
  75.0 37.1 %collective-permute-start.6 = (bf16[4,4,256,512]{3,2,1,0:T(8,128)(2,1)}, bf16[4,4,256,512]{3,2,1,0:T(8,128)(2,1)}, u32[]{:S(2)}, u32[]{:S(2)}) collective-permute-start(bf16[4,4,256,512]{3,2,1,0:T(8,128)(2,1)} %get-tuple-element.170), channel_id=1, source_target_pairs={{0,4},{4,0},{8,12},{12,8},{16,20},{20,16},{24,28},{28,24},{1,5},{5... | collective-permute-start | bytes 12582920 | tf_op jit(solution)/shard_map/ppermute | solution.py:615
  75.0 37.0 %collective-permute-start.7 = (bf16[4,4,256,512]{3,2,1,0:T(8,128)(2,1)}, bf16[4,4,256,512]{3,2,1,0:T(8,128)(2,1)}, u32[]{:S(2)}, u32[]{:S(2)}) collective-permute-start(bf16[4,4,256,512]{3,2,1,0:T(8,128)(2,1)} %get-tuple-element.171), channel_id=1, source_target_pairs={{0,4},{4,0},{8,12},{12,8},{16,20},{20,16},{24,28},{28,24},{1,5},{5... | collective-permute-start | bytes 12582920 | tf_op jit(solution)/shard_map/ppermute | solution.py:615
  75.5 46.0 %collective-permute-start.3 = (bf16[512,512]{1,0:T(8,128)(2,1)}, bf16[512,512]{1,0:T(8,128)(2,1)S(1)}, u32[]{:S(2)}, u32[]{:S(2)}) collective-permute-start(bf16[512,512]{1,0:T(8,128)(2,1)} %get-tuple-element.160), channel_id=1, source_target_pairs={{0,1},{1,2},{2,3},{3,0},{4,5},{5,6},{6,7},{7,4},{8,9},{9,10},{10,1... | collective-permute-start | bytes 1572872 | tf_op jit(solution)/shard_map/ppermute | solution.py:620
  78.4 43.1 %collective-permute-start.4 = (bf16[512,512]{1,0:T(8,128)(2,1)}, bf16[512,512]{1,0:T(8,128)(2,1)S(1)}, u32[]{:S(2)}, u32[]{:S(2)}) collective-permute-start(bf16[512,512]{1,0:T(8,128)(2,1)} %get-tuple-element.161), channel_id=1, source_target_pairs={{0,2},{1,3},{2,0},{3,1},{4,6},{5,7},{6,4},{7,5},{8,10},{9,11},{10,... | collective-permute-start | bytes 1572872 | tf_op jit(solution)/shard_map/ppermute | solution.py:620
  80.1 41.5 %collective-permute-start.5 = (bf16[512,512]{1,0:T(8,128)(2,1)}, bf16[512,512]{1,0:T(8,128)(2,1)}, u32[]{:S(2)}, u32[]{:S(2)}) collective-permute-start(bf16[512,512]{1,0:T(8,128)(2,1)} %get-tuple-element.162), channel_id=1, source_target_pairs={{0,3},{1,0},{2,1},{3,2},{4,7},{5,4},{6,5},{7,6},{8,11},{9,8},{10,9... | collective-permute-start | bytes 1572872 | tf_op jit(solution)/shard_map/ppermute | solution.py:620
  122.5 141.6 %reduce-scatter.5.cloned.1.call-start = ((), (), s32[]{:S(2)}) async-start(), calls=%async_computation.2 | async-start | bytes 2621440 | tf_op jit(solution)/shard_map/reduce_scatter | solution.py:789
  122.5 37.3 %collective-permute-start.8 = (bf16[512,512]{1,0:T(8,128)(2,1)}, bf16[512,512]{1,0:T(8,128)(2,1)S(1)}, u32[]{:S(2)}, u32[]{:S(2)}) collective-permute-start(bf16[512,512]{1,0:T(8,128)(2,1)} %get-tuple-element.182), channel_id=1, source_target_pairs={{0,1},{1,2},{2,3},{3,0},{4,5},{5,6},{6,7},{7,4},{8,9},{9,10},{10,1... | collective-permute-start | bytes 1572872 | tf_op jit(solution)/shard_map/ppermute | solution.py:620
  126.5 35.5 %collective-permute-start.9 = (bf16[512,512]{1,0:T(8,128)(2,1)}, bf16[512,512]{1,0:T(8,128)(2,1)S(1)}, u32[]{:S(2)}, u32[]{:S(2)}) collective-permute-start(bf16[512,512]{1,0:T(8,128)(2,1)} %get-tuple-element.183), channel_id=1, source_target_pairs={{0,2},{1,3},{2,0},{3,1},{4,6},{5,7},{6,4},{7,5},{8,10},{9,11},{10,... | collective-permute-start | bytes 1572872 | tf_op jit(solution)/shard_map/ppermute | solution.py:620
  128.2 33.8 %collective-permute-start.10 = (bf16[512,512]{1,0:T(8,128)(2,1)}, bf16[512,512]{1,0:T(8,128)(2,1)S(1)}, u32[]{:S(2)}, u32[]{:S(2)}) collective-permute-start(bf16[512,512]{1,0:T(8,128)(2,1)} %get-tuple-element.184), channel_id=1, source_target_pairs={{0,3},{1,0},{2,1},{3,2},{4,7},{5,4},{6,5},{7,6},{8,11},{9,8},{10,9... | collective-permute-start | bytes 1572872 | tf_op jit(solution)/shard_map/ppermute | solution.py:620
  162.0 29.9 %collective-permute-start.11 = (bf16[512,512]{1,0:T(8,128)(2,1)}, bf16[512,512]{1,0:T(8,128)(2,1)S(1)}, u32[]{:S(2)}, u32[]{:S(2)}) collective-permute-start(bf16[512,512]{1,0:T(8,128)(2,1)} %get-tuple-element.185), channel_id=1, source_target_pairs={{0,1},{1,2},{2,3},{3,0},{4,5},{5,6},{6,7},{7,4},{8,9},{9,10},{10,1... | collective-permute-start | bytes 1572872 | tf_op jit(solution)/shard_map/ppermute | solution.py:620
  173.7 35.6 %collective-permute-start.12 = (bf16[512,512]{1,0:T(8,128)(2,1)}, bf16[512,512]{1,0:T(8,128)(2,1)S(1)}, u32[]{:S(2)}, u32[]{:S(2)}) collective-permute-start(bf16[512,512]{1,0:T(8,128)(2,1)} %get-tuple-element.186), channel_id=1, source_target_pairs={{0,2},{1,3},{2,0},{3,1},{4,6},{5,7},{6,4},{7,5},{8,10},{9,11},{10,... | collective-permute-start | bytes 1572872 | tf_op jit(solution)/shard_map/ppermute | solution.py:620
  175.5 33.8 %collective-permute-start.13 = (bf16[512,512]{1,0:T(8,128)(2,1)}, bf16[512,512]{1,0:T(8,128)(2,1)S(1)}, u32[]{:S(2)}, u32[]{:S(2)}) collective-permute-start(bf16[512,512]{1,0:T(8,128)(2,1)} %get-tuple-element.187), channel_id=1, source_target_pairs={{0,3},{1,0},{2,1},{3,2},{4,7},{5,4},{6,5},{7,6},{8,11},{9,8},{10,9... | collective-permute-start | bytes 1572872 | tf_op jit(solution)/shard_map/ppermute | solution.py:620
  220.9 26.8 %collective-permute-start.18 = (bf16[4,4,128,512]{3,2,1,0:T(8,128)(2,1)}, bf16[4,4,128,512]{3,2,1,0:T(8,128)(2,1)}, u32[]{:S(2)}, u32[]{:S(2)}) collective-permute-start(bf16[4,4,128,512]{3,2,1,0:T(8,128)(2,1)} %get-tuple-element.227), channel_id=1, source_target_pairs={{0,4},{4,0},{8,12},{12,8},{16,20},{20,16},{24,28},{28,24},{1,5},{5... | collective-permute-start | bytes 6291464 | tf_op jit(solution)/shard_map/ppermute | solution.py:615
  221.4 15.1 %collective-permute-start.15 = (bf16[4,128,512]{2,1,0:T(8,128)(2,1)}, bf16[4,128,512]{2,1,0:T(8,128)(2,1)}, u32[]{:S(2)}, u32[]{:S(2)}) collective-permute-start(bf16[4,128,512]{2,1,0:T(8,128)(2,1)} %get-tuple-element.224), channel_id=1, source_target_pairs={{0,8},{4,12},{8,0},{12,4},{16,24},{20,28},{24,16},{28,20},{1,9},{5... | collective-permute-start | bytes 1572872 | tf_op jit(solution)/shard_map/ppermute | solution.py:615
  223.4 24.2 %collective-permute-start.17 = (bf16[4,128,512]{2,1,0:T(8,128)(2,1)S(1)}, bf16[4,128,512]{2,1,0:T(8,128)(2,1)}, u32[]{:S(2)}, u32[]{:S(2)}) collective-permute-start(bf16[4,128,512]{2,1,0:T(8,128)(2,1)S(1)} %get-tuple-element.226), channel_id=1, source_target_pairs={{0,24},{4,28},{8,16},{12,20},{16,8},{20,12},{24,0},{28,4},{1,25},{... | collective-permute-start | bytes 1572872 | tf_op jit(solution)/shard_map/ppermute | solution.py:615
  251.4 24.4 %collective-permute-start.21 = (bf16[4,128,512]{2,1,0:T(8,128)(2,1)}, bf16[4,128,512]{2,1,0:T(8,128)(2,1)S(1)}, u32[]{:S(2)}, u32[]{:S(2)}) collective-permute-start(bf16[4,128,512]{2,1,0:T(8,128)(2,1)} %get-tuple-element.236), channel_id=1, source_target_pairs={{0,16},{4,20},{8,24},{12,28},{16,0},{20,4},{24,8},{28,12},{1,17},{... | collective-permute-start | bytes 1572872 | tf_op jit(solution)/shard_map/ppermute | solution.py:615
  252.7 23.1 %collective-permute-start.22 = (bf16[4,128,512]{2,1,0:T(8,128)(2,1)S(1)}, bf16[4,128,512]{2,1,0:T(8,128)(2,1)}, u32[]{:S(2)}, u32[]{:S(2)}) collective-permute-start(bf16[4,128,512]{2,1,0:T(8,128)(2,1)S(1)} %get-tuple-element.237), channel_id=1, source_target_pairs={{0,24},{4,28},{8,16},{12,20},{16,8},{20,12},{24,0},{28,4},{1,25},{... | collective-permute-start | bytes 1572872 | tf_op jit(solution)/shard_map/ppermute | solution.py:615
  279.2 17.8 %collective-permute-start.24 = (bf16[512,512]{1,0:T(8,128)(2,1)S(1)}, bf16[512,512]{1,0:T(8,128)(2,1)S(1)}, u32[]{:S(2)}, u32[]{:S(2)}) collective-permute-start(bf16[512,512]{1,0:T(8,128)(2,1)S(1)} %bitcast.55), channel_id=1, source_target_pairs={{0,8},{4,12},{8,0},{12,4},{16,24},{20,28},{24,16},{28,20},{1,9},{5... | collective-permute-start | bytes 1572872 | tf_op jit(solution)/shard_map/ppermute | solution.py:615
  280.2 16.8 %collective-permute-start.25 = (bf16[512,512]{1,0:T(8,128)(2,1)S(1)}, bf16[512,512]{1,0:T(8,128)(2,1)S(1)}, u32[]{:S(2)}, u32[]{:S(2)}) collective-permute-start(bf16[512,512]{1,0:T(8,128)(2,1)S(1)} %bitcast.56), channel_id=1, source_target_pairs={{0,16},{4,20},{8,24},{12,28},{16,0},{20,4},{24,8},{28,12},{1,17},{... | collective-permute-start | bytes 1572872 | tf_op jit(solution)/shard_map/ppermute | solution.py:615
  281.2 22.2 %collective-permute-start.26 = (bf16[2,256,512]{2,1,0:T(8,128)(2,1)S(1)}, bf16[2,256,512]{2,1,0:T(8,128)(2,1)S(1)}, u32[]{:S(2)}, u32[]{:S(2)}) collective-permute-start(bf16[2,256,512]{2,1,0:T(8,128)(2,1)S(1)} %get-tuple-element.269), channel_id=1, source_target_pairs={{0,1},{1,0},{2,3},{3,2},{4,5},{5,4},{6,7},{7,6},{8,9},{9,8},{10,11... | collective-permute-start | bytes 1572872 | tf_op jit(solution)/shard_map/ppermute | solution.py:615
  (35 other events, 341.7 us)
Sparse Core Ops, SparseCore 0:
  121.7 89.2 reduce-scatter.6
  213.4 50.6 reduce-scatter.4
